TPU v7x, 128 devices: a whole 4x4x4 slice. The times are simulated.
128 devices in a mesh: member: 8 (over x_hi, z), space: 8 (over y, core), dp: 2 (over x_lo).
Axes of the slice: x: 4 (x_hi: 2, x_lo: 2; x = x_hi * 2 + x_lo), y: 4, z: 4, core: 2. Of those that a mesh axis runs over, the one named last changes fastest.
Arguments:
- latent: bfloat16 [2, 16, 16384, 1024], P('dp', 'member', 'space'), may hold values from -6 to 6
- w_in: bfloat16 [1024, 1024], replicated, may hold values from -0.1875 to 0.1875
- w_out: bfloat16 [1024, 100], replicated, may hold values from -0.1875 to 0.1875
- targets: bfloat16 [2, 100, 16384], P('dp', None, 'space'), may hold values from -4 to 4
- area_units: int32 [16384], P('space'), may hold values from 1000 to 3499
- var_weight: float32 [100], replicated, may hold values from 0.3 to 3
Outputs:
- loss: float32 [], replicated
- grad_latent: bfloat16 [2, 16, 16384, 1024], P('dp', 'member', 'space')
- grad_w_in: float32 [1024, 1024], P(('member', 'space', 'dp'))
- grad_w_out: float32 [1024, 100], P(('member', 'space', 'dp'))
All inputs are finite; a program needn't handle non-finite values.
Results may differ from a plain program's by a relative error of at most 0.025.
Values may be sent and summed in bfloat16 or wider, within the bound.
No kernel may reach another device: no remote copies, remote signals or barrier semaphores. Data moves between devices by JAX's collectives and lax.ppermute only.
A program may use at most 192 MiB of HBM per device.

v0:
```python
import math

import jax
import jax.numpy as jnp
from jax import lax
from jax.sharding import PartitionSpec as P

GELU_C = 0.7978845608
SMOOTH = 0.01


def gelu_parts(preact):
    inner = GELU_C * (preact + 0.044715 * preact * preact * preact)
    tangent = jnp.tanh(inner)
    value = 0.5 * preact * (1.0 + tangent)
    slopes = 0.5 * (1.0 + tangent) + 0.5 * preact * (1.0 - tangent * tangent) * GELU_C * (
        1.0 + 3.0 * 0.044715 * preact * preact
    )
    return (value, slopes)


def score_terms(own_values, every_values, truth, weight, members):
    to_truth = own_values - truth[:, None]
    phi_truth = jnp.sqrt(to_truth * to_truth + SMOOTH)
    spread = own_values[:, :, None] - every_values[:, None]
    phi_pair = jnp.sqrt(spread * spread + SMOOTH)
    pair_phi = jnp.sum(phi_pair, axis=2)
    pair_grad = jnp.sum(spread / phi_pair, axis=2)
    share = jnp.sum(weight * (phi_truth - pair_phi / (2.0 * (members - 1))))
    grad_pred = (weight * (to_truth / phi_truth - pair_grad / (members - 1))).astype(jnp.bfloat16)
    return (share, grad_pred)


def body(latent, w_in, w_out, targets, area_units, var_weight):
    date_count, member_count, point_count, channels = latent.shape
    variables = w_out.shape[1]
    members = member_count * lax.axis_size("member")
    npoints_all = point_count * lax.axis_size("space")
    dates_all = date_count * lax.axis_size("dp")
    area = area_units.astype(jnp.float32)
    area_total = lax.psum(jnp.sum(area), "space")
    area_norm = area * npoints_all / area_total
    weight = var_weight[:, None] * area_norm[None, :]
    row_count = date_count * member_count
    flat_latent = latent.reshape(row_count * point_count, channels)
    preact = jnp.dot(flat_latent, w_in, preferred_element_type=jnp.float32)
    value, slopes = gelu_parts(preact)
    hidden = value.astype(jnp.bfloat16).reshape(row_count, point_count, channels)
    pred = jnp.einsum("hv,rph->rvp", w_out, hidden, preferred_element_type=jnp.float32).astype(
        jnp.bfloat16
    )
    pred = pred.reshape(date_count, member_count, variables, point_count)
    every_pred = lax.all_gather(pred, "member", axis=1, tiled=True)
    share, grad_pred = score_terms(
        pred.astype(jnp.float32),
        every_pred.astype(jnp.float32),
        targets.astype(jnp.float32),
        weight,
        members,
    )
    upstream = grad_pred.reshape(row_count, variables, point_count)
    grad_hidden = jnp.einsum("rvp,hv->rph", upstream, w_out, preferred_element_type=jnp.float32)
    grad_preact = (grad_hidden.reshape(row_count * point_count, channels) * slopes).astype(
        jnp.bfloat16
    )
    grad_latent = jnp.dot(grad_preact, w_in.T, preferred_element_type=jnp.float32).astype(
        jnp.bfloat16
    )
    sum_in = jnp.dot(flat_latent.T, grad_preact, preferred_element_type=jnp.float32)
    sum_out = jnp.einsum("rph,rvp->hv", hidden, upstream, preferred_element_type=jnp.float32)
    total_in, total_out = (
        lax.psum_scatter(sum_in, ("member", "space", "dp"), scatter_dimension=0, tiled=True),
        lax.psum_scatter(sum_out, ("member", "space", "dp"), scatter_dimension=0, tiled=True),
    )
    grad_scale = math.sqrt(dates_all * members * npoints_all)
    loss_sum = lax.psum(share, ("member", "space", "dp"))
    loss = loss_sum / (dates_all * npoints_all * variables)
    return (loss, grad_latent.reshape(latent.shape), total_in / grad_scale, total_out / grad_scale)


def solution(mesh):
    return jax.shard_map(
        body,
        mesh=mesh,
        in_specs=(
            P("dp", "member", "space", None),
            P(),
            P(),
            P("dp", None, "space"),
            P("space"),
            P(),
        ),
        out_specs=(
            P(),
            P("dp", "member", "space", None),
            P(("member", "space", "dp"), None),
            P(("member", "space", "dp"), None),
        ),
        check_vma=False,
    )
```

profile of v0, /device:TPU:0, one launch (start us, length us, event | category | flops | bytes accessed | tf_op | source)
XLA Modules:
  0.0 979.0 jit_solution(12682062792776466585)
XLA Ops:
  7.2 0.0 copy-start
  7.2 0.0 all-gather.3.cloned.1.call-start
  7.2 1.5 copy-done
  8.8 0.0 copy-start.8
  8.8 17.8 %multiply_convert_fusion = (bf16[4096,1024]{1,0:T(8,128)(2,1)S(1)}, f32[4096,1024]{1,0:T(8,128)}) fusion(bf16[4096,1024]{1,0:T(8,128)(2,1)} %bitcast.58, bf16[1024,1024]{1,0:T(8,128)(2,1)S(1)} %copy-done), kind=kOutput, calls=%fused_computation.16 | convolution fusion | flops 8627683328 | bytes 35651584 | tf_op jit(solution)/shard_map/dot_general | solution.py:46
  26.6 0.0 copy-start.1
  26.6 0.0 copy-done.8
  26.6 0.0 copy-start.9
  26.6 0.0 copy-start.10
  26.6 0.0 copy-start.7
  26.6 4.2 bitcast_convert_fusion.1
  30.9 0.0 copy-done.1
  30.9 0.0 all-gather.3.cloned.1.call-update
  30.9 0.0 all-reduce.3.cloned.1.call-start
  31.0 0.0 copy-done.9
  31.0 0.6 convert_reduce_fusion
  31.6 15.7 %psum.14 = f32[]{:T(128)} all-reduce(f32[]{:T(128)} %convert_reduce_fusion), channel_id=1, replica_groups=mesh['member'=8,'space'=8,'dp'=2] {'space'}, use_global_device_ids=true, to_apply=%region_1.0 | all-reduce | flops 1 | bytes 8 | tf_op jit(solution)/shard_map/psum | solution.py:41
  47.3 0.6 multiply_divide_fusion
  48.0 0.0 copy-done.10
  48.0 1.0 broadcast_multiply_fusion.1
  49.0 1.0 broadcast_multiply_fusion
  50.1 0.0 copy-done.7
  50.1 1.4 fusion.19
  51.4 75.5 %all-gather.3.cloned.1.call-done = bf16[16,100,2048]{2,1,0:T(8,128)(2,1)} async-done(((bf16[2,100,2048]{2,1,0:T(8,128)(2,1)}), bf16[16,100,2048]{2,1,0:T(8,128)(2,1)}) %all-gather.3.cloned.1.call-update) | async-done | bytes 6553616 | tf_op jit(solution)/shard_map/all_gather | solution.py:53
  127.0 0.0 copy-start.3
  127.0 0.0 slice-start
  127.0 11.6 %copy_convert_fusion = f32[16,100,2048]{2,0,1:T(8,128)} fusion(bf16[16,100,2048]{2,1,0:T(8,128)(2,1)} %all-gather.3.cloned.1.call-done), kind=kLoop, calls=%fused_computation.18 | loop fusion | flops 3276800 | bytes 19660800 | tf_op jit(solution)/shard_map/sub | solution.py:25
  138.5 0.0 copy-done.3
  138.5 0.0 slice-start.1
  138.5 0.0 copy-start.2
  138.5 0.0 copy-start.4
  138.5 0.0 copy-start.5
  138.6 37.1 %fusion.4 = (f32[2,100,2048]{2,1,0:T(8,128)S(1)}, f32[2,100,2048]{2,1,0:T(8,128)}) fusion(f32[16,100,2048]{2,0,1:T(8,128)} %copy_convert_fusion, f32[2,100,2048]{2,1,0:T(8,128)S(1)} %copy-done.3), kind=kLoop, calls=%fused_computation.6 | loop fusion | flops 38502400 | bytes 18022400 | tf_op jit(solution)/shard_map/reduce_sum | solution.py:28
  175.6 1.2 copy-done.6
  176.9 0.0 slice-done
  176.9 0.0 slice-done.1
  176.9 0.0 copy-done.2
  176.9 0.0 copy-done.4
  176.9 0.0 copy-done.5
  176.9 3.3 convolution_bitcast_fusion.1
  180.2 0.0 all-reduce.3.cloned.1.call-update
  180.2 0.0 reduce-scatter.4.cloned.1.call-start
  180.3 2.5 fusion.13
  182.7 0.0 slice-start.2
  182.7 0.8 copy.32
  183.6 0.6 pad
  184.2 0.3 copy.29
  184.5 0.0 slice-start.3
  184.6 13.5 %fusion.11 = bf16[4096,1024]{1,0:T(8,128)(2,1)S(1)} fusion(f32[4096,1024]{1,0:T(8,128)} %get-tuple-element.29, bf16[4096,100]{0,1:T(8,128)(2,1)S(1)} %bitcast.57, bf16[1024,100]{0,1:T(8,128)(2,1)S(1)} %copy-done.8), kind=kOutput, calls=%fused_computation.15 | convolution fusion | flops 918552576 | bytes 26189824 | tf_op jit(solution)/shard_map/rvp,hv->rph/dot_general | solution.py:62
  198.1 0.0 copy-start.11
  198.1 3.2 copy-done.11
  201.3 0.0 slice-done.2
  201.3 0.0 slice-done.3
  201.3 10.4 %convolution_bitcast_fusion = f32[1024,1024]{0,1:T(8,128)} fusion(bf16[4096,1024]{1,0:T(8,128)(2,1)S(1)} %fusion.11, bf16[4096,1024]{1,0:T(8,128)(2,1)S(1)} %bitcast.61), kind=kOutput, calls=%fused_computation.20 | convolution fusion | flops 8589934592 | bytes 20971520 | tf_op jit(solution)/shard_map/dot_general | solution.py:69
  211.8 5.4 copy.27
  217.2 0.0 reduce-scatter.4.cloned.1.call-update
  217.2 3.4 multiply_reduce_fusion
  220.5 64.5 %psum.15 = f32[]{:T(128)} all-reduce(f32[]{:T(128)} %multiply_reduce_fusion), channel_id=1, replica_groups=mesh['member'=8,'space'=8,'dp'=2] {'member','space','dp'}, use_global_device_ids=true, to_apply=%region_4.0 | all-reduce | flops 1 | bytes 8 | tf_op jit(solution)/shard_map/psum | solution.py:76
  285.7 14.6 %convolution_convert_fusion = bf16[4096,1024]{1,0:T(8,128)(2,1)} fusion(bf16[4096,1024]{1,0:T(8,128)(2,1)} %copy-done.11, bf16[1024,1024]{1,0:T(8,128)(2,1)S(1)} %copy-done), kind=kOutput, calls=%fused_computation.17 | convolution fusion | flops 8594128896 | bytes 18874368 | tf_op jit(solution)/shard_map/dot_general | solution.py:66
  300.3 22.5 %all-reduce.3.cloned.1.call-done = f32[1024,100]{1,0:T(8,128)} async-done(((f32[1024,100]{1,0:T(8,128)}), f32[1024,100]{1,0:T(8,128)}) %all-reduce.3.cloned.1.call-update) | async-done | bytes 409616
  322.8 1.3 dynamic-slice_multiply_fusion
  324.1 645.0 %reduce-scatter.4.cloned.1.call-done = f32[8,1024]{1,0:T(8,128)} async-done(((f32[1024,1024]{1,0:T(8,128)}), f32[8,1024]{1,0:T(8,128)}) %reduce-scatter.4.cloned.1.call-update) | async-done | bytes 32784
  969.1 0.9 copy.28
  970.1 0.8 copy.25
  (4 shorter events, 0.1 us)
Async XLA Ops:
  7.2 1.6 copy-start
  7.2 119.8 %all-gather.3.cloned.1.call-start = ((), (), s32[]{:S(2)}) async-start(), calls=%async_computation.1 | async-start | bytes 7667712 | tf_op jit(solution)/shard_map/all_gather | solution.py:53
  8.8 17.9 %copy-start.8 = (bf16[1024,100]{0,1:T(8,128)(2,1)S(1)}, bf16[1024,100]{0,1:T(8,128)(2,1)}, u32[]{:S(2)}) copy-start(bf16[1024,100]{0,1:T(8,128)(2,1)} %param.8) | copy-start | bytes 614404
  26.6 4.3 copy-start.1
  26.6 4.4 copy-start.9
  26.6 21.4 %copy-start.10 = (f32[100]{0:T(128)S(1)}, f32[100]{0:T(128)}, u32[]{:S(2)}) copy-start(f32[100]{0:T(128)} %param.11) | copy-start | bytes 1204
  26.6 23.4 %copy-start.7 = (bf16[1,100,2048]{2,1,0:T(8,128)(2,1)S(1)}, bf16[1,100,2048]{2,1,0:T(8,128)(2,1)}, u32[]{:S(2)}) copy-start(bf16[1,100,2048]{2,1,0:T(8,128)(2,1)} %param.9) | copy-start | bytes 1228804
  30.9 291.9 %all-reduce.3.cloned.1.call-start = ((), (), s32[]{:S(2)}) async-start(), calls=%async_computation.3 | async-start | bytes 1048576
  127.0 11.6 %copy-start.3 = (f32[2,100,2048]{2,1,0:T(8,128)S(1)}, f32[2,100,2048]{2,1,0:T(8,128)}, u32[]{:S(2)}) copy-start(f32[2,100,2048]{2,1,0:T(8,128)} %get-tuple-element.30) | copy-start | bytes 4915204
  127.0 49.9 %slice-start = ((s8[8388608]{0:T(1024)(128)(4,1)}), s8[4194304]{0:T(1024)(128)(4,1)S(1)}, s32[]{:S(2)}) async-start(s8[8388608]{0:T(1024)(128)(4,1)} %bitcast.51), calls=%async_computation.4 | async-start | bytes 8388608
  138.5 38.3 %slice-start.1 = ((s8[8388608]{0:T(1024)(128)(4,1)}), s8[4194304]{0:T(1024)(128)(4,1)S(1)}, s32[]{:S(2)}) async-start(s8[8388608]{0:T(1024)(128)(4,1)} %bitcast.51), calls=%async_computation.5 | async-start | bytes 8388608
  138.5 38.3 %copy-start.2 = (bf16[2,2048,100]{1,2,0:T(8,128)(2,1)S(1)}, bf16[2,2048,100]{1,2,0:T(8,128)(2,1)}, u32[]{:S(2)}) copy-start(bf16[2,2048,100]{1,2,0:T(8,128)(2,1)} %get-tuple-element.31) | copy-start | bytes 2457604
  138.5 38.3 %copy-start.4 = (f32[100,2048]{1,0:T(8,128)S(1)}, f32[100,2048]{1,0:T(8,128)}, u32[]{:S(2)}) copy-start(f32[100,2048]{1,0:T(8,128)} %broadcast_multiply_fusion.1) | copy-start | bytes 2457604
  138.5 38.3 %copy-start.5 = (f32[100,2048]{1,0:T(8,128)S(1)}, f32[100,2048]{1,0:T(8,128)}, u32[]{:S(2)}) copy-start(f32[100,2048]{1,0:T(8,128)} %get-tuple-element.27) | copy-start | bytes 2457604
  175.6 1.2 copy-start.6
  180.2 788.9 %reduce-scatter.4.cloned.1.call-start = ((), (), s32[]{:S(2)}) async-start(), calls=%async_computation.2 | async-start | bytes 4227072
  182.7 18.6 %slice-start.2 = ((s8[8388608]{0:T(1024)(128)(4,1)}), s8[4194304]{0:T(1024)(128)(4,1)S(1)}, s32[]{:S(2)}) async-start(s8[8388608]{0:T(1024)(128)(4,1)} %bitcast.59), calls=%async_computation.6 | async-start | bytes 8388608
  184.5 16.8 %slice-start.3 = ((s8[8388608]{0:T(1024)(128)(4,1)}), s8[4194304]{0:T(1024)(128)(4,1)S(1)}, s32[]{:S(2)}) async-start(s8[8388608]{0:T(1024)(128)(4,1)} %bitcast.59), calls=%async_computation.7 | async-start | bytes 8388608
  198.1 3.2 copy-start.11
Sparse Core Ops, SparseCore 0:
  31.0 95.8 all-gather.2
  180.3 142.4 all-reduce.2
  325.3 643.7 reduce-scatter.3
where the time goes:
time: 985 us; the launch traced here: 979 us
  waiting for transfers between devices  743 us (75%)
  blocking collectives  80.3 us (8%)
  matrix products  64 us (6%)
  other arithmetic  60.5 us (6%)
  between operations  16.1 us (2%)
  local copies, waits for them, and re-layouts  14.9 us (2%)
    unnamed x5, waiting for transfers between devices  668 us
    all_gather x1, waiting for transfers between devices, body(): every_pred = lax.all_gather(pred, 'member', axis=1, tiled=True)  75.5 us
    psum x1, blocking collectives, body(): loss_sum = lax.psum(share, ('member', 'space', 'dp'))  64.5 us
    reduce_sum x1, other arithmetic, score_terms(): pair_grad = jnp.sum(spread / phi_pair, axis=2)  37.1 us
  transfers between devices with their start and end apart: 3, of which 3 were waited for; matrix products, arithmetic and copies ran while one was open for 6% of the time, Pallas kernels for 0%

commit v1 on v0

v1 whole, which is shorter than its diff:
```python
import functools
import math

import jax
import jax.numpy as jnp
from jax import lax
from jax.experimental import pallas as pl
from jax.experimental.pallas import tpu as pltpu
from jax.sharding import Mesh
from jax.sharding import PartitionSpec as P

GELU_C = 0.7978845608
GELU_A = 0.044715
SMOOTH = 0.01
BF16 = jnp.bfloat16
F32 = jnp.float32

BLOCK = 256
VPAD = 112
WIDE = 128
TILE = 512
SUB = 256
EXTRA = 112

MEMBER = ("xh", "z")
REST = ("xh", "z", "y", "dp")


def forward_kernel(lat_ref, win_ref, wout_ref, hidden_ref, slope_ref, pred_ref):
    for s in range(TILE // SUB):
        rows = pl.ds(s * SUB, SUB)
        u = jnp.dot(lat_ref[0, rows, :], win_ref[...], preferred_element_type=F32)
        u2 = u * u
        half = 0.5 + 0.5 * jnp.tanh(u * (GELU_C + (GELU_C * GELU_A) * u2))
        value = u * half
        hidden = value.astype(BF16)
        hidden_ref[0, rows, :] = hidden
        bend = (2.0 * GELU_C) + (6.0 * GELU_A * GELU_C) * u2
        slope_ref[0, rows, :] = (half + (value - value * half) * bend).astype(BF16)
        pred = jnp.dot(hidden, wout_ref[...], preferred_element_type=F32)
        pred_ref[s, 0] = pred.T[:VPAD].astype(BF16)


def forward(latent, w_in, w_out):
    members, points, channels = latent.shape
    per = TILE // BLOCK
    tile = pl.BlockSpec((1, TILE, channels), lambda m, i: (m, i, 0))
    return pl.pallas_call(
        forward_kernel,
        grid=(members, points // TILE),
        in_specs=[
            tile,
            pl.BlockSpec((channels, channels), lambda m, i: (0, 0)),
            pl.BlockSpec((channels, WIDE), lambda m, i: (0, 0)),
        ],
        out_specs=[
            tile,
            tile,
            pl.BlockSpec((per, 1, VPAD, BLOCK), lambda m, i: (i, m, 0, 0)),
        ],
        out_shape=[
            jax.ShapeDtypeStruct(latent.shape, BF16),
            jax.ShapeDtypeStruct(latent.shape, BF16),
            jax.ShapeDtypeStruct((points // BLOCK, members, VPAD, BLOCK), BF16),
        ],
        compiler_params=pltpu.CompilerParams(vmem_limit_bytes=40 << 20),
        name="forward",
    )(latent, w_in, w_out)


def score_kernel(members, scale_ref, pred_ref, truth_ref, var_ref, area_ref, grad_ref, share_ref):
    per = pred_ref.shape[1]
    scale = scale_ref[0, 0]
    self_phi = members * math.sqrt(SMOOTH) / (2.0 * (members - 1))

    def rows16(step, total):
        base = pl.multiple_of(step * 16, 16)
        rows = pl.ds(base, 16)
        for lane in range(BLOCK // 128):
            lanes = pl.ds(lane * 128, 128)
            loaded = [pred_ref[m // per, m % per, rows, lanes].astype(F32) for m in range(members)]
            truths = truth_ref[rows, lanes].astype(F32)
            area = area_ref[0, :, lanes].astype(F32) * scale
            weights = var_ref[rows, lanes] * area
            results = []
            for h in range(2):
                x = [v[h * 8 : h * 8 + 8] for v in loaded]
                truth = truths[h * 8 : h * 8 + 8]
                weight = weights[h * 8 : h * 8 + 8]
                grads = [None] * members
                pair_phi = None
                for m in range(members):
                    for k in range(m + 1, members):
                        d = x[m] - x[k]
                        q = d * d + SMOOTH
                        r = lax.rsqrt(q)
                        g = d * r
                        p = q * r
                        pair_phi = p if pair_phi is None else pair_phi + p
                        grads[m] = g if grads[m] is None else grads[m] + g
                        grads[k] = -g if grads[k] is None else grads[k] - g
                truth_phi = None
                outs = []
                for m in range(members):
                    d = x[m] - truth
                    q = d * d + SMOOTH
                    r = lax.rsqrt(q)
                    p = q * r
                    truth_phi = p if truth_phi is None else truth_phi + p
                    outs.append(weight * (d * r - grads[m] * (1.0 / (members - 1))))
                total = total + weight * (truth_phi - pair_phi * (1.0 / (members - 1)) - self_phi)
                results.append(outs)
            for m in range(members):
                grad_ref[m // per, m % per, rows, lanes] = jnp.concatenate(
                    [results[0][m], results[1][m]], axis=0
                ).astype(BF16)
        return total

    share_ref[...] = lax.fori_loop(0, VPAD // 16, rows16, jnp.zeros((8, 128), F32))


def score(me, scale, every, truth, var_weight, area):
    devices, per = every.shape[:2]
    members = devices * per
    grid_spec = pltpu.PrefetchScalarGridSpec(
        num_scalar_prefetch=1,
        grid=(1,),
        in_specs=[
            pl.BlockSpec(memory_space=pltpu.SMEM),
            pl.BlockSpec(every.shape, lambda i, me: (0, 0, 0, 0)),
            pl.BlockSpec((VPAD, BLOCK), lambda i, me: (0, me[0])),
            pl.BlockSpec((VPAD, BLOCK), lambda i, me: (0, 0)),
            pl.BlockSpec((1, 1, BLOCK), lambda i, me: (me[0], 0, 0)),
        ],
        out_specs=[
            pl.BlockSpec(every.shape, lambda i, me: (0, 0, 0, 0)),
            pl.BlockSpec((8, 128), lambda i, me: (0, 0)),
        ],
    )

    def kernel(me_ref, *refs):
        score_kernel(members, *refs)

    return pl.pallas_call(
        kernel,
        grid_spec=grid_spec,
        out_shape=[
            jax.ShapeDtypeStruct(every.shape, BF16),
            jax.ShapeDtypeStruct((8, 128), F32),
        ],
        compiler_params=pltpu.CompilerParams(vmem_limit_bytes=32 << 20),
        name="score",
    )(me, scale, every, truth, var_weight, area)


def backward_kernel(
    core_ref, lat_ref, hidden_ref, slope_ref, up_ref, wout_ref, share_ref, gp_ref, sums_ref, acc_in, acc_out
):
    step, last = pl.program_id(0), pl.num_programs(0) - 1
    channels = lat_ref.shape[2]

    @pl.when(step == 0)
    def _():
        acc_in[...] = jnp.zeros_like(acc_in)
        acc_out[...] = jnp.zeros_like(acc_out)

    ups = []
    for s in range(TILE // BLOCK):
        rows = pl.ds(s * BLOCK, BLOCK)
        block = jnp.concatenate(
            [up_ref[s, 0].astype(F32), jnp.zeros((WIDE - VPAD, BLOCK), F32)], axis=0
        )
        up = block.T.astype(BF16)
        ups.append(up)
        grad_hidden = jnp.dot(up, wout_ref[...], preferred_element_type=F32)
        gp_ref[0, rows, :] = (grad_hidden * slope_ref[0, rows, :].astype(F32)).astype(BF16)
    over_rows = (((0,), (0,)), ((), ()))
    acc_in[...] += lax.dot_general(
        lat_ref[0], gp_ref[0], over_rows, preferred_element_type=F32
    )
    acc_out[...] += lax.dot_general(
        hidden_ref[0], jnp.concatenate(ups, axis=0), over_rows, preferred_element_type=F32
    )

    @pl.when(step == last)
    def _():
        sums_ref[:, :channels] = acc_in[...].astype(BF16)
        share = jnp.sum(share_ref[...])
        high = share.astype(BF16).astype(F32)
        middle = (share - high).astype(BF16).astype(F32)
        low = share - high - middle
        column = lax.broadcasted_iota(jnp.int32, acc_out.shape, 1) - (EXTRA + 3 * core_ref[0])
        sums_ref[:, channels:] = jnp.where(
            column == 0,
            high,
            jnp.where(column == 1, middle, jnp.where(column == 2, low, acc_out[...])),
        ).astype(BF16)


def backward(core, latent, hidden, slopes, upstream, w_out_t, share):
    members, points, channels = latent.shape
    steps = points // TILE
    per = TILE // BLOCK
    tile = pl.BlockSpec((1, TILE, channels), lambda i, c: (i // steps, i % steps, 0))
    grid_spec = pltpu.PrefetchScalarGridSpec(
        num_scalar_prefetch=1,
        grid=(members * steps,),
        in_specs=[
            tile,
            tile,
            tile,
            pl.BlockSpec((per, 1, VPAD, BLOCK), lambda i, c: (i % steps, i // steps, 0, 0)),
            pl.BlockSpec((WIDE, channels), lambda i, c: (0, 0)),
            pl.BlockSpec((8, 128), lambda i, c: (0, 0)),
        ],
        out_specs=[
            tile,
            pl.BlockSpec((channels, channels + WIDE), lambda i, c: (0, 0)),
        ],
        scratch_shapes=[
            pltpu.VMEM((channels, channels), F32),
            pltpu.VMEM((channels, WIDE), F32),
        ],
    )
    return pl.pallas_call(
        backward_kernel,
        grid_spec=grid_spec,
        out_shape=[
            jax.ShapeDtypeStruct(latent.shape, BF16),
            jax.ShapeDtypeStruct((channels, channels + WIDE), BF16),
        ],
        compiler_params=pltpu.CompilerParams(vmem_limit_bytes=48 << 20),
        name="backward",
    )(core, latent, hidden, slopes, upstream, w_out_t, share)


def latent_kernel(gp_ref, win_ref, out_ref):
    for s in range(TILE // SUB):
        rows = pl.ds(s * SUB, SUB)
        out_ref[0, rows, :] = lax.dot_general(
            gp_ref[0, rows, :], win_ref[...], (((1,), (1,)), ((), ())), preferred_element_type=F32
        ).astype(BF16)


def latent_grad(gp, w_in):
    members, points, channels = gp.shape
    tile = pl.BlockSpec((1, TILE, channels), lambda m, i: (m, i, 0))
    return pl.pallas_call(
        latent_kernel,
        grid=(members, points // TILE),
        in_specs=[tile, pl.BlockSpec((channels, channels), lambda m, i: (0, 0))],
        out_specs=tile,
        out_shape=jax.ShapeDtypeStruct(gp.shape, BF16),
        compiler_params=pltpu.CompilerParams(vmem_limit_bytes=24 << 20),
        cost_estimate=pl.CostEstimate(
            flops=2 * members * points * channels * channels,
            bytes_accessed=4 * members * points * channels,
            transcendentals=0,
        ),
        name="latent_grad",
    )(gp, w_in)


def exchange(x, axis, xor):
    size = lax.axis_size(axis)
    return lax.ppermute(x, axis, [(i, i ^ xor) for i in range(size)])


def body(latent, w_in, w_out, targets, area_units, var_weight):
    date_count, per, points, channels = latent.shape
    variables = w_out.shape[1]
    member_devices = lax.axis_size("xh") * lax.axis_size("z")
    members = per * member_devices
    npoints = points * lax.axis_size("y") * lax.axis_size("core")
    dates = date_count * lax.axis_size("dp")
    me = (lax.axis_index("xh") * lax.axis_size("z") + lax.axis_index("z")).astype(jnp.int32)
    core = lax.axis_index("core").astype(jnp.int32)

    area_total = jnp.sum(area_units.astype(F32))
    for axis, xor in (("core", 1), ("y", 1), ("y", 2)):
        area_total = area_total + exchange(area_total, axis, xor)
    scale = (npoints / area_total).reshape(1, 1)

    rows = latent.reshape(date_count * per, points, channels)
    w_out_wide = jnp.pad(w_out, ((0, 0), (0, WIDE - variables)))
    hidden, slopes, pred = forward(rows, w_in, w_out_wide)
    every = lax.all_to_all(pred, MEMBER, 0, 0, tiled=True)
    truth = jnp.pad(targets[0], ((0, VPAD - variables), (0, 0)))
    var_wide = jnp.broadcast_to(
        jnp.pad(var_weight, (0, VPAD - variables))[:, None], (VPAD, BLOCK)
    )
    area = area_units.reshape(points // BLOCK, 1, BLOCK)
    grad_pred, share = score(me.reshape(1), scale, every, truth, var_wide, area)
    upstream = lax.all_to_all(grad_pred, MEMBER, 0, 0, tiled=True)
    gp, sums = backward(core.reshape(1), rows, hidden, slopes, upstream, w_out_wide.T, share)
    wide = channels + WIDE
    halves = sums.reshape(-1, 2, 16, wide)
    mine = lax.dynamic_index_in_dim(halves, core, 1, keepdims=False)
    other = lax.dynamic_index_in_dim(halves, 1 - core, 1, keepdims=False)
    both = (mine.astype(F32) + exchange(other, "core", 1).astype(F32)).astype(BF16)
    pieces = lax.all_to_all(both.reshape(-1, 8, wide), REST, 0, 0, tiled=True)
    grad_latent = latent_grad(gp, w_in)
    total = jnp.sum(pieces.astype(F32), axis=0)
    grad_scale = math.sqrt(dates * members * npoints)
    loss = jnp.sum(total[0, channels + EXTRA : channels + EXTRA + 6]) / (dates * npoints * variables)
    return (
        loss,
        grad_latent.reshape(latent.shape),
        total[:, :channels] / grad_scale,
        total[:, channels : channels + variables] / grad_scale,
    )


def solution(mesh):
    fine = Mesh(mesh.devices.reshape(2, 4, 4, 2, 2), ("xh", "z", "y", "core", "dp"))
    return jax.shard_map(
        body,
        mesh=fine,
        in_specs=(
            P("dp", MEMBER, ("y", "core"), None),
            P(),
            P(),
            P("dp", None, ("y", "core")),
            P(("y", "core")),
            P(),
        ),
        out_specs=(
            P(),
            P("dp", MEMBER, ("y", "core"), None),
            P(("xh", "z", "y", "core", "dp"), None),
            P(("xh", "z", "y", "core", "dp"), None),
        ),
        check_vma=False,
    )
```

time: 985 us -> 133 us (0.14)
  waiting for transfers between devices: 743 us -> 24.5 us
  blocking collectives: 80.3 us -> 0 us
  matrix products: 64 us -> 0 us
  Pallas kernels: 0 us -> 58.2 us
  other arithmetic: 60.5 us -> 5.25 us
  starting transfers between devices: 0.12 us -> 29.1 us
  between operations: 16.1 us -> 5.1 us
    unnamed x5 -> x0, waiting for transfers between devices: 668 us -> none
    psum x2 -> x0, blocking collectives: 80.3 us -> none  [the longest x1 64.5 us: body(): loss_sum = lax.psum(share, ('member', 'space', 'dp'))]
    all_gather x1 -> x0, waiting for transfers between devices: 75.5 us -> none  [body(): every_pred = lax.all_gather(pred, 'member', axis=1, tiled=True)]
    dot_general x6 -> x0, matrix products: 64 us -> none  [the longest x1 17.8 us: body(): preact = jnp.dot(flat_latent, w_in, preferred_element_type=jnp.float32)]
    pallas_call x0 -> x4, Pallas kernels: none -> 58.2 us  [the longest x1 21 us: forward(): pl.pallas_call(forward_kernel, grid=(members, points // TILE), in_specs=[...]
    reduce_sum x3, other arithmetic: 41 us -> 1.46 us  [the longest x1 0.67 us: body(): jnp.sum(total[0, channels + EXTRA:channels + EXTRA + 6])]
    all_to_all x0 -> x3, starting transfers between devices: none -> 21.6 us  [the longest x1 7.99 us: body(): every = lax.all_to_all(pred, MEMBER, 0, 0, tiled=True)]
    all_to_all x0 -> x3, waiting for transfers between devices: none -> 18.6 us  [the longest x1 13 us: body(): upstream = lax.all_to_all(grad_pred, MEMBER, 0, 0, tiled=True)]
  transfers between devices with their start and end apart: 3 -> 7, of which waited for: 3 -> 7; matrix products, arithmetic and copies ran while one was open for 6% -> 1% of each run, Pallas kernels for 0% -> 9%
where the time goes in v1:
time: 133 us
  Pallas kernels  58.2 us (44%)
  starting transfers between devices  29.1 us (22%)
  waiting for transfers between devices  24.5 us (18%)
  local copies, waits for them, and re-layouts  10.6 us (8%)
  other arithmetic  5.25 us (4%)
  between operations  5.1 us (4%)
    pallas_call x1, Pallas kernels, forward(): pl.pallas_call(forward_kernel, grid=(members, points // TILE), in_specs=[...  21 us
    pallas_call x1, Pallas kernels, backward(): pl.pallas_call(backward_kernel, grid_spec=grid_spec, out_shape=[jax.Shape...  19.8 us
    all_to_all x1, waiting for transfers between devices, body(): upstream = lax.all_to_all(grad_pred, MEMBER, 0, 0, tiled=True)  13 us
    pallas_call x1, Pallas kernels, latent_grad(): pl.pallas_call(latent_kernel, grid=(members, points // TILE), in_specs=[t...  11.3 us
    unnamed x17, local copies, waits for them, and re-layouts  9.31 us
    all_to_all x1, starting transfers between devices, body(): every = lax.all_to_all(pred, MEMBER, 0, 0, tiled=True)  7.99 us
    ppermute x4, starting transfers between devices, exchange(): return lax.ppermute(x, axis, [(i, i ^ xor) for i in range(size)])  7.53 us
    all_to_all x1, starting transfers between devices, body(): pieces = lax.all_to_all(both.reshape(-1, 8, wide), REST, 0, 0, tiled=True)  7.44 us
  transfers between devices with their start and end apart: 7, of which 7 were waited for; matrix products, arithmetic and copies ran while one was open for 1% of the time, Pallas kernels for 9%

profile of v1, /device:TPU:0, one launch (start us, length us, event | category | flops | bytes accessed | tf_op | source)
XLA Modules:
  0.0 132.7 jit_solution(4123049013978346212)
XLA Ops:
  0.6 1.1 copy.11
  1.7 0.1 pad.12.clone.wout_ref
  1.8 0.0 copy-start.1
  1.8 1.6 %copy-done.1 = bf16[1024,1024]{1,0:T(8,128)(2,1)S(1)} copy-done((bf16[1024,1024]{1,0:T(8,128)(2,1)S(1)}, bf16[1024,1024]{1,0:T(8,128)(2,1)}, u32[]{:S(2)}) %copy-start.1) | copy-done | bytes 2097176
  3.4 0.0 copy-start.3
  3.4 0.0 copy-start.6
  3.4 21.0 %forward.1 = (bf16[2,2048,1024]{2,1,0:T(8,128)(2,1)S(1)}, bf16[2,2048,1024]{2,1,0:T(8,128)(2,1)}, bf16[8,2,112,256]{3,2,1,0:T(8,128)(2,1)}) custom-call(bf16[2,2048,1024]{2,1,0:T(8,128)(2,1)} %bitcast.19, bf16[1024,1024]{1,0:T(8,128)(2,1)S(1)} %copy-done.1, bf16[1024,128]{1,0:T(8,128)(2,1)S(1)} %pad.12.clone.wout_ref), custom_call_target="tpu_custom_call" | custom-call | tf_op jit(solution)/shard_map/forward/pallas_call | solution.py:48
  24.4 0.0 copy-start
  24.4 3.2 %copy-done = bf16[2,2048,1024]{2,1,0:T(8,128)(2,1)} copy-done((bf16[2,2048,1024]{2,1,0:T(8,128)(2,1)}, bf16[2,2048,1024]{2,1,0:T(8,128)(2,1)S(1)}, u32[]{:S(2)}) %copy-start) | copy-done | bytes 8388632
  27.6 0.0 copy-start.7
  27.6 8.0 %all-to-all-start = ((bf16[8,2,112,256]{3,2,1,0:T(8,128)(2,1)}), bf16[8,2,112,256]{3,2,1,0:T(8,128)(2,1)S(1)}, u32[]{:S(2)}, u32[]{:S(2)}) async-start(bf16[8,2,112,256]{3,2,1,0:T(8,128)(2,1)} %get-tuple-element.13), calls=%async_computation | async-start | bytes 1835008 | tf_op jit(solution)/shard_map/all_to_all | solution.py:287
  35.6 0.0 copy-done.3
  35.6 0.0 copy-start.5
  35.6 0.6 convert_reduce_fusion.1
  36.2 0.0 collective-permute-start
  36.2 0.0 copy-done.6
  36.3 0.0 copy-done.7
  36.3 1.3 collective-permute-done
  38.9 3.0 %collective-permute-start.1 = (f32[]{:T(128)}, f32[]{:T(128)}, u32[]{:S(2)}, u32[]{:S(2)}) collective-permute-start(f32[]{:T(128)} %add.30), channel_id=1, source_target_pairs={{0,4},{4,0},{8,12},{12,8},{1,5},{5,1},{9,13},{13,9},{2,6},{6,2},{1... | collective-permute-start | bytes 20 | tf_op jit(solution)/shard_map/ppermute | solution.py:266
  41.8 0.8 collective-permute-done.1
  43.2 4.6 %collective-permute-start.2 = (f32[]{:T(128)}, f32[]{:T(128)}, u32[]{:S(2)}, u32[]{:S(2)}) collective-permute-start(f32[]{:T(128)} %add.31), channel_id=1, source_target_pairs={{0,8},{4,12},{8,0},{12,4},{1,9},{5,13},{9,1},{13,5},{2,10},{6,14},... | collective-permute-start | bytes 20 | tf_op jit(solution)/shard_map/ppermute | solution.py:266
  47.8 0.7 collective-permute-done.2
  49.1 1.1 all-to-all-done.refs_1_
  50.2 0.1 broadcast_in_dim.2.refs_3_
  50.3 6.1 %score.1 = (bf16[8,2,112,256]{3,2,1,0:T(8,128)(2,1)}, f32[8,128]{1,0:T(8,128)S(1)}) custom-call(s32[1]{0:T(128)} %bitcast.2.me_ref, f32[1,1]{1,0:T(1,128)} %bitcast.3.refs_0_, bf16[8,2,112,256]{3,2,1,0:T(8,128)(2,1)S(1)} %all-to-all-done.refs_1_, bf16[112,2048]{1,0:T(8,128)(2,1)S(1)} %pad.13.refs_2_, f32[112,256]{1,0:T(8,128)S(1)} %broadcast_in_dim.2.refs_3_, ...), custom_call_target="tpu_custom_call" | custom-call | tf_op jit(solution)/shard_map/score/pallas_call | solution.py:144
  56.4 6.1 %all-to-all-start.1 = ((bf16[8,2,112,256]{3,2,1,0:T(8,128)(2,1)}), bf16[8,2,112,256]{3,2,1,0:T(8,128)(2,1)S(1)}, u32[]{:S(2)}, u32[]{:S(2)}) async-start(bf16[8,2,112,256]{3,2,1,0:T(8,128)(2,1)} %get-tuple-element.14), calls=%async_computation.1 | async-start | bytes 1835008 | tf_op jit(solution)/shard_map/all_to_all | solution.py:294
  62.5 0.0 copy-done.5
  62.5 13.0 %all-to-all-done.1.up_ref = bf16[8,2,112,256]{3,2,1,0:T(8,128)(2,1)S(1)} async-done(((bf16[8,2,112,256]{3,2,1,0:T(8,128)(2,1)}), bf16[8,2,112,256]{3,2,1,0:T(8,128)(2,1)S(1)}, u32[]{:S(2)}, u32[]{:S(2)}) %all-to-all-start.1) | async-done | bytes 917536 | tf_op jit(solution)/shard_map/all_to_all | solution.py:294
  75.5 19.8 %backward.1 = (bf16[2,2048,1024]{2,1,0:T(8,128)(2,1)}, bf16[1024,1152]{1,0:T(8,128)(2,1)S(1)}) custom-call(s32[1]{0:T(128)} %bitcast.core_ref, bf16[2,2048,1024]{2,1,0:T(8,128)(2,1)} %bitcast.20, bf16[2,2048,1024]{2,1,0:T(8,128)(2,1)} %copy-done, bf16[2,2048,1024]{2,1,0:T(8,128)(2,1)} %get-tuple-element.12.slope_ref, ...), custom_call_target="tpu_custom_call" | custom-call | tf_op jit(solution)/shard_map/backward/pallas_call | solution.py:225
  95.3 1.1 dynamic-slice_bitcast_fusion
  96.4 0.0 collective-permute-start.3
  96.4 3.2 %collective-permute-done.3 = bf16[32,16,1152]{2,1,0:T(8,128)(2,1)} collective-permute-done((bf16[32,16,1152]{2,1,0:T(8,128)(2,1)}, bf16[32,16,1152]{2,1,0:T(8,128)(2,1)}, u32[]{:S(2)}, u32[]{:S(2)}) %collective-permute-start.3) | collective-permute-done | bytes 1179680 | tf_op jit(solution)/shard_map/ppermute | solution.py:266
  99.6 2.6 %fusion = bf16[32,16,1152]{2,1,0:T(8,128)(2,1)} fusion(bf16[32,16,1152]{2,1,0:T(8,128)(2,1)} %collective-permute-done.3, bf16[32,2,16,1152]{3,2,1,0:T(8,128)(2,1)S(1)} %bitcast.17, s32[]{:T(128)S(6)} %select_n.7), kind=kLoop, calls=%fused_computation.1 | loop fusion | flops 2359296 | bytes 3538948 | tf_op jit(solution)/shard_map/convert_element_type | solution.py:300
  102.2 0.0 copy-start.2
  102.2 7.4 %all-to-all-start.2 = ((bf16[64,8,1152]{2,1,0:T(8,128)(2,1)}), bf16[64,8,1152]{2,1,0:T(8,128)(2,1)S(1)}, u32[]{:S(2)}, u32[]{:S(2)}) async-start(bf16[64,8,1152]{2,1,0:T(8,128)(2,1)} %bitcast.21), calls=%async_computation.2 | async-start | bytes 2359296 | tf_op jit(solution)/shard_map/all_to_all | solution.py:301
  109.7 0.0 copy-done.2
  109.7 0.0 copy-start.4
  109.7 3.4 %copy-done.4 = bf16[2,2048,1024]{2,1,0:T(8,128)(2,1)S(1)} copy-done((bf16[2,2048,1024]{2,1,0:T(8,128)(2,1)S(1)}, bf16[2,2048,1024]{2,1,0:T(8,128)(2,1)}, u32[]{:S(2)}) %copy-start.4) | copy-done | bytes 8388632
  113.1 11.3 %latent_grad.1 = bf16[2,2048,1024]{2,1,0:T(8,128)(2,1)} custom-call(bf16[2,2048,1024]{2,1,0:T(8,128)(2,1)S(1)} %copy-done.4, bf16[1024,1024]{1,0:T(8,128)(2,1)S(1)} %copy-done.2), custom_call_target="tpu_custom_call" | custom-call | flops 8589934592 | bytes 16777216 | tf_op jit(solution)/shard_map/latent_grad/pallas_call | solution.py:248
  124.4 4.5 %all-to-all-done.2 = bf16[64,8,1152]{2,1,0:T(8,128)(2,1)S(1)} async-done(((bf16[64,8,1152]{2,1,0:T(8,128)(2,1)}), bf16[64,8,1152]{2,1,0:T(8,128)(2,1)S(1)}, u32[]{:S(2)}, u32[]{:S(2)}) %all-to-all-start.2) | async-done | bytes 1179680 | tf_op jit(solution)/shard_map/all_to_all | solution.py:301
  128.9 0.2 convert_reduce_fusion
  129.1 0.6 slice_multiply_fusion
  129.7 0.6 slice_multiply_fusion.1
  130.3 0.7 slice_reduce_fusion
  (3 shorter events, 0.1 us)
Async XLA Ops:
  1.8 1.6 %copy-start.1 = (bf16[1024,1024]{1,0:T(8,128)(2,1)S(1)}, bf16[1024,1024]{1,0:T(8,128)(2,1)}, u32[]{:S(2)}) copy-start(bf16[1024,1024]{1,0:T(8,128)(2,1)} %win_ref.3) | copy-start | bytes 6291460
  3.4 32.2 %copy-start.3 = (s32[2048]{0:T(1024)S(1)}, s32[2048]{0:T(1024)}, u32[]{:S(2)}) copy-start(s32[2048]{0:T(1024)} %param.10) | copy-start | bytes 24580
  3.4 32.8 %copy-start.6 = (bf16[1,100,2048]{2,1,0:T(8,128)(2,1)S(1)}, bf16[1,100,2048]{2,1,0:T(8,128)(2,1)}, u32[]{:S(2)}) copy-start(bf16[1,100,2048]{2,1,0:T(8,128)(2,1)} %param.9) | copy-start | bytes 1228804
  24.4 3.2 %copy-start = (bf16[2,2048,1024]{2,1,0:T(8,128)(2,1)}, bf16[2,2048,1024]{2,1,0:T(8,128)(2,1)S(1)}, u32[]{:S(2)}) copy-start(bf16[2,2048,1024]{2,1,0:T(8,128)(2,1)S(1)} %get-tuple-element.11.hidden_ref) | copy-start | bytes 25165828
  27.6 8.7 %copy-start.7 = (f32[100]{0:T(128)S(1)}, f32[100]{0:T(128)}, u32[]{:S(2)}) copy-start(f32[100]{0:T(128)} %param.11) | copy-start | bytes 1204
  27.6 22.6 %all-to-all-start = ((bf16[8,2,112,256]{3,2,1,0:T(8,128)(2,1)}), bf16[8,2,112,256]{3,2,1,0:T(8,128)(2,1)S(1)}, u32[]{:S(2)}, u32[]{:S(2)}) async-start(bf16[8,2,112,256]{3,2,1,0:T(8,128)(2,1)} %get-tuple-element.13), calls=%async_computation | async-start | bytes 1835008 | tf_op jit(solution)/shard_map/all_to_all | solution.py:287
  35.6 26.9 %copy-start.5 = (bf16[1024,100]{0,1:T(8,128)(2,1)S(1)}, bf16[1024,100]{0,1:T(8,128)(2,1)}, u32[]{:S(2)}) copy-start(bf16[1024,100]{0,1:T(8,128)(2,1)} %param.8) | copy-start | bytes 614404
  36.2 1.4 %collective-permute-start = (f32[]{:T(128)}, f32[]{:T(128)}, u32[]{:S(2)}, u32[]{:S(2)}) collective-permute-start(f32[]{:T(128)} %convert_reduce_fusion.1), channel_id=1, source_target_pairs={{0,2},{2,0},{1,3},{3,1},{4,6},{6,4},{5,7},{7,5},{8,10},{10,8},{9,1... | collective-permute-start | bytes 20 | tf_op jit(solution)/shard_map/ppermute | solution.py:266
  38.9 3.7 %collective-permute-start.1 = (f32[]{:T(128)}, f32[]{:T(128)}, u32[]{:S(2)}, u32[]{:S(2)}) collective-permute-start(f32[]{:T(128)} %add.30), channel_id=1, source_target_pairs={{0,4},{4,0},{8,12},{12,8},{1,5},{5,1},{9,13},{13,9},{2,6},{6,2},{1... | collective-permute-start | bytes 20 | tf_op jit(solution)/shard_map/ppermute | solution.py:266
  43.2 5.2 %collective-permute-start.2 = (f32[]{:T(128)}, f32[]{:T(128)}, u32[]{:S(2)}, u32[]{:S(2)}) collective-permute-start(f32[]{:T(128)} %add.31), channel_id=1, source_target_pairs={{0,8},{4,12},{8,0},{12,4},{1,9},{5,13},{9,1},{13,5},{2,10},{6,14},... | collective-permute-start | bytes 20 | tf_op jit(solution)/shard_map/ppermute | solution.py:266
  56.4 19.1 %all-to-all-start.1 = ((bf16[8,2,112,256]{3,2,1,0:T(8,128)(2,1)}), bf16[8,2,112,256]{3,2,1,0:T(8,128)(2,1)S(1)}, u32[]{:S(2)}, u32[]{:S(2)}) async-start(bf16[8,2,112,256]{3,2,1,0:T(8,128)(2,1)} %get-tuple-element.14), calls=%async_computation.1 | async-start | bytes 1835008 | tf_op jit(solution)/shard_map/all_to_all | solution.py:294
  96.4 3.2 %collective-permute-start.3 = (bf16[32,16,1152]{2,1,0:T(8,128)(2,1)}, bf16[32,16,1152]{2,1,0:T(8,128)(2,1)}, u32[]{:S(2)}, u32[]{:S(2)}) collective-permute-start(bf16[32,16,1152]{2,1,0:T(8,128)(2,1)} %dynamic-slice_bitcast_fusion), channel_id=1, source_target_pairs={{0,2},{2,0},{1,3},{3,1},{4,6},{6,4},{5,7},{7,5},{8,10},{10,8},{9,1... | collective-permute-start | bytes 3538952 | tf_op jit(solution)/shard_map/ppermute | solution.py:266
  102.2 7.5 %copy-start.2 = (bf16[1024,1024]{1,0:T(8,128)(2,1)S(1)}, bf16[1024,1024]{1,0:T(8,128)(2,1)}, u32[]{:S(2)}) copy-start(bf16[1024,1024]{1,0:T(8,128)(2,1)} %win_ref.3) | copy-start | bytes 6291460
  102.2 26.7 %all-to-all-start.2 = ((bf16[64,8,1152]{2,1,0:T(8,128)(2,1)}), bf16[64,8,1152]{2,1,0:T(8,128)(2,1)S(1)}, u32[]{:S(2)}, u32[]{:S(2)}) async-start(bf16[64,8,1152]{2,1,0:T(8,128)(2,1)} %bitcast.21), calls=%async_computation.2 | async-start | bytes 2359296 | tf_op jit(solution)/shard_map/all_to_all | solution.py:301
  109.7 3.4 %copy-start.4 = (bf16[2,2048,1024]{2,1,0:T(8,128)(2,1)S(1)}, bf16[2,2048,1024]{2,1,0:T(8,128)(2,1)}, u32[]{:S(2)}) copy-start(bf16[2,2048,1024]{2,1,0:T(8,128)(2,1)} %get-tuple-element.17.gp_ref) | copy-start | bytes 25165828

commit v2 on v1

v2 whole, which is shorter than its diff:
```python
import functools
import math

import jax
import jax.numpy as jnp
from jax import lax
from jax.experimental import pallas as pl
from jax.experimental.pallas import tpu as pltpu
from jax.sharding import Mesh
from jax.sharding import PartitionSpec as P

GELU_C = 0.7978845608
GELU_A = 0.044715
SMOOTH = 0.01
BF16 = jnp.bfloat16
F32 = jnp.float32

BLOCK = 256
VPAD = 112
WIDE = 128
TILE = 512
SUB = 256
EXTRA = 112

FORWARD_VMEM = 20 << 20
SHAPE_VMEM = 12 << 20
SCORE_VMEM = 8 << 20
BACKWARD_VMEM = 28 << 20
LATENT_VMEM = 16 << 20

MEMBER = ("xh", "z")
REST = ("xh", "z", "y", "dp")


def in_hbm(x):
    return pltpu.with_memory_space_constraint(x, pltpu.HBM)


def widen(wide_ref, wout_ref):
    variables = wout_ref.shape[0]
    wide_ref[...] = jnp.zeros_like(wide_ref)
    wide_ref[:variables, :] = wout_ref[...]


def forward_kernel(lat_ref, win_ref, wout_ref, preact_ref, pred_ref, wide_ref):
    @pl.when((pl.program_id(0) == 0) & (pl.program_id(1) == 0))
    def _():
        widen(wide_ref, wout_ref)

    for s in range(TILE // SUB):
        rows = pl.ds(s * SUB, SUB)
        u = jnp.dot(lat_ref[0, rows, :], win_ref[...], preferred_element_type=F32).astype(BF16)
        preact_ref[0, rows, :] = u
        bent = jnp.tanh(u * (BF16(GELU_C) + BF16(GELU_C * GELU_A) * (u * u)))
        twice = u + u * bent
        pred = lax.dot_general(
            twice, wide_ref[...], (((1,), (1,)), ((), ())), preferred_element_type=F32
        )
        pred_ref[s, 0] = (0.5 * pred.T[:VPAD]).astype(BF16)


def forward(latent, w_in, w_out_t):
    members, points, channels = latent.shape
    per = TILE // BLOCK
    tile = pl.BlockSpec((1, TILE, channels), lambda m, i: (m, i, 0))
    return pl.pallas_call(
        forward_kernel,
        grid=(members, points // TILE),
        in_specs=[
            tile,
            pl.BlockSpec((channels, channels), lambda m, i: (0, 0)),
            pl.BlockSpec(w_out_t.shape, lambda m, i: (0, 0)),
        ],
        out_specs=[
            tile,
            pl.BlockSpec((per, 1, VPAD, BLOCK), lambda m, i: (i, m, 0, 0)),
        ],
        out_shape=[
            pltpu.HBM(latent.shape, BF16),
            jax.ShapeDtypeStruct((points // BLOCK, members, VPAD, BLOCK), BF16),
        ],
        scratch_shapes=[pltpu.VMEM((WIDE, channels), BF16)],
        compiler_params=pltpu.CompilerParams(vmem_limit_bytes=FORWARD_VMEM),
        name="forward",
    )(in_hbm(latent), in_hbm(w_in), w_out_t)


def shape_kernel(preact_ref, hidden_ref, slope_ref):
    u = preact_ref[...].astype(F32)
    u2 = u * u
    half = 0.5 + 0.5 * jnp.tanh(u * (GELU_C + (GELU_C * GELU_A) * u2))
    value = u * half
    hidden_ref[...] = value.astype(BF16)
    bend = (2.0 * GELU_C) + (6.0 * GELU_A * GELU_C) * u2
    slope_ref[...] = (half + (value - value * half) * bend).astype(BF16)


def shape(preact):
    members, points, channels = preact.shape
    tile = pl.BlockSpec((1, TILE, channels), lambda m, i: (m, i, 0))
    return pl.pallas_call(
        shape_kernel,
        grid=(members, points // TILE),
        in_specs=[tile],
        out_specs=[tile, tile],
        out_shape=[pltpu.HBM(preact.shape, BF16)] * 2,
        compiler_params=pltpu.CompilerParams(vmem_limit_bytes=SHAPE_VMEM),
        cost_estimate=pl.CostEstimate(
            flops=16 * preact.size, bytes_accessed=6 * preact.size, transcendentals=preact.size
        ),
        name="shape",
    )(in_hbm(preact))


def score_kernel(members, scale_ref, pred_ref, truth_ref, var_ref, area_ref, grad_ref, share_ref):
    per = pred_ref.shape[1]
    scale = scale_ref[0, 0]
    self_phi = members * math.sqrt(SMOOTH) / (2.0 * (members - 1))

    smooth = BF16(SMOOTH)

    def parts(d):
        q = d * d + smooth
        r = lax.rsqrt(q)
        return q * r, d * r

    def rows16(step, total):
        rows = pl.ds(pl.multiple_of(step * 16, 16), 16)
        for lane in range(BLOCK // 128):
            lanes = pl.ds(lane * 128, 128)
            x = [pred_ref[m // per, m % per, rows, lanes] for m in range(members)]
            truth = truth_ref[rows, lanes]
            weight = var_ref[rows, lanes] * (area_ref[0, :, lanes].astype(F32) * scale)
            grads = [None] * members
            pair_phi = jnp.zeros((16, 128), F32)
            for m in range(members - 1):
                row_phi = None
                for k in range(m + 1, members):
                    p, g = parts(x[m] - x[k])
                    row_phi = p if row_phi is None else row_phi + p
                    grads[m] = g if grads[m] is None else grads[m] + g
                    grads[k] = -g if grads[k] is None else grads[k] - g
                pair_phi = pair_phi + row_phi.astype(F32)
            truth_phi = jnp.zeros((16, 128), F32)
            for m in range(members):
                p, g = parts(x[m] - truth)
                truth_phi = truth_phi + p.astype(F32)
                grad = weight * (g.astype(F32) - grads[m].astype(F32) * (1.0 / (members - 1)))
                grad_ref[m // per, m % per, rows, lanes] = grad.astype(BF16)
            share = weight * (truth_phi - pair_phi * (1.0 / (members - 1)) - self_phi)
            total = total + share[:8] + share[8:]
        return total

    share_ref[...] = lax.fori_loop(0, VPAD // 16, rows16, jnp.zeros((8, 128), F32))


def score(me, scale, every, truth, var_weight, area):
    devices, per = every.shape[:2]
    members = devices * per
    grid_spec = pltpu.PrefetchScalarGridSpec(
        num_scalar_prefetch=1,
        grid=(1,),
        in_specs=[
            pl.BlockSpec(memory_space=pltpu.SMEM),
            pl.BlockSpec(every.shape, lambda i, me: (0, 0, 0, 0)),
            pl.BlockSpec((VPAD, BLOCK), lambda i, me: (0, me[0])),
            pl.BlockSpec((VPAD, BLOCK), lambda i, me: (0, 0)),
            pl.BlockSpec((1, 1, BLOCK), lambda i, me: (me[0], 0, 0)),
        ],
        out_specs=[
            pl.BlockSpec(every.shape, lambda i, me: (0, 0, 0, 0)),
            pl.BlockSpec((8, 128), lambda i, me: (0, 0)),
        ],
    )

    def kernel(me_ref, *refs):
        score_kernel(members, *refs)

    return pl.pallas_call(
        kernel,
        grid_spec=grid_spec,
        out_shape=[
            jax.ShapeDtypeStruct(every.shape, BF16),
            jax.ShapeDtypeStruct((8, 128), F32),
        ],
        compiler_params=pltpu.CompilerParams(vmem_limit_bytes=SCORE_VMEM),
        name="score",
    )(me, scale, every, truth, var_weight, area)


def backward_kernel(
    core_ref, lat_ref, hidden_ref, slope_ref, up_ref, wout_ref, share_ref,
    gp_ref, mine_ref, other_ref, acc_in, acc_out, wide_ref,
):
    step, last = pl.program_id(0), pl.num_programs(0) - 1
    channels = lat_ref.shape[2]

    @pl.when(step == 0)
    def _():
        acc_in[...] = jnp.zeros_like(acc_in)
        acc_out[...] = jnp.zeros_like(acc_out)
        widen(wide_ref, wout_ref)

    for s in range(TILE // BLOCK):
        rows = pl.ds(s * BLOCK, BLOCK)
        block = jnp.concatenate(
            [up_ref[s, 0].astype(F32), jnp.zeros((WIDE - VPAD, BLOCK), F32)], axis=0
        )
        grad_hidden = jnp.dot(block.T.astype(BF16), wide_ref[...], preferred_element_type=F32)
        gp_ref[0, rows, :] = grad_hidden.astype(BF16) * slope_ref[0, rows, :]
    ups = jnp.concatenate([up_ref[s, 0] for s in range(TILE // BLOCK)], axis=1)
    acc_out[:VPAD, :] += jnp.dot(ups, hidden_ref[0], preferred_element_type=F32)
    product = lax.dot_general(
        lat_ref[0], gp_ref[0], (((0,), (0,)), ((), ())), preferred_element_type=F32
    )
    acc_in[...] += product.reshape(acc_in.shape)

    @pl.when(step == last)
    def _():
        core = core_ref[0]
        share = jnp.sum(share_ref[...])
        high = share.astype(BF16).astype(F32)
        middle = (share - high).astype(BF16).astype(F32)
        low = share - high - middle
        row = lax.broadcasted_iota(jnp.int32, acc_out.shape, 0) - (EXTRA + 3 * core)
        whole = jnp.where(
            row == 0,
            high,
            jnp.where(row == 1, middle, jnp.where(row == 2, low, acc_out[...])),
        )
        acc_out[...] = whole
        for chunk in range(channels // WIDE):
            piece = acc_out[:, chunk * WIDE : (chunk + 1) * WIDE].T.reshape(-1, 16, WIDE)
            for j in range(WIDE // 32):
                @pl.when(core == 0)
                def _():
                    mine_ref[chunk * 4 + j, :, channels:] = piece[2 * j].astype(BF16)
                    other_ref[chunk * 4 + j, :, channels:] = piece[2 * j + 1].astype(BF16)

                @pl.when(core == 1)
                def _():
                    mine_ref[chunk * 4 + j, :, channels:] = piece[2 * j + 1].astype(BF16)
                    other_ref[chunk * 4 + j, :, channels:] = piece[2 * j].astype(BF16)

        def group(g, carry):
            mine_ref[g, :, :channels] = acc_in[2 * g + core].astype(BF16)
            other_ref[g, :, :channels] = acc_in[2 * g + 1 - core].astype(BF16)
            return carry

        lax.fori_loop(0, channels // 32, group, 0, unroll=4)


def backward(core, latent, hidden, slopes, upstream, w_out_t, share):
    members, points, channels = latent.shape
    steps = points // TILE
    per = TILE // BLOCK
    tile = pl.BlockSpec((1, TILE, channels), lambda i, c: (i // steps, i % steps, 0))
    half = (channels // 32, 16, channels + WIDE)
    grid_spec = pltpu.PrefetchScalarGridSpec(
        num_scalar_prefetch=1,
        grid=(members * steps,),
        in_specs=[
            tile,
            tile,
            tile,
            pl.BlockSpec((per, 1, VPAD, BLOCK), lambda i, c: (i % steps, i // steps, 0, 0)),
            pl.BlockSpec(w_out_t.shape, lambda i, c: (0, 0)),
            pl.BlockSpec((8, 128), lambda i, c: (0, 0)),
        ],
        out_specs=[
            tile,
            pl.BlockSpec(half, lambda i, c: (0, 0, 0)),
            pl.BlockSpec(half, lambda i, c: (0, 0, 0)),
        ],
        scratch_shapes=[
            pltpu.VMEM((channels // 16, 16, channels), F32),
            pltpu.VMEM((WIDE, channels), F32),
            pltpu.VMEM((WIDE, channels), BF16),
        ],
    )
    return pl.pallas_call(
        backward_kernel,
        grid_spec=grid_spec,
        out_shape=[
            pltpu.HBM(latent.shape, BF16),
            jax.ShapeDtypeStruct(half, BF16),
            jax.ShapeDtypeStruct(half, BF16),
        ],
        compiler_params=pltpu.CompilerParams(vmem_limit_bytes=BACKWARD_VMEM),
        name="backward",
    )(core, in_hbm(latent), in_hbm(hidden), in_hbm(slopes), upstream, w_out_t, share)


def latent_kernel(gp_ref, win_ref, out_ref):
    for s in range(TILE // SUB):
        rows = pl.ds(s * SUB, SUB)
        out_ref[0, rows, :] = lax.dot_general(
            gp_ref[0, rows, :], win_ref[...], (((1,), (1,)), ((), ())), preferred_element_type=F32
        ).astype(BF16)


def latent_grad(gp, w_in):
    members, points, channels = gp.shape
    tile = pl.BlockSpec((1, TILE, channels), lambda m, i: (m, i, 0))
    return pl.pallas_call(
        latent_kernel,
        grid=(members, points // TILE),
        in_specs=[tile, pl.BlockSpec((channels, channels), lambda m, i: (0, 0))],
        out_specs=tile,
        out_shape=pltpu.HBM(gp.shape, BF16),
        compiler_params=pltpu.CompilerParams(vmem_limit_bytes=LATENT_VMEM),
        cost_estimate=pl.CostEstimate(
            flops=2 * members * points * channels * channels,
            bytes_accessed=4 * members * points * channels,
            transcendentals=0,
        ),
        name="latent_grad",
    )(in_hbm(gp), w_in)


def exchange(x, axis, xor):
    size = lax.axis_size(axis)
    return lax.ppermute(x, axis, [(i, i ^ xor) for i in range(size)])


def body(latent, w_in, w_out, targets, area_units, var_weight):
    date_count, per, points, channels = latent.shape
    variables = w_out.shape[1]
    member_devices = lax.axis_size("xh") * lax.axis_size("z")
    members = per * member_devices
    npoints = points * lax.axis_size("y") * lax.axis_size("core")
    dates = date_count * lax.axis_size("dp")
    me = (lax.axis_index("xh") * lax.axis_size("z") + lax.axis_index("z")).astype(jnp.int32)
    core = lax.axis_index("core").astype(jnp.int32)

    area_total = jnp.sum(area_units.astype(F32))
    for axis, xor in (("core", 1), ("y", 1), ("y", 2)):
        area_total = area_total + exchange(area_total, axis, xor)
    scale = (npoints / area_total).reshape(1, 1)

    rows = latent.reshape(date_count * per, points, channels)
    w_out_t = w_out.T
    preact, pred = forward(rows, w_in, w_out_t)
    every = lax.all_to_all(pred, MEMBER, 0, 0, tiled=True)
    hidden, slopes = shape(preact)
    truth = jnp.pad(targets[0], ((0, VPAD - variables), (0, 0)))
    var_wide = jnp.broadcast_to(
        jnp.pad(var_weight, (0, VPAD - variables))[:, None], (VPAD, BLOCK)
    )
    area = area_units.reshape(points // BLOCK, 1, BLOCK)
    grad_pred, share = score(me.reshape(1), scale, every, truth, var_wide, area)
    upstream = lax.all_to_all(grad_pred, MEMBER, 0, 0, tiled=True)
    gp, mine, other = backward(core.reshape(1), rows, hidden, slopes, upstream, w_out_t, share)
    wide = channels + WIDE
    both = (mine.astype(F32) + exchange(other, "core", 1).astype(F32)).astype(BF16)
    pieces = lax.all_to_all(both.reshape(-1, 8, wide), REST, 0, 0, tiled=True)
    grad_latent = latent_grad(gp, w_in)
    total = jnp.sum(pieces.astype(F32), axis=0)
    grad_scale = math.sqrt(dates * members * npoints)
    loss = jnp.sum(total[0, channels + EXTRA : channels + EXTRA + 6]) / (dates * npoints * variables)
    return (
        loss,
        grad_latent.reshape(latent.shape),
        total[:, :channels] / grad_scale,
        total[:, channels : channels + variables] / grad_scale,
    )


def solution(mesh):
    fine = Mesh(mesh.devices.reshape(2, 4, 4, 2, 2), ("xh", "z", "y", "core", "dp"))
    return jax.shard_map(
        body,
        mesh=fine,
        in_specs=(
            P("dp", MEMBER, ("y", "core"), None),
            P(),
            P(),
            P("dp", None, ("y", "core")),
            P(("y", "core")),
            P(),
        ),
        out_specs=(
            P(),
            P("dp", MEMBER, ("y", "core"), None),
            P(("xh", "z", "y", "core", "dp"), None),
            P(("xh", "z", "y", "core", "dp"), None),
        ),
        check_vma=False,
    )
```

time: 133 us -> 125 us (0.940)
  waiting for transfers between devices: 24.5 us -> 12.5 us
  Pallas kernels: 58.2 us -> 69.8 us
  local copies, waits for them, and re-layouts: 10.6 us -> 1.06 us
  starting transfers between devices: 29.1 us -> 32 us
    pallas_call x1 -> x2, Pallas kernels: 19.8 us -> 33.1 us  [the longest x1 20.2 us: backward(): pl.pallas_call(backward_kernel, grid_spec=grid_spec, out_shape=[pltpu.HBM...]
    all_to_all x1, waiting for transfers between devices: 13 us -> 0.19 us  [body(): upstream = lax.all_to_all(grad_pred, MEMBER, 0, 0, tiled=True)]
    unnamed x17 -> x12, local copies, waits for them, and re-layouts: 9.31 us -> 0.95 us
    pallas_call x1, Pallas kernels: 21 us -> 16.9 us  [forward(): pl.pallas_call(forward_kernel, grid=(members, points // TILE), in_specs=[...]
    all_to_all x1, starting transfers between devices: 7.44 us -> 10.7 us  [body(): pieces = lax.all_to_all(both.reshape(-1, 8, wide), REST, 0, 0, tiled=True)]
    pallas_call x1, Pallas kernels: 11.3 us -> 13.7 us  [latent_grad(): pl.pallas_call(latent_kernel, grid=(members, points // TILE), in_specs=[t...]
  transfers between devices with their start and end apart: 7 -> 7, of which waited for: 7 -> 7; matrix products, arithmetic and copies ran while one was open for 1% -> 1% of each run, Pallas kernels for 9% -> 21%
where the time goes in v2:
time: 125 us; the launch traced here: 124 us
  Pallas kernels  69.8 us (56%)
  starting transfers between devices  32 us (26%)
  waiting for transfers between devices  12.5 us (10%)
  between operations  4.89 us (4%)
  other arithmetic  4.03 us (3%)
    pallas_call x1, Pallas kernels, backward(): pl.pallas_call(backward_kernel, grid_spec=grid_spec, out_shape=[pltpu.HBM...  20.2 us
    pallas_call x1, Pallas kernels, forward(): pl.pallas_call(forward_kernel, grid=(members, points // TILE), in_specs=[...  16.9 us
    pallas_call x1, Pallas kernels, latent_grad(): pl.pallas_call(latent_kernel, grid=(members, points // TILE), in_specs=[t...  13.7 us
    pallas_call x1, Pallas kernels, shape(): pl.pallas_call(shape_kernel, grid=(members, points // TILE), in_specs=[ti...  12.8 us
    all_to_all x1, starting transfers between devices, body(): pieces = lax.all_to_all(both.reshape(-1, 8, wide), REST, 0, 0, tiled=True)  10.7 us
    all_to_all x1, starting transfers between devices, body(): every = lax.all_to_all(pred, MEMBER, 0, 0, tiled=True)  7.86 us
    ppermute x4, starting transfers between devices, exchange(): return lax.ppermute(x, axis, [(i, i ^ xor) for i in range(size)])  7.53 us
    pallas_call x1, Pallas kernels, score(): pl.pallas_call(kernel, grid_spec=grid_spec, out_shape=[jax.ShapeDtypeStru...  6.16 us
  transfers between devices with their start and end apart: 7, of which 7 were waited for; matrix products, arithmetic and copies ran while one was open for 1% of the time, Pallas kernels for 21%

profile of v2, /device:TPU:0, one launch (start us, length us, event | category | flops | bytes accessed | tf_op | source)
XLA Modules:
  0.0 124.4 jit_solution(15783218047072479586)
XLA Ops:
  0.6 0.0 copy-start.1
  0.6 0.9 copy-done.1
  1.6 0.0 copy-start.3
  1.6 0.0 copy-start.5
  1.6 0.0 copy-start.4
  1.6 16.9 %forward.1 = (bf16[2,2048,1024]{2,1,0:T(8,128)(2,1)}, bf16[8,2,112,256]{3,2,1,0:T(8,128)(2,1)}) custom-call(bf16[2,2048,1024]{2,1,0:T(8,128)(2,1)} %bitcast.12, bf16[1024,1024]{1,0:T(8,128)(2,1)} %win_ref.3, bf16[100,1024]{1,0:T(8,128)(2,1)S(1)} %bitcast.9), custom_call_target="tpu_custom_call" | custom-call | tf_op jit(solution)/shard_map/forward/pallas_call | solution.py:66
  18.5 7.9 %all-to-all-start = ((bf16[8,2,112,256]{3,2,1,0:T(8,128)(2,1)}), bf16[8,2,112,256]{3,2,1,0:T(8,128)(2,1)S(1)}, u32[]{:S(2)}, u32[]{:S(2)}) async-start(bf16[8,2,112,256]{3,2,1,0:T(8,128)(2,1)} %get-tuple-element.16), calls=%async_computation | async-start | bytes 1835008 | tf_op jit(solution)/shard_map/all_to_all | solution.py:344
  26.4 0.0 copy-done.3
  26.4 0.6 convert_reduce_fusion.1
  27.0 0.0 collective-permute-start
  27.0 0.0 copy-done.5
  27.0 0.0 copy-done.4
  27.0 1.3 %collective-permute-done = f32[]{:T(128)} collective-permute-done((f32[]{:T(128)}, f32[]{:T(128)}, u32[]{:S(2)}, u32[]{:S(2)}) %collective-permute-start) | collective-permute-done | bytes 36 | tf_op jit(solution)/shard_map/ppermute | solution.py:323
  29.6 2.9 %collective-permute-start.1 = (f32[]{:T(128)}, f32[]{:T(128)}, u32[]{:S(2)}, u32[]{:S(2)}) collective-permute-start(f32[]{:T(128)} %add.20), channel_id=1, source_target_pairs={{0,4},{4,0},{8,12},{12,8},{1,5},{5,1},{9,13},{13,9},{2,6},{6,2},{1... | collective-permute-start | bytes 20 | tf_op jit(solution)/shard_map/ppermute | solution.py:323
  32.5 0.8 collective-permute-done.1
  33.9 4.6 %collective-permute-start.2 = (f32[]{:T(128)}, f32[]{:T(128)}, u32[]{:S(2)}, u32[]{:S(2)}) collective-permute-start(f32[]{:T(128)} %add.21), channel_id=1, source_target_pairs={{0,8},{4,12},{8,0},{12,4},{1,9},{5,13},{9,1},{13,5},{2,10},{6,14},... | collective-permute-start | bytes 20 | tf_op jit(solution)/shard_map/ppermute | solution.py:323
  38.4 0.7 collective-permute-done.2
  39.7 1.3 %all-to-all-done.refs_1_ = bf16[8,2,112,256]{3,2,1,0:T(8,128)(2,1)S(1)} async-done(((bf16[8,2,112,256]{3,2,1,0:T(8,128)(2,1)}), bf16[8,2,112,256]{3,2,1,0:T(8,128)(2,1)S(1)}, u32[]{:S(2)}, u32[]{:S(2)}) %all-to-all-start) | async-done | bytes 917536 | tf_op jit(solution)/shard_map/all_to_all | solution.py:344
  41.0 0.1 broadcast_in_dim.2.refs_3_
  41.0 6.2 %score.1 = (bf16[8,2,112,256]{3,2,1,0:T(8,128)(2,1)}, f32[8,128]{1,0:T(8,128)S(1)}) custom-call(s32[1]{0:T(128)} %bitcast.3.me_ref, f32[1,1]{1,0:T(1,128)} %bitcast.4.refs_0_, bf16[8,2,112,256]{3,2,1,0:T(8,128)(2,1)S(1)} %all-to-all-done.refs_1_, bf16[112,2048]{1,0:T(8,128)(2,1)S(1)} %pad.8.refs_2_, f32[112,256]{1,0:T(8,128)S(1)} %broadcast_in_dim.2.refs_3_, ...), custom_call_target="tpu_custom_call" | custom-call | tf_op jit(solution)/shard_map/score/pallas_call | solution.py:179
  47.2 6.0 %all-to-all-start.1 = ((bf16[8,2,112,256]{3,2,1,0:T(8,128)(2,1)}), bf16[8,2,112,256]{3,2,1,0:T(8,128)(2,1)S(1)}, u32[]{:S(2)}, u32[]{:S(2)}) async-start(bf16[8,2,112,256]{3,2,1,0:T(8,128)(2,1)} %get-tuple-element.17), calls=%async_computation.1 | async-start | bytes 1835008 | tf_op jit(solution)/shard_map/all_to_all | solution.py:352
  53.2 0.0 copy-start.2
  53.2 12.8 %shape.1 = (bf16[2,2048,1024]{2,1,0:T(8,128)(2,1)}, bf16[2,2048,1024]{2,1,0:T(8,128)(2,1)}) custom-call(bf16[2,2048,1024]{2,1,0:T(8,128)(2,1)} %get-tuple-element.13.preact_ref), custom_call_target="tpu_custom_call" | custom-call | flops 67108864 | bytes 25165824 | tf_op jit(solution)/shard_map/shape/pallas_call | solution.py:101
  66.0 0.2 all-to-all-done.1.up_ref
  66.2 0.0 copy-done.2
  66.2 20.2 %backward.1 = (bf16[2,2048,1024]{2,1,0:T(8,128)(2,1)}, bf16[32,16,1152]{2,1,0:T(8,128)(2,1)S(1)}, bf16[32,16,1152]{2,1,0:T(8,128)(2,1)S(1)}) custom-call(s32[1]{0:T(128)} %bitcast.core_ref, bf16[2,2048,1024]{2,1,0:T(8,128)(2,1)} %bitcast.13, bf16[2,2048,1024]{2,1,0:T(8,128)(2,1)} %get-tuple-element.14.hidden_ref, ...), custom_call_target="tpu_custom_call" | custom-call | tf_op jit(solution)/shard_map/backward/pallas_call | solution.py:281
  86.4 0.0 collective-permute-start.3
  86.4 2.8 %collective-permute-done.3 = bf16[32,16,1152]{2,1,0:T(8,128)(2,1)S(1)} collective-permute-done((bf16[32,16,1152]{2,1,0:T(8,128)(2,1)S(1)}, bf16[32,16,1152]{2,1,0:T(8,128)(2,1)S(1)}, u32[]{:S(2)}, u32[]{:S(2)}) %collective-permute-start.3) | collective-permute-done | bytes 1179680 | tf_op jit(solution)/shard_map/ppermute | solution.py:323
  89.3 0.0 copy-start
  89.3 1.4 %add_convert_fusion = bf16[32,16,1152]{2,1,0:T(8,128)(2,1)} fusion(bf16[32,16,1152]{2,1,0:T(8,128)(2,1)S(1)} %collective-permute-done.3, bf16[32,16,1152]{2,1,0:T(8,128)(2,1)S(1)} %get-tuple-element.19), kind=kLoop, calls=%fused_computation.1 | loop fusion | flops 2359296 | bytes 3538944 | tf_op jit(solution)/shard_map/convert_element_type | solution.py:355
  90.6 10.7 %all-to-all-start.2 = ((bf16[64,8,1152]{2,1,0:T(8,128)(2,1)}), bf16[64,8,1152]{2,1,0:T(8,128)(2,1)S(1)}, u32[]{:S(2)}, u32[]{:S(2)}) async-start(bf16[64,8,1152]{2,1,0:T(8,128)(2,1)} %bitcast.7), calls=%async_computation.2 | async-start | bytes 2359296 | tf_op jit(solution)/shard_map/all_to_all | solution.py:356
  101.3 0.0 copy-done
  101.3 13.7 %latent_grad.1 = bf16[2,2048,1024]{2,1,0:T(8,128)(2,1)} custom-call(bf16[2,2048,1024]{2,1,0:T(8,128)(2,1)} %get-tuple-element.21.gp_ref, bf16[1024,1024]{1,0:T(8,128)(2,1)S(1)} %copy-done), custom_call_target="tpu_custom_call" | custom-call | flops 8589934592 | bytes 16777216 | tf_op jit(solution)/shard_map/latent_grad/pallas_call | solution.py:305
  115.0 5.5 %all-to-all-done.2 = bf16[64,8,1152]{2,1,0:T(8,128)(2,1)S(1)} async-done(((bf16[64,8,1152]{2,1,0:T(8,128)(2,1)}), bf16[64,8,1152]{2,1,0:T(8,128)(2,1)S(1)}, u32[]{:S(2)}, u32[]{:S(2)}) %all-to-all-start.2) | async-done | bytes 1179680 | tf_op jit(solution)/shard_map/all_to_all | solution.py:356
  120.5 0.2 convert_reduce_fusion
  120.7 0.7 slice_reduce_fusion
  121.4 0.6 slice_multiply_fusion.1
  122.0 0.6 slice_multiply_fusion
  (2 shorter events, 0.0 us)
Async XLA Ops:
  0.6 0.9 copy-start.1
  1.6 24.8 %copy-start.3 = (s32[2048]{0:T(1024)S(1)}, s32[2048]{0:T(1024)}, u32[]{:S(2)}) copy-start(s32[2048]{0:T(1024)} %param.10) | copy-start | bytes 24580
  1.6 25.4 %copy-start.5 = (f32[100]{0:T(128)S(1)}, f32[100]{0:T(128)}, u32[]{:S(2)}) copy-start(f32[100]{0:T(128)} %param.11) | copy-start | bytes 1204
  1.6 25.4 %copy-start.4 = (bf16[1,100,2048]{2,1,0:T(8,128)(2,1)S(1)}, bf16[1,100,2048]{2,1,0:T(8,128)(2,1)}, u32[]{:S(2)}) copy-start(bf16[1,100,2048]{2,1,0:T(8,128)(2,1)} %param.9) | copy-start | bytes 1228804
  18.5 22.5 %all-to-all-start = ((bf16[8,2,112,256]{3,2,1,0:T(8,128)(2,1)}), bf16[8,2,112,256]{3,2,1,0:T(8,128)(2,1)S(1)}, u32[]{:S(2)}, u32[]{:S(2)}) async-start(bf16[8,2,112,256]{3,2,1,0:T(8,128)(2,1)} %get-tuple-element.16), calls=%async_computation | async-start | bytes 1835008 | tf_op jit(solution)/shard_map/all_to_all | solution.py:344
  27.0 1.4 %collective-permute-start = (f32[]{:T(128)}, f32[]{:T(128)}, u32[]{:S(2)}, u32[]{:S(2)}) collective-permute-start(f32[]{:T(128)} %convert_reduce_fusion.1), channel_id=1, source_target_pairs={{0,2},{2,0},{1,3},{3,1},{4,6},{6,4},{5,7},{7,5},{8,10},{10,8},{9,1... | collective-permute-start | bytes 20 | tf_op jit(solution)/shard_map/ppermute | solution.py:323
  29.6 3.7 %collective-permute-start.1 = (f32[]{:T(128)}, f32[]{:T(128)}, u32[]{:S(2)}, u32[]{:S(2)}) collective-permute-start(f32[]{:T(128)} %add.20), channel_id=1, source_target_pairs={{0,4},{4,0},{8,12},{12,8},{1,5},{5,1},{9,13},{13,9},{2,6},{6,2},{1... | collective-permute-start | bytes 20 | tf_op jit(solution)/shard_map/ppermute | solution.py:323
  33.9 5.2 %collective-permute-start.2 = (f32[]{:T(128)}, f32[]{:T(128)}, u32[]{:S(2)}, u32[]{:S(2)}) collective-permute-start(f32[]{:T(128)} %add.21), channel_id=1, source_target_pairs={{0,8},{4,12},{8,0},{12,4},{1,9},{5,13},{9,1},{13,5},{2,10},{6,14},... | collective-permute-start | bytes 20 | tf_op jit(solution)/shard_map/ppermute | solution.py:323
  47.2 19.0 %all-to-all-start.1 = ((bf16[8,2,112,256]{3,2,1,0:T(8,128)(2,1)}), bf16[8,2,112,256]{3,2,1,0:T(8,128)(2,1)S(1)}, u32[]{:S(2)}, u32[]{:S(2)}) async-start(bf16[8,2,112,256]{3,2,1,0:T(8,128)(2,1)} %get-tuple-element.17), calls=%async_computation.1 | async-start | bytes 1835008 | tf_op jit(solution)/shard_map/all_to_all | solution.py:352
  53.2 13.0 %copy-start.2 = (bf16[1024,100]{0,1:T(8,128)(2,1)S(1)}, bf16[1024,100]{0,1:T(8,128)(2,1)}, u32[]{:S(2)}) copy-start(bf16[1024,100]{0,1:T(8,128)(2,1)} %param.8) | copy-start | bytes 614404
  86.4 2.8 %collective-permute-start.3 = (bf16[32,16,1152]{2,1,0:T(8,128)(2,1)S(1)}, bf16[32,16,1152]{2,1,0:T(8,128)(2,1)S(1)}, u32[]{:S(2)}, u32[]{:S(2)}) collective-permute-start(bf16[32,16,1152]{2,1,0:T(8,128)(2,1)S(1)} %get-tuple-element.20), channel_id=1, source_target_pairs={{0,2},{2,0},{1,3},{3,1},{4,6},{6,4},{5,7},{7,5},{8,10},{10,8},{9,1... | collective-permute-start | bytes 3538952 | tf_op jit(solution)/shard_map/ppermute | solution.py:323
  89.3 12.0 %copy-start = (bf16[1024,1024]{1,0:T(8,128)(2,1)S(1)}, bf16[1024,1024]{1,0:T(8,128)(2,1)}, u32[]{:S(2)}) copy-start(bf16[1024,1024]{1,0:T(8,128)(2,1)} %win_ref.3) | copy-start | bytes 6291460
  90.6 29.9 %all-to-all-start.2 = ((bf16[64,8,1152]{2,1,0:T(8,128)(2,1)}), bf16[64,8,1152]{2,1,0:T(8,128)(2,1)S(1)}, u32[]{:S(2)}, u32[]{:S(2)}) async-start(bf16[64,8,1152]{2,1,0:T(8,128)(2,1)} %bitcast.7), calls=%async_computation.2 | async-start | bytes 2359296 | tf_op jit(solution)/shard_map/all_to_all | solution.py:356

commit v3 on v2

--- a/solution.py
+++ b/solution.py
@@ -18,15 +18,15 @@
 BLOCK = 256
 VPAD = 112
 WIDE = 128
-TILE = 512
+TILE = 1024
 SUB = 256
 EXTRA = 112
 
-FORWARD_VMEM = 20 << 20
-SHAPE_VMEM = 12 << 20
-SCORE_VMEM = 8 << 20
-BACKWARD_VMEM = 28 << 20
-LATENT_VMEM = 16 << 20
+FORWARD_VMEM = 40 << 20
+SHAPE_VMEM = 36 << 20
+SCORE_VMEM = 16 << 20
+BACKWARD_VMEM = 50 << 20
+LATENT_VMEM = 40 << 20
 
 MEMBER = ("xh", "z")
 REST = ("xh", "z", "y", "dp")
@@ -82,7 +82,7 @@
         scratch_shapes=[pltpu.VMEM((WIDE, channels), BF16)],
         compiler_params=pltpu.CompilerParams(vmem_limit_bytes=FORWARD_VMEM),
         name="forward",
-    )(in_hbm(latent), in_hbm(w_in), w_out_t)
+    )(in_hbm(latent), in_hbm(w_in), in_hbm(w_out_t))
 
 
 def shape_kernel(preact_ref, hidden_ref, slope_ref):
@@ -112,65 +112,64 @@
     )(in_hbm(preact))
 
 
-def score_kernel(members, scale_ref, pred_ref, truth_ref, var_ref, area_ref, grad_ref, share_ref):
+def score_kernel(
+    members, scale_ref, pred_ref, truth_ref, var_ref, area_ref, grad_ref, share_ref, held_ref
+):
     per = pred_ref.shape[1]
     scale = scale_ref[0, 0]
     self_phi = members * math.sqrt(SMOOTH) / (2.0 * (members - 1))
 
-    smooth = BF16(SMOOTH)
-
-    def parts(d):
-        q = d * d + smooth
-        r = lax.rsqrt(q)
-        return q * r, d * r
-
-    def rows16(step, total):
-        rows = pl.ds(pl.multiple_of(step * 16, 16), 16)
-        for lane in range(BLOCK // 128):
-            lanes = pl.ds(lane * 128, 128)
-            x = [pred_ref[m // per, m % per, rows, lanes] for m in range(members)]
-            truth = truth_ref[rows, lanes]
-            weight = var_ref[rows, lanes] * (area_ref[0, :, lanes].astype(F32) * scale)
+    @pl.when(pl.program_id(0) == 0)
+    def _():
+        share_ref[...] = jnp.zeros_like(share_ref)
+
+    for lane in range(BLOCK // 128):
+        lanes = pl.ds(lane * 128, 128)
+        for half in range(2):
+            rows = slice(8 * half, 8 * half + 8)
+            truth = truth_ref[:, lanes].astype(F32)[rows]
+            x = [pred_ref[m // per, m % per, :, lanes].astype(F32)[rows] - truth for m in range(members)]
+            weight = (var_ref[:, lanes] * (area_ref[0, :, lanes].astype(F32) * scale))[rows]
             grads = [None] * members
-            pair_phi = jnp.zeros((16, 128), F32)
+            roots = None
             for m in range(members - 1):
-                row_phi = None
                 for k in range(m + 1, members):
-                    p, g = parts(x[m] - x[k])
-                    row_phi = p if row_phi is None else row_phi + p
+                    d = x[m] - x[k]
+                    r = lax.rsqrt(d * d + SMOOTH)
+                    g = d * r
+                    roots = r if roots is None else roots + r
                     grads[m] = g if grads[m] is None else grads[m] + g
                     grads[k] = -g if grads[k] is None else grads[k] - g
-                pair_phi = pair_phi + row_phi.astype(F32)
-            truth_phi = jnp.zeros((16, 128), F32)
+            score = None
             for m in range(members):
-                p, g = parts(x[m] - truth)
-                truth_phi = truth_phi + p.astype(F32)
-                grad = weight * (g.astype(F32) - grads[m].astype(F32) * (1.0 / (members - 1)))
-                grad_ref[m // per, m % per, rows, lanes] = grad.astype(BF16)
-            share = weight * (truth_phi - pair_phi * (1.0 / (members - 1)) - self_phi)
-            total = total + share[:8] + share[8:]
-        return total
-
-    share_ref[...] = lax.fori_loop(0, VPAD // 16, rows16, jnp.zeros((8, 128), F32))
+                q = x[m] * x[m] + SMOOTH
+                r = lax.rsqrt(q)
+                spread = grads[m] * (1.0 / (members - 1))
+                mine = q * r - x[m] * spread
+                score = mine if score is None else score + mine
+                held_ref[m, rows, :] = weight * (x[m] * r - spread)
+            score = score - roots * (SMOOTH / (members - 1)) - self_phi
+            share_ref[...] += weight * score
+        for m in range(members):
+            grad_ref[m // per, m % per, :, lanes] = held_ref[m].astype(BF16)
 
 
 def score(me, scale, every, truth, var_weight, area):
     devices, per = every.shape[:2]
     members = devices * per
+    block = pl.BlockSpec((devices, per, 16, BLOCK), lambda i, me: (0, 0, i, 0))
     grid_spec = pltpu.PrefetchScalarGridSpec(
         num_scalar_prefetch=1,
-        grid=(1,),
+        grid=(VPAD // 16,),
         in_specs=[
             pl.BlockSpec(memory_space=pltpu.SMEM),
-            pl.BlockSpec(every.shape, lambda i, me: (0, 0, 0, 0)),
-            pl.BlockSpec((VPAD, BLOCK), lambda i, me: (0, me[0])),
-            pl.BlockSpec((VPAD, BLOCK), lambda i, me: (0, 0)),
+            block,
+            pl.BlockSpec((16, BLOCK), lambda i, me: (i, me[0])),
+            pl.BlockSpec((16, BLOCK), lambda i, me: (i, 0)),
             pl.BlockSpec((1, 1, BLOCK), lambda i, me: (me[0], 0, 0)),
         ],
-        out_specs=[
-            pl.BlockSpec(every.shape, lambda i, me: (0, 0, 0, 0)),
-            pl.BlockSpec((8, 128), lambda i, me: (0, 0)),
-        ],
+        out_specs=[block, pl.BlockSpec((8, 128), lambda i, me: (0, 0))],
+        scratch_shapes=[pltpu.VMEM((members, 16, 128), F32)],
     )
 
     def kernel(me_ref, *refs):
@@ -188,9 +187,17 @@
     )(me, scale, every, truth, var_weight, area)
 
 
+def preact_grad(up_ref, slope_ref, wide, s):
+    block = jnp.concatenate(
+        [up_ref[s, 0].astype(F32), jnp.zeros((WIDE - VPAD, BLOCK), F32)], axis=0
+    )
+    grad_hidden = jnp.dot(block.T.astype(BF16), wide, preferred_element_type=F32)
+    return grad_hidden.astype(BF16) * slope_ref[0, pl.ds(s * BLOCK, BLOCK), :]
+
+
 def backward_kernel(
     core_ref, lat_ref, hidden_ref, slope_ref, up_ref, wout_ref, share_ref,
-    gp_ref, mine_ref, other_ref, acc_in, acc_out, wide_ref,
+    mine_ref, other_ref, acc_in, acc_out, wide_ref, gp_ref,
 ):
     step, last = pl.program_id(0), pl.num_programs(0) - 1
     channels = lat_ref.shape[2]
@@ -202,16 +209,11 @@
         widen(wide_ref, wout_ref)
 
     for s in range(TILE // BLOCK):
-        rows = pl.ds(s * BLOCK, BLOCK)
-        block = jnp.concatenate(
-            [up_ref[s, 0].astype(F32), jnp.zeros((WIDE - VPAD, BLOCK), F32)], axis=0
-        )
-        grad_hidden = jnp.dot(block.T.astype(BF16), wide_ref[...], preferred_element_type=F32)
-        gp_ref[0, rows, :] = grad_hidden.astype(BF16) * slope_ref[0, rows, :]
+        gp_ref[pl.ds(s * BLOCK, BLOCK), :] = preact_grad(up_ref, slope_ref, wide_ref[...], s)
     ups = jnp.concatenate([up_ref[s, 0] for s in range(TILE // BLOCK)], axis=1)
     acc_out[:VPAD, :] += jnp.dot(ups, hidden_ref[0], preferred_element_type=F32)
     product = lax.dot_general(
-        lat_ref[0], gp_ref[0], (((0,), (0,)), ((), ())), preferred_element_type=F32
+        lat_ref[0], gp_ref[...], (((0,), (0,)), ((), ())), preferred_element_type=F32
     )
     acc_in[...] += product.reshape(acc_in.shape)
 
@@ -223,24 +225,23 @@
         middle = (share - high).astype(BF16).astype(F32)
         low = share - high - middle
         row = lax.broadcasted_iota(jnp.int32, acc_out.shape, 0) - (EXTRA + 3 * core)
-        whole = jnp.where(
+        acc_out[...] = jnp.where(
             row == 0,
             high,
             jnp.where(row == 1, middle, jnp.where(row == 2, low, acc_out[...])),
         )
-        acc_out[...] = whole
         for chunk in range(channels // WIDE):
-            piece = acc_out[:, chunk * WIDE : (chunk + 1) * WIDE].T.reshape(-1, 16, WIDE)
+            piece = acc_out[:, chunk * WIDE : (chunk + 1) * WIDE].T.astype(BF16).reshape(-1, 16, WIDE)
             for j in range(WIDE // 32):
                 @pl.when(core == 0)
                 def _():
-                    mine_ref[chunk * 4 + j, :, channels:] = piece[2 * j].astype(BF16)
-                    other_ref[chunk * 4 + j, :, channels:] = piece[2 * j + 1].astype(BF16)
+                    mine_ref[chunk * 4 + j, :, channels:] = piece[2 * j]
+                    other_ref[chunk * 4 + j, :, channels:] = piece[2 * j + 1]
 
                 @pl.when(core == 1)
                 def _():
-                    mine_ref[chunk * 4 + j, :, channels:] = piece[2 * j + 1].astype(BF16)
-                    other_ref[chunk * 4 + j, :, channels:] = piece[2 * j].astype(BF16)
+                    mine_ref[chunk * 4 + j, :, channels:] = piece[2 * j + 1]
+                    other_ref[chunk * 4 + j, :, channels:] = piece[2 * j]
 
         def group(g, carry):
             mine_ref[g, :, :channels] = acc_in[2 * g + core].astype(BF16)
@@ -267,55 +268,93 @@
             pl.BlockSpec(w_out_t.shape, lambda i, c: (0, 0)),
             pl.BlockSpec((8, 128), lambda i, c: (0, 0)),
         ],
-        out_specs=[
-            tile,
-            pl.BlockSpec(half, lambda i, c: (0, 0, 0)),
-            pl.BlockSpec(half, lambda i, c: (0, 0, 0)),
-        ],
+        out_specs=[pl.BlockSpec(half, lambda i, c: (0, 0, 0))] * 2,
         scratch_shapes=[
             pltpu.VMEM((channels // 16, 16, channels), F32),
             pltpu.VMEM((WIDE, channels), F32),
             pltpu.VMEM((WIDE, channels), BF16),
+            pltpu.VMEM((TILE, channels), BF16),
         ],
     )
     return pl.pallas_call(
         backward_kernel,
         grid_spec=grid_spec,
-        out_shape=[
-            pltpu.HBM(latent.shape, BF16),
-            jax.ShapeDtypeStruct(half, BF16),
-            jax.ShapeDtypeStruct(half, BF16),
-        ],
+        out_shape=[jax.ShapeDtypeStruct(half, BF16)] * 2,
         compiler_params=pltpu.CompilerParams(vmem_limit_bytes=BACKWARD_VMEM),
         name="backward",
-    )(core, in_hbm(latent), in_hbm(hidden), in_hbm(slopes), upstream, w_out_t, share)
-
-
-def latent_kernel(gp_ref, win_ref, out_ref):
-    for s in range(TILE // SUB):
-        rows = pl.ds(s * SUB, SUB)
-        out_ref[0, rows, :] = lax.dot_general(
-            gp_ref[0, rows, :], win_ref[...], (((1,), (1,)), ((), ())), preferred_element_type=F32
+    )(core, in_hbm(latent), in_hbm(hidden), in_hbm(slopes), upstream, in_hbm(w_out_t), share)
+
+
+def latent_kernel(slope_ref, up_ref, wout_ref, win_ref, out_ref, wide_ref):
+    @pl.when((pl.program_id(0) == 0) & (pl.program_id(1) == 0))
+    def _():
+        widen(wide_ref, wout_ref)
+
+    for s in range(TILE // BLOCK):
+        out_ref[0, pl.ds(s * BLOCK, BLOCK), :] = lax.dot_general(
+            preact_grad(up_ref, slope_ref, wide_ref[...], s),
+            win_ref[...],
+            (((1,), (1,)), ((), ())),
+            preferred_element_type=F32,
         ).astype(BF16)
 
 
-def latent_grad(gp, w_in):
-    members, points, channels = gp.shape
+def latent_grad(slopes, upstream, w_out_t, w_in):
+    members, points, channels = slopes.shape
+    per = TILE // BLOCK
     tile = pl.BlockSpec((1, TILE, channels), lambda m, i: (m, i, 0))
     return pl.pallas_call(
         latent_kernel,
         grid=(members, points // TILE),
-        in_specs=[tile, pl.BlockSpec((channels, channels), lambda m, i: (0, 0))],
+        in_specs=[
+            tile,
+            pl.BlockSpec((per, 1, VPAD, BLOCK), lambda m, i: (i, m, 0, 0)),
+            pl.BlockSpec(w_out_t.shape, lambda m, i: (0, 0)),
+            pl.BlockSpec((channels, channels), lambda m, i: (0, 0)),
+        ],
         out_specs=tile,
-        out_shape=pltpu.HBM(gp.shape, BF16),
+        out_shape=pltpu.HBM(slopes.shape, BF16),
+        scratch_shapes=[pltpu.VMEM((WIDE, channels), BF16)],
         compiler_params=pltpu.CompilerParams(vmem_limit_bytes=LATENT_VMEM),
         cost_estimate=pl.CostEstimate(
-            flops=2 * members * points * channels * channels,
+            flops=2 * members * points * channels * (channels + WIDE),
             bytes_accessed=4 * members * points * channels,
             transcendentals=0,
         ),
         name="latent_grad",
-    )(in_hbm(gp), w_in)
+    )(in_hbm(slopes), upstream, in_hbm(w_out_t), in_hbm(w_in))
+
+
+def finish_kernel(grad_scale, loss_scale, pieces_ref, in_ref, out_ref, loss_ref):
+    channels, variables = in_ref.shape[1], out_ref.shape[1]
+    total = pieces_ref[0].astype(F32)
+    for p in range(1, pieces_ref.shape[0]):
+        total = total + pieces_ref[p].astype(F32)
+    in_ref[...] = total[:, :channels] / grad_scale
+    out_ref[...] = total[:, channels : channels + variables] / grad_scale
+    tail = total[:1, channels:]
+    column = lax.broadcasted_iota(jnp.int32, tail.shape, 1)
+    loss_ref[0, 0] = jnp.sum(jnp.where(column >= EXTRA, tail, 0.0)) / loss_scale
+
+
+def finish(pieces, variables, grad_scale, loss_scale):
+    rows, wide = pieces.shape[1:]
+    channels = wide - WIDE
+    return pl.pallas_call(
+        functools.partial(finish_kernel, grad_scale, loss_scale),
+        out_specs=[
+            pl.BlockSpec(memory_space=pltpu.VMEM),
+            pl.BlockSpec(memory_space=pltpu.VMEM),
+            pl.BlockSpec(memory_space=pltpu.SMEM),
+        ],
+        out_shape=[
+            jax.ShapeDtypeStruct((rows, channels), F32),
+            jax.ShapeDtypeStruct((rows, variables), F32),
+            jax.ShapeDtypeStruct((1, 1), F32),
+        ],
+        compiler_params=pltpu.CompilerParams(vmem_limit_bytes=16 << 20),
+        name="finish",
+    )(pieces)
 
 
 def exchange(x, axis, xor):
@@ -350,20 +389,14 @@
     area = area_units.reshape(points // BLOCK, 1, BLOCK)
     grad_pred, share = score(me.reshape(1), scale, every, truth, var_wide, area)
     upstream = lax.all_to_all(grad_pred, MEMBER, 0, 0, tiled=True)
-    gp, mine, other = backward(core.reshape(1), rows, hidden, slopes, upstream, w_out_t, share)
+    mine, other = backward(core.reshape(1), rows, hidden, slopes, upstream, w_out_t, share)
     wide = channels + WIDE
     both = (mine.astype(F32) + exchange(other, "core", 1).astype(F32)).astype(BF16)
     pieces = lax.all_to_all(both.reshape(-1, 8, wide), REST, 0, 0, tiled=True)
-    grad_latent = latent_grad(gp, w_in)
-    total = jnp.sum(pieces.astype(F32), axis=0)
+    grad_latent = latent_grad(slopes, upstream, w_out_t, w_in)
     grad_scale = math.sqrt(dates * members * npoints)
-    loss = jnp.sum(total[0, channels + EXTRA : channels + EXTRA + 6]) / (dates * npoints * variables)
-    return (
-        loss,
-        grad_latent.reshape(latent.shape),
-        total[:, :channels] / grad_scale,
-        total[:, channels : channels + variables] / grad_scale,
-    )
+    grad_in, grad_out, loss = finish(pieces, variables, grad_scale, dates * npoints * variables)
+    return loss.reshape(()), grad_latent.reshape(latent.shape), grad_in, grad_out
 
 
 def solution(mesh):

time: 125 us -> 116 us (0.928)
  Pallas kernels: 69.8 us -> 67.3 us
  other arithmetic: 4.03 us -> 1.99 us
  between operations: 4.89 us -> 3.43 us
  starting transfers between devices: 32 us -> 30.7 us
    pallas_call x1 -> x2, Pallas kernels: 20.2 us -> 18.4 us  [the longest x1 17.6 us: backward(): pl.pallas_call(backward_kernel, grid_spec=grid_spec, out_shape=[jax.Shape...]
    pallas_call x1, Pallas kernels: 13.7 us -> 15.4 us  [latent_grad(): pl.pallas_call(latent_kernel, grid=(members, points // TILE), in_specs=[t...]
    all_to_all x1, waiting for transfers between devices: 5.5 us -> 3.79 us  [body(): pieces = lax.all_to_all(both.reshape(-1, 8, wide), REST, 0, 0, tiled=True)]
    all_to_all x1, waiting for transfers between devices: 0.19 us -> 1.44 us  [body(): upstream = lax.all_to_all(grad_pred, MEMBER, 0, 0, tiled=True)]
  transfers between devices with their start and end apart: 7 -> 7, of which waited for: 7 -> 7; matrix products, arithmetic and copies ran while one was open for 1% -> 1% of each run, Pallas kernels for 21% -> 24%
where the time goes in v3:
time: 116 us; the launch traced here: 115 us
  Pallas kernels  67.3 us (58%)
  starting transfers between devices  30.7 us (26%)
  waiting for transfers between devices  11.9 us (10%)
  between operations  3.43 us (3%)
  other arithmetic  1.99 us (2%)
    pallas_call x1, Pallas kernels, backward(): pl.pallas_call(backward_kernel, grid_spec=grid_spec, out_shape=[jax.Shape...  17.6 us
    pallas_call x1, Pallas kernels, forward(): pl.pallas_call(forward_kernel, grid=(members, points // TILE), in_specs=[...  16 us
    pallas_call x1, Pallas kernels, latent_grad(): pl.pallas_call(latent_kernel, grid=(members, points // TILE), in_specs=[t...  15.4 us
    pallas_call x1, Pallas kernels, shape(): pl.pallas_call(shape_kernel, grid=(members, points // TILE), in_specs=[ti...  12 us
    all_to_all x1, starting transfers between devices, body(): pieces = lax.all_to_all(both.reshape(-1, 8, wide), REST, 0, 0, tiled=True)  9.43 us
    all_to_all x1, starting transfers between devices, body(): every = lax.all_to_all(pred, MEMBER, 0, 0, tiled=True)  7.99 us
    ppermute x4, starting transfers between devices, exchange(): return lax.ppermute(x, axis, [(i, i ^ xor) for i in range(size)])  7.6 us
    all_to_all x1, starting transfers between devices, body(): upstream = lax.all_to_all(grad_pred, MEMBER, 0, 0, tiled=True)  5.65 us
  transfers between devices with their start and end apart: 7, of which 7 were waited for; matrix products, arithmetic and copies ran while one was open for 1% of the time, Pallas kernels for 24%

profile of v3, /device:TPU:0, one launch (start us, length us, event | category | flops | bytes accessed | tf_op | source)
XLA Modules:
  0.0 115.4 jit_solution(15880344792489459995)
XLA Ops:
  0.6 0.0 copy-start
  0.6 16.0 %forward.1 = (bf16[2,2048,1024]{2,1,0:T(8,128)(2,1)}, bf16[8,2,112,256]{3,2,1,0:T(8,128)(2,1)}) custom-call(bf16[2,2048,1024]{2,1,0:T(8,128)(2,1)} %bitcast.11, bf16[1024,1024]{1,0:T(8,128)(2,1)} %win_ref.3, bf16[100,1024]{1,0:T(8,128)(2,1)} %bitcast.13), custom_call_target="tpu_custom_call" | custom-call | tf_op jit(solution)/shard_map/forward/pallas_call | solution.py:66
  16.6 0.0 copy-start.1
  16.6 0.0 copy-start.2
  16.6 8.0 %all-to-all-start = ((bf16[8,2,112,256]{3,2,1,0:T(8,128)(2,1)}), bf16[8,2,112,256]{3,2,1,0:T(8,128)(2,1)S(1)}, u32[]{:S(2)}, u32[]{:S(2)}) async-start(bf16[8,2,112,256]{3,2,1,0:T(8,128)(2,1)} %get-tuple-element.18), calls=%async_computation | async-start | bytes 1835008 | tf_op jit(solution)/shard_map/all_to_all | solution.py:383
  24.6 0.0 copy-done
  24.6 0.6 convert_reduce_fusion
  25.2 0.0 collective-permute-start
  25.2 0.0 copy-done.1
  25.2 0.0 copy-done.2
  25.3 1.2 %collective-permute-done = f32[]{:T(128)} collective-permute-done((f32[]{:T(128)}, f32[]{:T(128)}, u32[]{:S(2)}, u32[]{:S(2)}) %collective-permute-start) | collective-permute-done | bytes 36 | tf_op jit(solution)/shard_map/ppermute | solution.py:362
  27.7 2.9 %collective-permute-start.1 = (f32[]{:T(128)}, f32[]{:T(128)}, u32[]{:S(2)}, u32[]{:S(2)}) collective-permute-start(f32[]{:T(128)} %add.20), channel_id=1, source_target_pairs={{0,4},{4,0},{8,12},{12,8},{1,5},{5,1},{9,13},{13,9},{2,6},{6,2},{1... | collective-permute-start | bytes 20 | tf_op jit(solution)/shard_map/ppermute | solution.py:362
  30.6 0.6 collective-permute-done.1
  31.9 4.6 %collective-permute-start.2 = (f32[]{:T(128)}, f32[]{:T(128)}, u32[]{:S(2)}, u32[]{:S(2)}) collective-permute-start(f32[]{:T(128)} %add.21), channel_id=1, source_target_pairs={{0,8},{4,12},{8,0},{12,4},{1,9},{5,13},{9,1},{13,5},{2,10},{6,14},... | collective-permute-start | bytes 20 | tf_op jit(solution)/shard_map/ppermute | solution.py:362
  36.5 0.5 collective-permute-done.2
  37.6 1.6 %all-to-all-done.refs_1_ = bf16[8,2,112,256]{3,2,1,0:T(8,128)(2,1)S(1)} async-done(((bf16[8,2,112,256]{3,2,1,0:T(8,128)(2,1)}), bf16[8,2,112,256]{3,2,1,0:T(8,128)(2,1)S(1)}, u32[]{:S(2)}, u32[]{:S(2)}) %all-to-all-start) | async-done | bytes 917536 | tf_op jit(solution)/shard_map/all_to_all | solution.py:383
  39.2 0.1 broadcast_in_dim.2.refs_3_
  39.3 5.5 %score.1 = (bf16[8,2,112,256]{3,2,1,0:T(8,128)(2,1)}, f32[8,128]{1,0:T(8,128)S(1)}) custom-call(s32[1]{0:T(128)} %bitcast.3.me_ref, f32[1,1]{1,0:T(1,128)} %bitcast.4.refs_0_, bf16[8,2,112,256]{3,2,1,0:T(8,128)(2,1)S(1)} %all-to-all-done.refs_1_, bf16[112,2048]{1,0:T(8,128)(2,1)S(1)} %pad.8.refs_2_, f32[112,256]{1,0:T(8,128)S(1)} %broadcast_in_dim.2.refs_3_, ...), custom_call_target="tpu_custom_call" | custom-call | tf_op jit(solution)/shard_map/score/pallas_call | solution.py:178
  44.8 5.7 %all-to-all-start.1 = ((bf16[8,2,112,256]{3,2,1,0:T(8,128)(2,1)}), bf16[8,2,112,256]{3,2,1,0:T(8,128)(2,1)S(1)}, u32[]{:S(2)}, u32[]{:S(2)}) async-start(bf16[8,2,112,256]{3,2,1,0:T(8,128)(2,1)} %get-tuple-element.19), calls=%async_computation.1 | async-start | bytes 1835008 | tf_op jit(solution)/shard_map/all_to_all | solution.py:391
  50.5 12.0 %shape.1 = (bf16[2,2048,1024]{2,1,0:T(8,128)(2,1)}, bf16[2,2048,1024]{2,1,0:T(8,128)(2,1)}) custom-call(bf16[2,2048,1024]{2,1,0:T(8,128)(2,1)} %get-tuple-element.15.preact_ref), custom_call_target="tpu_custom_call" | custom-call | flops 67108864 | bytes 25165824 | tf_op jit(solution)/shard_map/shape/pallas_call | solution.py:101
  62.5 1.4 %all-to-all-done.1.up_ref = bf16[8,2,112,256]{3,2,1,0:T(8,128)(2,1)S(1)} async-done(((bf16[8,2,112,256]{3,2,1,0:T(8,128)(2,1)}), bf16[8,2,112,256]{3,2,1,0:T(8,128)(2,1)S(1)}, u32[]{:S(2)}, u32[]{:S(2)}) %all-to-all-start.1) | async-done | bytes 917536 | tf_op jit(solution)/shard_map/all_to_all | solution.py:391
  63.9 17.6 %backward.1 = (bf16[32,16,1152]{2,1,0:T(8,128)(2,1)S(1)}, bf16[32,16,1152]{2,1,0:T(8,128)(2,1)S(1)}) custom-call(s32[1]{0:T(128)} %bitcast.core_ref, bf16[2,2048,1024]{2,1,0:T(8,128)(2,1)} %bitcast.12, bf16[2,2048,1024]{2,1,0:T(8,128)(2,1)} %get-tuple-element.16.hidden_ref, bf16[2,2048,1024]{2,1,0:T(8,128)(2,1)} %get-tuple-element.17.slope_ref, ...), custom_call_target="tpu_custom_call" | custom-call | tf_op jit(solution)/shard_map/backward/pallas_call | solution.py:279
  81.5 0.1 collective-permute-start.3
  81.6 2.8 %collective-permute-done.3 = bf16[32,16,1152]{2,1,0:T(8,128)(2,1)S(1)} collective-permute-done((bf16[32,16,1152]{2,1,0:T(8,128)(2,1)S(1)}, bf16[32,16,1152]{2,1,0:T(8,128)(2,1)S(1)}, u32[]{:S(2)}, u32[]{:S(2)}) %collective-permute-start.3) | collective-permute-done | bytes 1179680 | tf_op jit(solution)/shard_map/ppermute | solution.py:362
  84.5 1.4 %add_convert_fusion = bf16[32,16,1152]{2,1,0:T(8,128)(2,1)} fusion(bf16[32,16,1152]{2,1,0:T(8,128)(2,1)S(1)} %collective-permute-done.3, bf16[32,16,1152]{2,1,0:T(8,128)(2,1)S(1)} %get-tuple-element.21), kind=kLoop, calls=%fused_computation | loop fusion | flops 2359296 | bytes 3538944 | tf_op jit(solution)/shard_map/convert_element_type | solution.py:394
  85.8 9.4 %all-to-all-start.2 = ((bf16[64,8,1152]{2,1,0:T(8,128)(2,1)}), bf16[64,8,1152]{2,1,0:T(8,128)(2,1)S(1)}, u32[]{:S(2)}, u32[]{:S(2)}) async-start(bf16[64,8,1152]{2,1,0:T(8,128)(2,1)} %bitcast.7), calls=%async_computation.2 | async-start | bytes 2359296 | tf_op jit(solution)/shard_map/all_to_all | solution.py:395
  95.3 15.4 %latent_grad.1 = bf16[2,2048,1024]{2,1,0:T(8,128)(2,1)} custom-call(bf16[2,2048,1024]{2,1,0:T(8,128)(2,1)} %get-tuple-element.17.slope_ref, bf16[8,2,112,256]{3,2,1,0:T(8,128)(2,1)S(1)} %all-to-all-done.1.up_ref, bf16[100,1024]{1,0:T(8,128)(2,1)} %bitcast.15, bf16[1024,1024]{1,0:T(8,128)(2,1)} %win_ref.3), custom_call_target="tpu_custom_call" | custom-call | flops 9663676416 | bytes 16777216 | tf_op jit(solution)/shard_map/latent_grad/pallas_call | solution.py:306
  110.7 3.8 %all-to-all-done.2.pieces_ref = bf16[64,8,1152]{2,1,0:T(8,128)(2,1)S(1)} async-done(((bf16[64,8,1152]{2,1,0:T(8,128)(2,1)}), bf16[64,8,1152]{2,1,0:T(8,128)(2,1)S(1)}, u32[]{:S(2)}, u32[]{:S(2)}) %all-to-all-start.2) | async-done | bytes 1179680 | tf_op jit(solution)/shard_map/all_to_all | solution.py:395
  114.5 0.8 finish.1
  (2 shorter events, 0.0 us)
Async XLA Ops:
  0.6 24.0 %copy-start = (s32[2048]{0:T(1024)S(1)}, s32[2048]{0:T(1024)}, u32[]{:S(2)}) copy-start(s32[2048]{0:T(1024)} %param.10) | copy-start | bytes 24580
  16.6 8.6 %copy-start.1 = (bf16[1,100,2048]{2,1,0:T(8,128)(2,1)S(1)}, bf16[1,100,2048]{2,1,0:T(8,128)(2,1)}, u32[]{:S(2)}) copy-start(bf16[1,100,2048]{2,1,0:T(8,128)(2,1)} %param.9) | copy-start | bytes 1228804
  16.6 8.7 %copy-start.2 = (f32[100]{0:T(128)S(1)}, f32[100]{0:T(128)}, u32[]{:S(2)}) copy-start(f32[100]{0:T(128)} %param.11) | copy-start | bytes 1204
  16.6 22.6 %all-to-all-start = ((bf16[8,2,112,256]{3,2,1,0:T(8,128)(2,1)}), bf16[8,2,112,256]{3,2,1,0:T(8,128)(2,1)S(1)}, u32[]{:S(2)}, u32[]{:S(2)}) async-start(bf16[8,2,112,256]{3,2,1,0:T(8,128)(2,1)} %get-tuple-element.18), calls=%async_computation | async-start | bytes 1835008 | tf_op jit(solution)/shard_map/all_to_all | solution.py:383
  25.2 1.2 %collective-permute-start = (f32[]{:T(128)}, f32[]{:T(128)}, u32[]{:S(2)}, u32[]{:S(2)}) collective-permute-start(f32[]{:T(128)} %convert_reduce_fusion), channel_id=1, source_target_pairs={{0,2},{2,0},{1,3},{3,1},{4,6},{6,4},{5,7},{7,5},{8,10},{10,8},{9,1... | collective-permute-start | bytes 20 | tf_op jit(solution)/shard_map/ppermute | solution.py:362
  27.7 3.6 %collective-permute-start.1 = (f32[]{:T(128)}, f32[]{:T(128)}, u32[]{:S(2)}, u32[]{:S(2)}) collective-permute-start(f32[]{:T(128)} %add.20), channel_id=1, source_target_pairs={{0,4},{4,0},{8,12},{12,8},{1,5},{5,1},{9,13},{13,9},{2,6},{6,2},{1... | collective-permute-start | bytes 20 | tf_op jit(solution)/shard_map/ppermute | solution.py:362
  31.9 5.1 %collective-permute-start.2 = (f32[]{:T(128)}, f32[]{:T(128)}, u32[]{:S(2)}, u32[]{:S(2)}) collective-permute-start(f32[]{:T(128)} %add.21), channel_id=1, source_target_pairs={{0,8},{4,12},{8,0},{12,4},{1,9},{5,13},{9,1},{13,5},{2,10},{6,14},... | collective-permute-start | bytes 20 | tf_op jit(solution)/shard_map/ppermute | solution.py:362
  44.8 19.1 %all-to-all-start.1 = ((bf16[8,2,112,256]{3,2,1,0:T(8,128)(2,1)}), bf16[8,2,112,256]{3,2,1,0:T(8,128)(2,1)S(1)}, u32[]{:S(2)}, u32[]{:S(2)}) async-start(bf16[8,2,112,256]{3,2,1,0:T(8,128)(2,1)} %get-tuple-element.19), calls=%async_computation.1 | async-start | bytes 1835008 | tf_op jit(solution)/shard_map/all_to_all | solution.py:391
  81.5 2.9 %collective-permute-start.3 = (bf16[32,16,1152]{2,1,0:T(8,128)(2,1)S(1)}, bf16[32,16,1152]{2,1,0:T(8,128)(2,1)S(1)}, u32[]{:S(2)}, u32[]{:S(2)}) collective-permute-start(bf16[32,16,1152]{2,1,0:T(8,128)(2,1)S(1)} %get-tuple-element.22), channel_id=1, source_target_pairs={{0,2},{2,0},{1,3},{3,1},{4,6},{6,4},{5,7},{7,5},{8,10},{10,8},{9,1... | collective-permute-start | bytes 3538952 | tf_op jit(solution)/shard_map/ppermute | solution.py:362
  85.8 28.6 %all-to-all-start.2 = ((bf16[64,8,1152]{2,1,0:T(8,128)(2,1)}), bf16[64,8,1152]{2,1,0:T(8,128)(2,1)S(1)}, u32[]{:S(2)}, u32[]{:S(2)}) async-start(bf16[64,8,1152]{2,1,0:T(8,128)(2,1)} %bitcast.7), calls=%async_computation.2 | async-start | bytes 2359296 | tf_op jit(solution)/shard_map/all_to_all | solution.py:395

commit v4 on v3

--- a/solution.py
+++ b/solution.py
@@ -16,7 +16,7 @@
 F32 = jnp.float32
 
 BLOCK = 256
-VPAD = 112
+VPAD = 104
 WIDE = 128
 TILE = 1024
 SUB = 256
@@ -113,63 +113,69 @@
 
 
 def score_kernel(
-    members, scale_ref, pred_ref, truth_ref, var_ref, area_ref, grad_ref, share_ref, held_ref
+    members, scale_ref, pred_ref, truth_ref, var_ref, area_ref, grad_ref, share_ref, held_ref, true_ref
 ):
     per = pred_ref.shape[1]
     scale = scale_ref[0, 0]
     self_phi = members * math.sqrt(SMOOTH) / (2.0 * (members - 1))
-
-    @pl.when(pl.program_id(0) == 0)
-    def _():
-        share_ref[...] = jnp.zeros_like(share_ref)
-
-    for lane in range(BLOCK // 128):
-        lanes = pl.ds(lane * 128, 128)
-        for half in range(2):
-            rows = slice(8 * half, 8 * half + 8)
-            truth = truth_ref[:, lanes].astype(F32)[rows]
-            x = [pred_ref[m // per, m % per, :, lanes].astype(F32)[rows] - truth for m in range(members)]
-            weight = (var_ref[:, lanes] * (area_ref[0, :, lanes].astype(F32) * scale))[rows]
-            grads = [None] * members
-            roots = None
-            for m in range(members - 1):
-                for k in range(m + 1, members):
-                    d = x[m] - x[k]
-                    r = lax.rsqrt(d * d + SMOOTH)
-                    g = d * r
-                    roots = r if roots is None else roots + r
-                    grads[m] = g if grads[m] is None else grads[m] + g
-                    grads[k] = -g if grads[k] is None else grads[k] - g
-            score = None
-            for m in range(members):
-                q = x[m] * x[m] + SMOOTH
-                r = lax.rsqrt(q)
-                spread = grads[m] * (1.0 / (members - 1))
-                mine = q * r - x[m] * spread
-                score = mine if score is None else score + mine
-                held_ref[m, rows, :] = weight * (x[m] * r - spread)
-            score = score - roots * (SMOOTH / (members - 1)) - self_phi
-            share_ref[...] += weight * score
+    true_ref[...] = truth_ref[...].astype(F32)
+    for m in range(members):
+        held_ref[m] = pred_ref[m // per, m % per].astype(F32)
+
+    def part(rows, lanes):
+        truth = true_ref[rows, lanes]
+        x = [held_ref[m, rows, lanes] - truth for m in range(members)]
+        weight = var_ref[rows, lanes] * (area_ref[0, :, lanes].astype(F32) * scale)
+        grads = [None] * members
+        roots = None
+        for m in range(members - 1):
+            for k in range(m + 1, members):
+                d = x[m] - x[k]
+                r = lax.rsqrt(d * d + SMOOTH)
+                g = d * r
+                roots = r if roots is None else roots + r
+                grads[m] = g if grads[m] is None else grads[m] + g
+                grads[k] = -g if grads[k] is None else grads[k] - g
+        score = None
         for m in range(members):
-            grad_ref[m // per, m % per, :, lanes] = held_ref[m].astype(BF16)
+            q = x[m] * x[m] + SMOOTH
+            r = lax.rsqrt(q)
+            spread = grads[m] * (1.0 / (members - 1))
+            mine = q * r - x[m] * spread
+            score = mine if score is None else score + mine
+            held_ref[m, rows, lanes] = weight * (x[m] * r - spread)
+        return weight * (score - roots * (SMOOTH / (members - 1)) - self_phi)
+
+    def rows8(step, total):
+        rows = pl.ds(pl.multiple_of(step * 8, 8), 8)
+        for lane in range(BLOCK // 128):
+            total = total + part(rows, pl.ds(lane * 128, 128))
+        return total
+
+    share_ref[...] = lax.fori_loop(0, VPAD // 8, rows8, jnp.zeros((8, 128), F32))
+    for m in range(members):
+        grad_ref[m // per, m % per] = held_ref[m].astype(BF16)
 
 
 def score(me, scale, every, truth, var_weight, area):
     devices, per = every.shape[:2]
     members = devices * per
-    block = pl.BlockSpec((devices, per, 16, BLOCK), lambda i, me: (0, 0, i, 0))
+    vmem = pl.BlockSpec(memory_space=pltpu.VMEM)
     grid_spec = pltpu.PrefetchScalarGridSpec(
         num_scalar_prefetch=1,
-        grid=(VPAD // 16,),
+        grid=(1,),
         in_specs=[
             pl.BlockSpec(memory_space=pltpu.SMEM),
-            block,
-            pl.BlockSpec((16, BLOCK), lambda i, me: (i, me[0])),
-            pl.BlockSpec((16, BLOCK), lambda i, me: (i, 0)),
+            vmem,
+            pl.BlockSpec((VPAD, BLOCK), lambda i, me: (0, me[0])),
+            vmem,
             pl.BlockSpec((1, 1, BLOCK), lambda i, me: (me[0], 0, 0)),
         ],
-        out_specs=[block, pl.BlockSpec((8, 128), lambda i, me: (0, 0))],
-        scratch_shapes=[pltpu.VMEM((members, 16, 128), F32)],
+        out_specs=[vmem, vmem],
+        scratch_shapes=[
+            pltpu.VMEM((members, VPAD, BLOCK), F32),
+            pltpu.VMEM((VPAD, BLOCK), F32),
+        ],
     )
 
     def kernel(me_ref, *refs):
@@ -373,7 +379,7 @@
     core = lax.axis_index("core").astype(jnp.int32)
 
     area_total = jnp.sum(area_units.astype(F32))
-    for axis, xor in (("core", 1), ("y", 1), ("y", 2)):
+    for axis, xor in (("core", 1), ("y", 1), ("y", 3)):
         area_total = area_total + exchange(area_total, axis, xor)
     scale = (npoints / area_total).reshape(1, 1)
 

time: 116 us -> 115 us (level)
  waiting for transfers between devices: 11.9 us -> 10.7 us
  starting transfers between devices: 30.7 us -> 31.9 us
where the time goes in v4:
time: 115 us
  Pallas kernels  67.1 us (58%)
  starting transfers between devices  31.9 us (28%)
  waiting for transfers between devices  10.7 us (9%)
  between operations  3.28 us (3%)
  other arithmetic  1.99 us (2%)
    pallas_call x1, Pallas kernels, backward(): pl.pallas_call(backward_kernel, grid_spec=grid_spec, out_shape=[jax.Shape...  17.6 us
    pallas_call x1, Pallas kernels, forward(): pl.pallas_call(forward_kernel, grid=(members, points // TILE), in_specs=[...  16 us
    pallas_call x1, Pallas kernels, latent_grad(): pl.pallas_call(latent_kernel, grid=(members, points // TILE), in_specs=[t...  15.4 us
    pallas_call x1, Pallas kernels, shape(): pl.pallas_call(shape_kernel, grid=(members, points // TILE), in_specs=[ti...  12 us
    all_to_all x1, starting transfers between devices, body(): pieces = lax.all_to_all(both.reshape(-1, 8, wide), REST, 0, 0, tiled=True)  10.2 us
    all_to_all x1, starting transfers between devices, body(): every = lax.all_to_all(pred, MEMBER, 0, 0, tiled=True)  7.98 us
    ppermute x4, starting transfers between devices, exchange(): return lax.ppermute(x, axis, [(i, i ^ xor) for i in range(size)])  7.43 us
    all_to_all x1, starting transfers between devices, body(): upstream = lax.all_to_all(grad_pred, MEMBER, 0, 0, tiled=True)  6.28 us
  transfers between devices with their start and end apart: 7, of which 7 were waited for; matrix products, arithmetic and copies ran while one was open for 1% of the time, Pallas kernels for 24%

profile of v4, /device:TPU:0, one launch (start us, length us, event | category | flops | bytes accessed | tf_op | source)
XLA Modules:
  0.0 115.1 jit_solution(15384429806004799654)
XLA Ops:
  0.6 0.0 copy-start
  0.6 0.0 copy-start.1
  0.7 16.0 %forward.1 = (bf16[2,2048,1024]{2,1,0:T(8,128)(2,1)}, bf16[8,2,104,256]{3,2,1,0:T(8,128)(2,1)}) custom-call(bf16[2,2048,1024]{2,1,0:T(8,128)(2,1)} %bitcast.11, bf16[1024,1024]{1,0:T(8,128)(2,1)} %win_ref.3, bf16[100,1024]{1,0:T(8,128)(2,1)} %bitcast.13), custom_call_target="tpu_custom_call" | custom-call | tf_op jit(solution)/shard_map/forward/pallas_call | solution.py:66
  16.6 0.0 copy-start.2
  16.7 8.0 %all-to-all-start = ((bf16[8,2,104,256]{3,2,1,0:T(8,128)(2,1)}), bf16[8,2,104,256]{3,2,1,0:T(8,128)(2,1)S(1)}, u32[]{:S(2)}, u32[]{:S(2)}) async-start(bf16[8,2,104,256]{3,2,1,0:T(8,128)(2,1)} %get-tuple-element.18), calls=%async_computation | async-start | bytes 1703936 | tf_op jit(solution)/shard_map/all_to_all | solution.py:389
  24.6 0.0 copy-done
  24.6 0.6 convert_reduce_fusion
  25.2 0.0 collective-permute-start
  25.2 0.0 copy-done.1
  25.3 0.0 copy-done.2
  25.3 1.3 %collective-permute-done = f32[]{:T(128)} collective-permute-done((f32[]{:T(128)}, f32[]{:T(128)}, u32[]{:S(2)}, u32[]{:S(2)}) %collective-permute-start) | collective-permute-done | bytes 36 | tf_op jit(solution)/shard_map/ppermute | solution.py:368
  27.8 3.0 %collective-permute-start.1 = (f32[]{:T(128)}, f32[]{:T(128)}, u32[]{:S(2)}, u32[]{:S(2)}) collective-permute-start(f32[]{:T(128)} %add.20), channel_id=1, source_target_pairs={{0,4},{4,0},{8,12},{12,8},{1,5},{5,1},{9,13},{13,9},{2,6},{6,2},{1... | collective-permute-start | bytes 20 | tf_op jit(solution)/shard_map/ppermute | solution.py:368
  30.8 0.8 collective-permute-done.1
  32.1 4.4 %collective-permute-start.2 = (f32[]{:T(128)}, f32[]{:T(128)}, u32[]{:S(2)}, u32[]{:S(2)}) collective-permute-start(f32[]{:T(128)} %add.21), channel_id=1, source_target_pairs={{0,12},{4,8},{8,4},{12,0},{1,13},{5,9},{9,5},{13,1},{2,14},{6,10},... | collective-permute-start | bytes 20 | tf_op jit(solution)/shard_map/ppermute | solution.py:368
  36.5 0.5 collective-permute-done.2
  37.7 0.9 all-to-all-done.refs_1_
  38.6 0.1 broadcast_in_dim.2.refs_3_
  38.7 5.3 %score.1 = (bf16[8,2,104,256]{3,2,1,0:T(8,128)(2,1)}, f32[8,128]{1,0:T(8,128)S(1)}) custom-call(s32[1]{0:T(128)} %bitcast.3.me_ref, f32[1,1]{1,0:T(1,128)} %bitcast.4.refs_0_, bf16[8,2,104,256]{3,2,1,0:T(8,128)(2,1)S(1)} %all-to-all-done.refs_1_, bf16[104,2048]{1,0:T(8,128)(2,1)S(1)} %pad.8.refs_2_, f32[104,256]{1,0:T(8,128)S(1)} %broadcast_in_dim.2.refs_3_, ...), custom_call_target="tpu_custom_call" | custom-call | tf_op jit(solution)/shard_map/score/pallas_call | solution.py:184
  44.0 6.3 %all-to-all-start.1 = ((bf16[8,2,104,256]{3,2,1,0:T(8,128)(2,1)}), bf16[8,2,104,256]{3,2,1,0:T(8,128)(2,1)S(1)}, u32[]{:S(2)}, u32[]{:S(2)}) async-start(bf16[8,2,104,256]{3,2,1,0:T(8,128)(2,1)} %get-tuple-element.19), calls=%async_computation.1 | async-start | bytes 1703936 | tf_op jit(solution)/shard_map/all_to_all | solution.py:397
  50.3 12.0 %shape.1 = (bf16[2,2048,1024]{2,1,0:T(8,128)(2,1)}, bf16[2,2048,1024]{2,1,0:T(8,128)(2,1)}) custom-call(bf16[2,2048,1024]{2,1,0:T(8,128)(2,1)} %get-tuple-element.15.preact_ref), custom_call_target="tpu_custom_call" | custom-call | flops 67108864 | bytes 25165824 | tf_op jit(solution)/shard_map/shape/pallas_call | solution.py:101
  62.3 0.5 all-to-all-done.1.up_ref
  62.8 17.6 %backward.1 = (bf16[32,16,1152]{2,1,0:T(8,128)(2,1)S(1)}, bf16[32,16,1152]{2,1,0:T(8,128)(2,1)S(1)}) custom-call(s32[1]{0:T(128)} %bitcast.core_ref, bf16[2,2048,1024]{2,1,0:T(8,128)(2,1)} %bitcast.12, bf16[2,2048,1024]{2,1,0:T(8,128)(2,1)} %get-tuple-element.16.hidden_ref, bf16[2,2048,1024]{2,1,0:T(8,128)(2,1)} %get-tuple-element.17.slope_ref, ...), custom_call_target="tpu_custom_call" | custom-call | tf_op jit(solution)/shard_map/backward/pallas_call | solution.py:285
  80.4 0.1 collective-permute-start.3
  80.5 2.8 %collective-permute-done.3 = bf16[32,16,1152]{2,1,0:T(8,128)(2,1)S(1)} collective-permute-done((bf16[32,16,1152]{2,1,0:T(8,128)(2,1)S(1)}, bf16[32,16,1152]{2,1,0:T(8,128)(2,1)S(1)}, u32[]{:S(2)}, u32[]{:S(2)}) %collective-permute-start.3) | collective-permute-done | bytes 1179680 | tf_op jit(solution)/shard_map/ppermute | solution.py:368
  83.3 1.4 %add_convert_fusion = bf16[32,16,1152]{2,1,0:T(8,128)(2,1)} fusion(bf16[32,16,1152]{2,1,0:T(8,128)(2,1)S(1)} %collective-permute-done.3, bf16[32,16,1152]{2,1,0:T(8,128)(2,1)S(1)} %get-tuple-element.21), kind=kLoop, calls=%fused_computation | loop fusion | flops 2359296 | bytes 3538944 | tf_op jit(solution)/shard_map/convert_element_type | solution.py:400
  84.7 10.2 %all-to-all-start.2 = ((bf16[64,8,1152]{2,1,0:T(8,128)(2,1)}), bf16[64,8,1152]{2,1,0:T(8,128)(2,1)S(1)}, u32[]{:S(2)}, u32[]{:S(2)}) async-start(bf16[64,8,1152]{2,1,0:T(8,128)(2,1)} %bitcast.7), calls=%async_computation.2 | async-start | bytes 2359296 | tf_op jit(solution)/shard_map/all_to_all | solution.py:401
  94.9 15.4 %latent_grad.1 = bf16[2,2048,1024]{2,1,0:T(8,128)(2,1)} custom-call(bf16[2,2048,1024]{2,1,0:T(8,128)(2,1)} %get-tuple-element.17.slope_ref, bf16[8,2,104,256]{3,2,1,0:T(8,128)(2,1)S(1)} %all-to-all-done.1.up_ref, bf16[100,1024]{1,0:T(8,128)(2,1)} %bitcast.15, bf16[1024,1024]{1,0:T(8,128)(2,1)} %win_ref.3), custom_call_target="tpu_custom_call" | custom-call | flops 9663676416 | bytes 16777216 | tf_op jit(solution)/shard_map/latent_grad/pallas_call | solution.py:312
  110.3 3.8 %all-to-all-done.2.pieces_ref = bf16[64,8,1152]{2,1,0:T(8,128)(2,1)S(1)} async-done(((bf16[64,8,1152]{2,1,0:T(8,128)(2,1)}), bf16[64,8,1152]{2,1,0:T(8,128)(2,1)S(1)}, u32[]{:S(2)}, u32[]{:S(2)}) %all-to-all-start.2) | async-done | bytes 1179680 | tf_op jit(solution)/shard_map/all_to_all | solution.py:401
  114.1 0.8 finish.1
  (2 shorter events, 0.0 us)
Async XLA Ops:
  0.6 24.0 %copy-start = (s32[2048]{0:T(1024)S(1)}, s32[2048]{0:T(1024)}, u32[]{:S(2)}) copy-start(s32[2048]{0:T(1024)} %param.10) | copy-start | bytes 24580
  0.6 24.6 %copy-start.1 = (bf16[1,100,2048]{2,1,0:T(8,128)(2,1)S(1)}, bf16[1,100,2048]{2,1,0:T(8,128)(2,1)}, u32[]{:S(2)}) copy-start(bf16[1,100,2048]{2,1,0:T(8,128)(2,1)} %param.9) | copy-start | bytes 1228804
  16.6 8.6 %copy-start.2 = (f32[100]{0:T(128)S(1)}, f32[100]{0:T(128)}, u32[]{:S(2)}) copy-start(f32[100]{0:T(128)} %param.11) | copy-start | bytes 1204
  16.7 22.0 %all-to-all-start = ((bf16[8,2,104,256]{3,2,1,0:T(8,128)(2,1)}), bf16[8,2,104,256]{3,2,1,0:T(8,128)(2,1)S(1)}, u32[]{:S(2)}, u32[]{:S(2)}) async-start(bf16[8,2,104,256]{3,2,1,0:T(8,128)(2,1)} %get-tuple-element.18), calls=%async_computation | async-start | bytes 1703936 | tf_op jit(solution)/shard_map/all_to_all | solution.py:389
  25.2 1.4 %collective-permute-start = (f32[]{:T(128)}, f32[]{:T(128)}, u32[]{:S(2)}, u32[]{:S(2)}) collective-permute-start(f32[]{:T(128)} %convert_reduce_fusion), channel_id=1, source_target_pairs={{0,2},{2,0},{1,3},{3,1},{4,6},{6,4},{5,7},{7,5},{8,10},{10,8},{9,1... | collective-permute-start | bytes 20 | tf_op jit(solution)/shard_map/ppermute | solution.py:368
  27.8 3.7 %collective-permute-start.1 = (f32[]{:T(128)}, f32[]{:T(128)}, u32[]{:S(2)}, u32[]{:S(2)}) collective-permute-start(f32[]{:T(128)} %add.20), channel_id=1, source_target_pairs={{0,4},{4,0},{8,12},{12,8},{1,5},{5,1},{9,13},{13,9},{2,6},{6,2},{1... | collective-permute-start | bytes 20 | tf_op jit(solution)/shard_map/ppermute | solution.py:368
  32.1 4.9 %collective-permute-start.2 = (f32[]{:T(128)}, f32[]{:T(128)}, u32[]{:S(2)}, u32[]{:S(2)}) collective-permute-start(f32[]{:T(128)} %add.21), channel_id=1, source_target_pairs={{0,12},{4,8},{8,4},{12,0},{1,13},{5,9},{9,5},{13,1},{2,14},{6,10},... | collective-permute-start | bytes 20 | tf_op jit(solution)/shard_map/ppermute | solution.py:368
  44.0 18.8 %all-to-all-start.1 = ((bf16[8,2,104,256]{3,2,1,0:T(8,128)(2,1)}), bf16[8,2,104,256]{3,2,1,0:T(8,128)(2,1)S(1)}, u32[]{:S(2)}, u32[]{:S(2)}) async-start(bf16[8,2,104,256]{3,2,1,0:T(8,128)(2,1)} %get-tuple-element.19), calls=%async_computation.1 | async-start | bytes 1703936 | tf_op jit(solution)/shard_map/all_to_all | solution.py:397
  80.4 2.9 %collective-permute-start.3 = (bf16[32,16,1152]{2,1,0:T(8,128)(2,1)S(1)}, bf16[32,16,1152]{2,1,0:T(8,128)(2,1)S(1)}, u32[]{:S(2)}, u32[]{:S(2)}) collective-permute-start(bf16[32,16,1152]{2,1,0:T(8,128)(2,1)S(1)} %get-tuple-element.22), channel_id=1, source_target_pairs={{0,2},{2,0},{1,3},{3,1},{4,6},{6,4},{5,7},{7,5},{8,10},{10,8},{9,1... | collective-permute-start | bytes 3538952 | tf_op jit(solution)/shard_map/ppermute | solution.py:368
  84.7 29.4 %all-to-all-start.2 = ((bf16[64,8,1152]{2,1,0:T(8,128)(2,1)}), bf16[64,8,1152]{2,1,0:T(8,128)(2,1)S(1)}, u32[]{:S(2)}, u32[]{:S(2)}) async-start(bf16[64,8,1152]{2,1,0:T(8,128)(2,1)} %bitcast.7), calls=%async_computation.2 | async-start | bytes 2359296 | tf_op jit(solution)/shard_map/all_to_all | solution.py:401

commit v5 on v4

--- a/solution.py
+++ b/solution.py
@@ -15,6 +15,7 @@
 BF16 = jnp.bfloat16
 F32 = jnp.float32
 
+SHAPE_TILE = 2048
 BLOCK = 256
 VPAD = 104
 WIDE = 128
@@ -23,7 +24,7 @@
 EXTRA = 112
 
 FORWARD_VMEM = 40 << 20
-SHAPE_VMEM = 36 << 20
+SHAPE_VMEM = 44 << 20
 SCORE_VMEM = 16 << 20
 BACKWARD_VMEM = 50 << 20
 LATENT_VMEM = 40 << 20
@@ -86,21 +87,24 @@
 
 
 def shape_kernel(preact_ref, hidden_ref, slope_ref):
-    u = preact_ref[...].astype(F32)
-    u2 = u * u
-    half = 0.5 + 0.5 * jnp.tanh(u * (GELU_C + (GELU_C * GELU_A) * u2))
-    value = u * half
-    hidden_ref[...] = value.astype(BF16)
-    bend = (2.0 * GELU_C) + (6.0 * GELU_A * GELU_C) * u2
-    slope_ref[...] = (half + (value - value * half) * bend).astype(BF16)
+    for s in range(SHAPE_TILE // SUB):
+        rows = pl.ds(s * SUB, SUB)
+        u = preact_ref[0, rows, :]
+        u2 = u * u
+        bent = jnp.tanh(u * (BF16(GELU_C) + BF16(GELU_C * GELU_A) * u2))
+        half = BF16(0.5) + BF16(0.5) * bent
+        value = u * half
+        hidden_ref[0, rows, :] = value
+        bend = BF16(GELU_C) + BF16(3.0 * GELU_A * GELU_C) * u2
+        slope_ref[0, rows, :] = half + value * ((BF16(1.0) - bent) * bend)
 
 
 def shape(preact):
     members, points, channels = preact.shape
-    tile = pl.BlockSpec((1, TILE, channels), lambda m, i: (m, i, 0))
+    tile = pl.BlockSpec((1, SHAPE_TILE, channels), lambda m, i: (m, i, 0))
     return pl.pallas_call(
         shape_kernel,
-        grid=(members, points // TILE),
+        grid=(members, points // SHAPE_TILE),
         in_specs=[tile],
         out_specs=[tile, tile],
         out_shape=[pltpu.HBM(preact.shape, BF16)] * 2,
@@ -203,25 +207,26 @@
 
 def backward_kernel(
     core_ref, lat_ref, hidden_ref, slope_ref, up_ref, wout_ref, share_ref,
-    mine_ref, other_ref, acc_in, acc_out, wide_ref, gp_ref,
+    mine_ref, other_ref, acc_in, acc_out, tail_ref, wide_ref, gp_ref,
 ):
     step, last = pl.program_id(0), pl.num_programs(0) - 1
     channels = lat_ref.shape[2]
 
     @pl.when(step == 0)
     def _():
-        acc_in[...] = jnp.zeros_like(acc_in)
-        acc_out[...] = jnp.zeros_like(acc_out)
         widen(wide_ref, wout_ref)
+
+    def onward(acc):
+        return jnp.where(step == 0, 0.0, acc[...])
 
     for s in range(TILE // BLOCK):
         gp_ref[pl.ds(s * BLOCK, BLOCK), :] = preact_grad(up_ref, slope_ref, wide_ref[...], s)
     ups = jnp.concatenate([up_ref[s, 0] for s in range(TILE // BLOCK)], axis=1)
-    acc_out[:VPAD, :] += jnp.dot(ups, hidden_ref[0], preferred_element_type=F32)
+    acc_out[...] = onward(acc_out) + jnp.dot(ups, hidden_ref[0], preferred_element_type=F32)
     product = lax.dot_general(
         lat_ref[0], gp_ref[...], (((0,), (0,)), ((), ())), preferred_element_type=F32
     )
-    acc_in[...] += product.reshape(acc_in.shape)
+    acc_in[...] = onward(acc_in) + product.reshape(acc_in.shape)
 
     @pl.when(step == last)
     def _():
@@ -230,28 +235,17 @@
         high = share.astype(BF16).astype(F32)
         middle = (share - high).astype(BF16).astype(F32)
         low = share - high - middle
-        row = lax.broadcasted_iota(jnp.int32, acc_out.shape, 0) - (EXTRA + 3 * core)
-        acc_out[...] = jnp.where(
-            row == 0,
-            high,
-            jnp.where(row == 1, middle, jnp.where(row == 2, low, acc_out[...])),
+        column = lax.broadcasted_iota(jnp.int32, (channels, WIDE), 1) - (EXTRA + 3 * core)
+        whole = jnp.concatenate([acc_out[...], jnp.zeros((WIDE - VPAD, channels), F32)], axis=0).T
+        score = jnp.where(
+            column == 0, high, jnp.where(column == 1, middle, jnp.where(column == 2, low, whole))
         )
-        for chunk in range(channels // WIDE):
-            piece = acc_out[:, chunk * WIDE : (chunk + 1) * WIDE].T.astype(BF16).reshape(-1, 16, WIDE)
-            for j in range(WIDE // 32):
-                @pl.when(core == 0)
-                def _():
-                    mine_ref[chunk * 4 + j, :, channels:] = piece[2 * j]
-                    other_ref[chunk * 4 + j, :, channels:] = piece[2 * j + 1]
-
-                @pl.when(core == 1)
-                def _():
-                    mine_ref[chunk * 4 + j, :, channels:] = piece[2 * j + 1]
-                    other_ref[chunk * 4 + j, :, channels:] = piece[2 * j]
+        tail_ref[...] = score.reshape(tail_ref.shape)
 
         def group(g, carry):
-            mine_ref[g, :, :channels] = acc_in[2 * g + core].astype(BF16)
-            other_ref[g, :, :channels] = acc_in[2 * g + 1 - core].astype(BF16)
+            for half_ref, n in ((mine_ref, 2 * g + core), (other_ref, 2 * g + 1 - core)):
+                half_ref[g, :, :channels] = acc_in[n].astype(BF16)
+                half_ref[g, :, channels:] = tail_ref[n].astype(BF16)
             return carry
 
         lax.fori_loop(0, channels // 32, group, 0, unroll=4)
@@ -274,10 +268,11 @@
             pl.BlockSpec(w_out_t.shape, lambda i, c: (0, 0)),
             pl.BlockSpec((8, 128), lambda i, c: (0, 0)),
         ],
-        out_specs=[pl.BlockSpec(half, lambda i, c: (0, 0, 0))] * 2,
+        out_specs=[pl.BlockSpec(memory_space=pltpu.VMEM)] * 2,
         scratch_shapes=[
             pltpu.VMEM((channels // 16, 16, channels), F32),
-            pltpu.VMEM((WIDE, channels), F32),
+            pltpu.VMEM((VPAD, channels), F32),
+            pltpu.VMEM((channels // 16, 16, WIDE), F32),
             pltpu.VMEM((WIDE, channels), BF16),
             pltpu.VMEM((TILE, channels), BF16),
         ],

time: 115 us -> 113 us (0.983)
  Pallas kernels: 67.1 us -> 64.3 us
  waiting for transfers between devices: 10.7 us -> 12.4 us
  starting transfers between devices: 31.9 us -> 30.2 us
    all_to_all x1, waiting for transfers between devices: 0.46 us -> 2.37 us  [body(): upstream = lax.all_to_all(grad_pred, MEMBER, 0, 0, tiled=True)]
    pallas_call x1, Pallas kernels: 12 us -> 10.1 us  [shape(): pl.pallas_call(shape_kernel, grid=(members, points // SHAPE_TILE), in_spe...]
    all_to_all x1, starting transfers between devices: 10.2 us -> 8.5 us  [body(): pieces = lax.all_to_all(both.reshape(-1, 8, wide), REST, 0, 0, tiled=True)]
  transfers between devices with their start and end apart: 7 -> 7, of which waited for: 7 -> 7; matrix products, arithmetic and copies ran while one was open for 1% -> 1% of each run, Pallas kernels for 24% -> 23%
where the time goes in v5:
time: 113 us; the launch traced here: 112 us
  Pallas kernels  64.3 us (57%)
  starting transfers between devices  30.2 us (27%)
  waiting for transfers between devices  12.4 us (11%)
  between operations  3.28 us (3%)
  other arithmetic  1.99 us (2%)
    pallas_call x1, Pallas kernels, backward(): pl.pallas_call(backward_kernel, grid_spec=grid_spec, out_shape=[jax.Shape...  16.7 us
    pallas_call x1, Pallas kernels, forward(): pl.pallas_call(forward_kernel, grid=(members, points // TILE), in_specs=[...  16 us
    pallas_call x1, Pallas kernels, latent_grad(): pl.pallas_call(latent_kernel, grid=(members, points // TILE), in_specs=[t...  15.4 us
    pallas_call x1, Pallas kernels, shape(): pl.pallas_call(shape_kernel, grid=(members, points // SHAPE_TILE), in_spe...  10.1 us
    all_to_all x1, starting transfers between devices, body(): pieces = lax.all_to_all(both.reshape(-1, 8, wide), REST, 0, 0, tiled=True)  8.5 us
    all_to_all x1, starting transfers between devices, body(): every = lax.all_to_all(pred, MEMBER, 0, 0, tiled=True)  7.98 us
    ppermute x4, starting transfers between devices, exchange(): return lax.ppermute(x, axis, [(i, i ^ xor) for i in range(size)])  7.43 us
    all_to_all x1, starting transfers between devices, body(): upstream = lax.all_to_all(grad_pred, MEMBER, 0, 0, tiled=True)  6.28 us
  transfers between devices with their start and end apart: 7, of which 7 were waited for; matrix products, arithmetic and copies ran while one was open for 1% of the time, Pallas kernels for 23%

profile of v5, /device:TPU:0, one launch (start us, length us, event | category | flops | bytes accessed | tf_op | source)
XLA Modules:
  0.0 112.3 jit_solution(11967226594130877675)
XLA Ops:
  0.6 0.0 copy-start
  0.6 0.0 copy-start.1
  0.7 16.0 %forward.1 = (bf16[2,2048,1024]{2,1,0:T(8,128)(2,1)}, bf16[8,2,104,256]{3,2,1,0:T(8,128)(2,1)}) custom-call(bf16[2,2048,1024]{2,1,0:T(8,128)(2,1)} %bitcast.11, bf16[1024,1024]{1,0:T(8,128)(2,1)} %win_ref.3, bf16[100,1024]{1,0:T(8,128)(2,1)} %bitcast.13), custom_call_target="tpu_custom_call" | custom-call | tf_op jit(solution)/shard_map/forward/pallas_call | solution.py:67
  16.6 0.0 copy-start.2
  16.7 8.0 %all-to-all-start = ((bf16[8,2,104,256]{3,2,1,0:T(8,128)(2,1)}), bf16[8,2,104,256]{3,2,1,0:T(8,128)(2,1)S(1)}, u32[]{:S(2)}, u32[]{:S(2)}) async-start(bf16[8,2,104,256]{3,2,1,0:T(8,128)(2,1)} %get-tuple-element.18), calls=%async_computation | async-start | bytes 1703936 | tf_op jit(solution)/shard_map/all_to_all | solution.py:384
  24.6 0.0 copy-done
  24.6 0.6 convert_reduce_fusion
  25.2 0.0 collective-permute-start
  25.2 0.0 copy-done.1
  25.3 0.0 copy-done.2
  25.3 1.3 %collective-permute-done = f32[]{:T(128)} collective-permute-done((f32[]{:T(128)}, f32[]{:T(128)}, u32[]{:S(2)}, u32[]{:S(2)}) %collective-permute-start) | collective-permute-done | bytes 36 | tf_op jit(solution)/shard_map/ppermute | solution.py:363
  27.8 3.0 %collective-permute-start.1 = (f32[]{:T(128)}, f32[]{:T(128)}, u32[]{:S(2)}, u32[]{:S(2)}) collective-permute-start(f32[]{:T(128)} %add.20), channel_id=1, source_target_pairs={{0,4},{4,0},{8,12},{12,8},{1,5},{5,1},{9,13},{13,9},{2,6},{6,2},{1... | collective-permute-start | bytes 20 | tf_op jit(solution)/shard_map/ppermute | solution.py:363
  30.8 0.8 collective-permute-done.1
  32.1 4.4 %collective-permute-start.2 = (f32[]{:T(128)}, f32[]{:T(128)}, u32[]{:S(2)}, u32[]{:S(2)}) collective-permute-start(f32[]{:T(128)} %add.21), channel_id=1, source_target_pairs={{0,12},{4,8},{8,4},{12,0},{1,13},{5,9},{9,5},{13,1},{2,14},{6,10},... | collective-permute-start | bytes 20 | tf_op jit(solution)/shard_map/ppermute | solution.py:363
  36.5 0.5 collective-permute-done.2
  37.7 0.9 all-to-all-done.refs_1_
  38.6 0.1 broadcast_in_dim.2.refs_3_
  38.7 5.3 %score.1 = (bf16[8,2,104,256]{3,2,1,0:T(8,128)(2,1)}, f32[8,128]{1,0:T(8,128)S(1)}) custom-call(s32[1]{0:T(128)} %bitcast.3.me_ref, f32[1,1]{1,0:T(1,128)} %bitcast.4.refs_0_, bf16[8,2,104,256]{3,2,1,0:T(8,128)(2,1)S(1)} %all-to-all-done.refs_1_, bf16[104,2048]{1,0:T(8,128)(2,1)S(1)} %pad.8.refs_2_, f32[104,256]{1,0:T(8,128)S(1)} %broadcast_in_dim.2.refs_3_, ...), custom_call_target="tpu_custom_call" | custom-call | tf_op jit(solution)/shard_map/score/pallas_call | solution.py:188
  44.0 6.3 %all-to-all-start.1 = ((bf16[8,2,104,256]{3,2,1,0:T(8,128)(2,1)}), bf16[8,2,104,256]{3,2,1,0:T(8,128)(2,1)S(1)}, u32[]{:S(2)}, u32[]{:S(2)}) async-start(bf16[8,2,104,256]{3,2,1,0:T(8,128)(2,1)} %get-tuple-element.19), calls=%async_computation.1 | async-start | bytes 1703936 | tf_op jit(solution)/shard_map/all_to_all | solution.py:392
  50.3 10.1 %shape.1 = (bf16[2,2048,1024]{2,1,0:T(8,128)(2,1)}, bf16[2,2048,1024]{2,1,0:T(8,128)(2,1)}) custom-call(bf16[2,2048,1024]{2,1,0:T(8,128)(2,1)} %get-tuple-element.15.preact_ref), custom_call_target="tpu_custom_call" | custom-call | flops 67108864 | bytes 25165824 | tf_op jit(solution)/shard_map/shape/pallas_call | solution.py:105
  60.4 2.4 %all-to-all-done.1.up_ref = bf16[8,2,104,256]{3,2,1,0:T(8,128)(2,1)S(1)} async-done(((bf16[8,2,104,256]{3,2,1,0:T(8,128)(2,1)}), bf16[8,2,104,256]{3,2,1,0:T(8,128)(2,1)S(1)}, u32[]{:S(2)}, u32[]{:S(2)}) %all-to-all-start.1) | async-done | bytes 852000 | tf_op jit(solution)/shard_map/all_to_all | solution.py:392
  62.8 16.7 %backward.1 = (bf16[32,16,1152]{2,1,0:T(8,128)(2,1)S(1)}, bf16[32,16,1152]{2,1,0:T(8,128)(2,1)S(1)}) custom-call(s32[1]{0:T(128)} %bitcast.core_ref, bf16[2,2048,1024]{2,1,0:T(8,128)(2,1)} %bitcast.12, bf16[2,2048,1024]{2,1,0:T(8,128)(2,1)} %get-tuple-element.16.hidden_ref, bf16[2,2048,1024]{2,1,0:T(8,128)(2,1)} %get-tuple-element.17.slope_ref, ...), custom_call_target="tpu_custom_call" | custom-call | tf_op jit(solution)/shard_map/backward/pallas_call | solution.py:280
  79.5 0.1 collective-permute-start.3
  79.6 2.8 %collective-permute-done.3 = bf16[32,16,1152]{2,1,0:T(8,128)(2,1)S(1)} collective-permute-done((bf16[32,16,1152]{2,1,0:T(8,128)(2,1)S(1)}, bf16[32,16,1152]{2,1,0:T(8,128)(2,1)S(1)}, u32[]{:S(2)}, u32[]{:S(2)}) %collective-permute-start.3) | collective-permute-done | bytes 1179680 | tf_op jit(solution)/shard_map/ppermute | solution.py:363
  82.4 1.4 %add_convert_fusion = bf16[32,16,1152]{2,1,0:T(8,128)(2,1)} fusion(bf16[32,16,1152]{2,1,0:T(8,128)(2,1)S(1)} %collective-permute-done.3, bf16[32,16,1152]{2,1,0:T(8,128)(2,1)S(1)} %get-tuple-element.21), kind=kLoop, calls=%fused_computation | loop fusion | flops 2359296 | bytes 3538944 | tf_op jit(solution)/shard_map/convert_element_type | solution.py:395
  83.8 8.5 %all-to-all-start.2 = ((bf16[64,8,1152]{2,1,0:T(8,128)(2,1)}), bf16[64,8,1152]{2,1,0:T(8,128)(2,1)S(1)}, u32[]{:S(2)}, u32[]{:S(2)}) async-start(bf16[64,8,1152]{2,1,0:T(8,128)(2,1)} %bitcast.7), calls=%async_computation.2 | async-start | bytes 2359296 | tf_op jit(solution)/shard_map/all_to_all | solution.py:396
  92.3 15.4 %latent_grad.1 = bf16[2,2048,1024]{2,1,0:T(8,128)(2,1)} custom-call(bf16[2,2048,1024]{2,1,0:T(8,128)(2,1)} %get-tuple-element.17.slope_ref, bf16[8,2,104,256]{3,2,1,0:T(8,128)(2,1)S(1)} %all-to-all-done.1.up_ref, bf16[100,1024]{1,0:T(8,128)(2,1)} %bitcast.15, bf16[1024,1024]{1,0:T(8,128)(2,1)} %win_ref.3), custom_call_target="tpu_custom_call" | custom-call | flops 9663676416 | bytes 16777216 | tf_op jit(solution)/shard_map/latent_grad/pallas_call | solution.py:307
  107.7 3.6 %all-to-all-done.2.pieces_ref = bf16[64,8,1152]{2,1,0:T(8,128)(2,1)S(1)} async-done(((bf16[64,8,1152]{2,1,0:T(8,128)(2,1)}), bf16[64,8,1152]{2,1,0:T(8,128)(2,1)S(1)}, u32[]{:S(2)}, u32[]{:S(2)}) %all-to-all-start.2) | async-done | bytes 1179680 | tf_op jit(solution)/shard_map/all_to_all | solution.py:396
  111.3 0.8 finish.1
  (2 shorter events, 0.0 us)
Async XLA Ops:
  0.6 24.0 %copy-start = (s32[2048]{0:T(1024)S(1)}, s32[2048]{0:T(1024)}, u32[]{:S(2)}) copy-start(s32[2048]{0:T(1024)} %param.10) | copy-start | bytes 24580
  0.6 24.6 %copy-start.1 = (bf16[1,100,2048]{2,1,0:T(8,128)(2,1)S(1)}, bf16[1,100,2048]{2,1,0:T(8,128)(2,1)}, u32[]{:S(2)}) copy-start(bf16[1,100,2048]{2,1,0:T(8,128)(2,1)} %param.9) | copy-start | bytes 1228804
  16.6 8.6 %copy-start.2 = (f32[100]{0:T(128)S(1)}, f32[100]{0:T(128)}, u32[]{:S(2)}) copy-start(f32[100]{0:T(128)} %param.11) | copy-start | bytes 1204
  16.7 22.0 %all-to-all-start = ((bf16[8,2,104,256]{3,2,1,0:T(8,128)(2,1)}), bf16[8,2,104,256]{3,2,1,0:T(8,128)(2,1)S(1)}, u32[]{:S(2)}, u32[]{:S(2)}) async-start(bf16[8,2,104,256]{3,2,1,0:T(8,128)(2,1)} %get-tuple-element.18), calls=%async_computation | async-start | bytes 1703936 | tf_op jit(solution)/shard_map/all_to_all | solution.py:384
  25.2 1.4 %collective-permute-start = (f32[]{:T(128)}, f32[]{:T(128)}, u32[]{:S(2)}, u32[]{:S(2)}) collective-permute-start(f32[]{:T(128)} %convert_reduce_fusion), channel_id=1, source_target_pairs={{0,2},{2,0},{1,3},{3,1},{4,6},{6,4},{5,7},{7,5},{8,10},{10,8},{9,1... | collective-permute-start | bytes 20 | tf_op jit(solution)/shard_map/ppermute | solution.py:363
  27.8 3.7 %collective-permute-start.1 = (f32[]{:T(128)}, f32[]{:T(128)}, u32[]{:S(2)}, u32[]{:S(2)}) collective-permute-start(f32[]{:T(128)} %add.20), channel_id=1, source_target_pairs={{0,4},{4,0},{8,12},{12,8},{1,5},{5,1},{9,13},{13,9},{2,6},{6,2},{1... | collective-permute-start | bytes 20 | tf_op jit(solution)/shard_map/ppermute | solution.py:363
  32.1 4.9 %collective-permute-start.2 = (f32[]{:T(128)}, f32[]{:T(128)}, u32[]{:S(2)}, u32[]{:S(2)}) collective-permute-start(f32[]{:T(128)} %add.21), channel_id=1, source_target_pairs={{0,12},{4,8},{8,4},{12,0},{1,13},{5,9},{9,5},{13,1},{2,14},{6,10},... | collective-permute-start | bytes 20 | tf_op jit(solution)/shard_map/ppermute | solution.py:363
  44.0 18.8 %all-to-all-start.1 = ((bf16[8,2,104,256]{3,2,1,0:T(8,128)(2,1)}), bf16[8,2,104,256]{3,2,1,0:T(8,128)(2,1)S(1)}, u32[]{:S(2)}, u32[]{:S(2)}) async-start(bf16[8,2,104,256]{3,2,1,0:T(8,128)(2,1)} %get-tuple-element.19), calls=%async_computation.1 | async-start | bytes 1703936 | tf_op jit(solution)/shard_map/all_to_all | solution.py:392
  79.5 2.9 %collective-permute-start.3 = (bf16[32,16,1152]{2,1,0:T(8,128)(2,1)S(1)}, bf16[32,16,1152]{2,1,0:T(8,128)(2,1)S(1)}, u32[]{:S(2)}, u32[]{:S(2)}) collective-permute-start(bf16[32,16,1152]{2,1,0:T(8,128)(2,1)S(1)} %get-tuple-element.22), channel_id=1, source_target_pairs={{0,2},{2,0},{1,3},{3,1},{4,6},{6,4},{5,7},{7,5},{8,10},{10,8},{9,1... | collective-permute-start | bytes 3538952 | tf_op jit(solution)/shard_map/ppermute | solution.py:363
  83.8 27.5 %all-to-all-start.2 = ((bf16[64,8,1152]{2,1,0:T(8,128)(2,1)}), bf16[64,8,1152]{2,1,0:T(8,128)(2,1)S(1)}, u32[]{:S(2)}, u32[]{:S(2)}) async-start(bf16[64,8,1152]{2,1,0:T(8,128)(2,1)} %bitcast.7), calls=%async_computation.2 | async-start | bytes 2359296 | tf_op jit(solution)/shard_map/all_to_all | solution.py:396

commit v6 on v5

--- a/solution.py
+++ b/solution.py
@@ -15,7 +15,6 @@
 BF16 = jnp.bfloat16
 F32 = jnp.float32
 
-SHAPE_TILE = 2048
 BLOCK = 256
 VPAD = 104
 WIDE = 128
@@ -24,7 +23,6 @@
 EXTRA = 112
 
 FORWARD_VMEM = 40 << 20
-SHAPE_VMEM = 44 << 20
 SCORE_VMEM = 16 << 20
 BACKWARD_VMEM = 50 << 20
 LATENT_VMEM = 40 << 20
@@ -43,7 +41,7 @@
     wide_ref[:variables, :] = wout_ref[...]
 
 
-def forward_kernel(lat_ref, win_ref, wout_ref, preact_ref, pred_ref, wide_ref):
+def forward_kernel(lat_ref, win_ref, wout_ref, hidden_ref, slope_ref, pred_ref, wide_ref):
     @pl.when((pl.program_id(0) == 0) & (pl.program_id(1) == 0))
     def _():
         widen(wide_ref, wout_ref)
@@ -51,13 +49,17 @@
     for s in range(TILE // SUB):
         rows = pl.ds(s * SUB, SUB)
         u = jnp.dot(lat_ref[0, rows, :], win_ref[...], preferred_element_type=F32).astype(BF16)
-        preact_ref[0, rows, :] = u
-        bent = jnp.tanh(u * (BF16(GELU_C) + BF16(GELU_C * GELU_A) * (u * u)))
-        twice = u + u * bent
+        u2 = u * u
+        bent = jnp.tanh(u * (BF16(GELU_C) + BF16(GELU_C * GELU_A) * u2))
+        half = BF16(0.5) + BF16(0.5) * bent
+        hidden = u * half
+        hidden_ref[0, rows, :] = hidden
+        bend = BF16(GELU_C) + BF16(3.0 * GELU_A * GELU_C) * u2
+        slope_ref[0, rows, :] = half + hidden * ((BF16(1.0) - bent) * bend)
         pred = lax.dot_general(
-            twice, wide_ref[...], (((1,), (1,)), ((), ())), preferred_element_type=F32
+            hidden, wide_ref[...], (((1,), (1,)), ((), ())), preferred_element_type=F32
         )
-        pred_ref[s, 0] = (0.5 * pred.T[:VPAD]).astype(BF16)
+        pred_ref[s, 0] = pred.T[:VPAD].astype(BF16)
 
 
 def forward(latent, w_in, w_out_t):
@@ -74,9 +76,11 @@
         ],
         out_specs=[
             tile,
+            tile,
             pl.BlockSpec((per, 1, VPAD, BLOCK), lambda m, i: (i, m, 0, 0)),
         ],
         out_shape=[
+            pltpu.HBM(latent.shape, BF16),
             pltpu.HBM(latent.shape, BF16),
             jax.ShapeDtypeStruct((points // BLOCK, members, VPAD, BLOCK), BF16),
         ],
@@ -84,36 +88,6 @@
         compiler_params=pltpu.CompilerParams(vmem_limit_bytes=FORWARD_VMEM),
         name="forward",
     )(in_hbm(latent), in_hbm(w_in), in_hbm(w_out_t))
-
-
-def shape_kernel(preact_ref, hidden_ref, slope_ref):
-    for s in range(SHAPE_TILE // SUB):
-        rows = pl.ds(s * SUB, SUB)
-        u = preact_ref[0, rows, :]
-        u2 = u * u
-        bent = jnp.tanh(u * (BF16(GELU_C) + BF16(GELU_C * GELU_A) * u2))
-        half = BF16(0.5) + BF16(0.5) * bent
-        value = u * half
-        hidden_ref[0, rows, :] = value
-        bend = BF16(GELU_C) + BF16(3.0 * GELU_A * GELU_C) * u2
-        slope_ref[0, rows, :] = half + value * ((BF16(1.0) - bent) * bend)
-
-
-def shape(preact):
-    members, points, channels = preact.shape
-    tile = pl.BlockSpec((1, SHAPE_TILE, channels), lambda m, i: (m, i, 0))
-    return pl.pallas_call(
-        shape_kernel,
-        grid=(members, points // SHAPE_TILE),
-        in_specs=[tile],
-        out_specs=[tile, tile],
-        out_shape=[pltpu.HBM(preact.shape, BF16)] * 2,
-        compiler_params=pltpu.CompilerParams(vmem_limit_bytes=SHAPE_VMEM),
-        cost_estimate=pl.CostEstimate(
-            flops=16 * preact.size, bytes_accessed=6 * preact.size, transcendentals=preact.size
-        ),
-        name="shape",
-    )(in_hbm(preact))
 
 
 def score_kernel(
@@ -380,9 +354,8 @@
 
     rows = latent.reshape(date_count * per, points, channels)
     w_out_t = w_out.T
-    preact, pred = forward(rows, w_in, w_out_t)
+    hidden, slopes, pred = forward(rows, w_in, w_out_t)
     every = lax.all_to_all(pred, MEMBER, 0, 0, tiled=True)
-    hidden, slopes = shape(preact)
     truth = jnp.pad(targets[0], ((0, VPAD - variables), (0, 0)))
     var_wide = jnp.broadcast_to(
         jnp.pad(var_weight, (0, VPAD - variables))[:, None], (VPAD, BLOCK)

time: 113 us -> 113 us (level)
  waiting for transfers between devices: 12.4 us -> 22.8 us
  Pallas kernels: 64.3 us -> 55.5 us
  starting transfers between devices: 30.2 us -> 28.4 us
    all_to_all x1, waiting for transfers between devices: 2.37 us -> 12.9 us  [body(): upstream = lax.all_to_all(grad_pred, MEMBER, 0, 0, tiled=True)]
    pallas_call x1 -> x0, Pallas kernels: 10.1 us -> none  [shape(): pl.pallas_call(shape_kernel, grid=(members, points // SHAPE_TILE), in_spe...]
    all_to_all x1, starting transfers between devices: 8.5 us -> 6.97 us  [body(): pieces = lax.all_to_all(both.reshape(-1, 8, wide), REST, 0, 0, tiled=True)]
    pallas_call x1, Pallas kernels: 16 us -> 17.2 us  [forward(): pl.pallas_call(forward_kernel, grid=(members, points // TILE), in_specs=[...]
  transfers between devices with their start and end apart: 7 -> 7, of which waited for: 7 -> 7; matrix products, arithmetic and copies ran while one was open for 1% -> 1% of each run, Pallas kernels for 23% -> 14%
where the time goes in v6:
time: 113 us; the launch traced here: 112 us
  Pallas kernels  55.5 us (49%)
  starting transfers between devices  28.4 us (25%)
  waiting for transfers between devices  22.8 us (20%)
  between operations  3.44 us (3%)
  other arithmetic  1.99 us (2%)
    pallas_call x1, Pallas kernels, forward(): pl.pallas_call(forward_kernel, grid=(members, points // TILE), in_specs=[...  17.2 us
    pallas_call x1, Pallas kernels, backward(): pl.pallas_call(backward_kernel, grid_spec=grid_spec, out_shape=[jax.Shape...  16.7 us
    pallas_call x1, Pallas kernels, latent_grad(): pl.pallas_call(latent_kernel, grid=(members, points // TILE), in_specs=[t...  15.4 us
    all_to_all x1, waiting for transfers between devices, body(): upstream = lax.all_to_all(grad_pred, MEMBER, 0, 0, tiled=True)  12.9 us
    all_to_all x1, starting transfers between devices, body(): every = lax.all_to_all(pred, MEMBER, 0, 0, tiled=True)  7.85 us
    ppermute x4, starting transfers between devices, exchange(): return lax.ppermute(x, axis, [(i, i ^ xor) for i in range(size)])  7.45 us
    all_to_all x1, starting transfers between devices, body(): pieces = lax.all_to_all(both.reshape(-1, 8, wide), REST, 0, 0, tiled=True)  6.97 us
    all_to_all x1, starting transfers between devices, body(): upstream = lax.all_to_all(grad_pred, MEMBER, 0, 0, tiled=True)  6.13 us
  transfers between devices with their start and end apart: 7, of which 7 were waited for; matrix products, arithmetic and copies ran while one was open for 1% of the time, Pallas kernels for 14%

profile of v6, /device:TPU:0, one launch (start us, length us, event | category | flops | bytes accessed | tf_op | source)
XLA Modules:
  0.0 112.2 jit_solution(15563333044460450882)
XLA Ops:
  0.6 0.0 copy-start
  0.6 0.0 copy-start.2
  0.7 0.0 copy-start.1
  0.7 17.2 %forward.1 = (bf16[2,2048,1024]{2,1,0:T(8,128)(2,1)}, bf16[2,2048,1024]{2,1,0:T(8,128)(2,1)}, bf16[8,2,104,256]{3,2,1,0:T(8,128)(2,1)}) custom-call(bf16[2,2048,1024]{2,1,0:T(8,128)(2,1)} %bitcast.11, bf16[1024,1024]{1,0:T(8,128)(2,1)} %win_ref.3, bf16[100,1024]{1,0:T(8,128)(2,1)} %bitcast.13), custom_call_target="tpu_custom_call" | custom-call | tf_op jit(solution)/shard_map/forward/pallas_call | solution.py:69
  17.9 7.9 %all-to-all-start = ((bf16[8,2,104,256]{3,2,1,0:T(8,128)(2,1)}), bf16[8,2,104,256]{3,2,1,0:T(8,128)(2,1)S(1)}, u32[]{:S(2)}, u32[]{:S(2)}) async-start(bf16[8,2,104,256]{3,2,1,0:T(8,128)(2,1)} %get-tuple-element.16), calls=%async_computation | async-start | bytes 1703936 | tf_op jit(solution)/shard_map/all_to_all | solution.py:358
  25.7 0.0 copy-done
  25.7 0.6 convert_reduce_fusion
  26.3 0.0 collective-permute-start
  26.3 0.0 copy-done.2
  26.3 0.0 copy-done.1
  26.4 1.2 %collective-permute-done = f32[]{:T(128)} collective-permute-done((f32[]{:T(128)}, f32[]{:T(128)}, u32[]{:S(2)}, u32[]{:S(2)}) %collective-permute-start) | collective-permute-done | bytes 36 | tf_op jit(solution)/shard_map/ppermute | solution.py:337
  28.9 3.0 %collective-permute-start.1 = (f32[]{:T(128)}, f32[]{:T(128)}, u32[]{:S(2)}, u32[]{:S(2)}) collective-permute-start(f32[]{:T(128)} %add.20), channel_id=1, source_target_pairs={{0,4},{4,0},{8,12},{12,8},{1,5},{5,1},{9,13},{13,9},{2,6},{6,2},{1... | collective-permute-start | bytes 20 | tf_op jit(solution)/shard_map/ppermute | solution.py:337
  31.9 0.6 collective-permute-done.1
  33.1 4.4 %collective-permute-start.2 = (f32[]{:T(128)}, f32[]{:T(128)}, u32[]{:S(2)}, u32[]{:S(2)}) collective-permute-start(f32[]{:T(128)} %add.21), channel_id=1, source_target_pairs={{0,12},{4,8},{8,4},{12,0},{1,13},{5,9},{9,5},{13,1},{2,14},{6,10},... | collective-permute-start | bytes 20 | tf_op jit(solution)/shard_map/ppermute | solution.py:337
  37.5 0.4 collective-permute-done.2
  38.6 1.1 all-to-all-done.refs_1_
  39.7 0.1 broadcast_in_dim.2.refs_3_
  39.8 5.4 %score.1 = (bf16[8,2,104,256]{3,2,1,0:T(8,128)(2,1)}, f32[8,128]{1,0:T(8,128)S(1)}) custom-call(s32[1]{0:T(128)} %bitcast.3.me_ref, f32[1,1]{1,0:T(1,128)} %bitcast.4.refs_0_, bf16[8,2,104,256]{3,2,1,0:T(8,128)(2,1)S(1)} %all-to-all-done.refs_1_, bf16[104,2048]{1,0:T(8,128)(2,1)S(1)} %pad.8.refs_2_, f32[104,256]{1,0:T(8,128)S(1)} %broadcast_in_dim.2.refs_3_, ...), custom_call_target="tpu_custom_call" | custom-call | tf_op jit(solution)/shard_map/score/pallas_call | solution.py:162
  45.2 6.1 %all-to-all-start.1 = ((bf16[8,2,104,256]{3,2,1,0:T(8,128)(2,1)}), bf16[8,2,104,256]{3,2,1,0:T(8,128)(2,1)S(1)}, u32[]{:S(2)}, u32[]{:S(2)}) async-start(bf16[8,2,104,256]{3,2,1,0:T(8,128)(2,1)} %get-tuple-element.17), calls=%async_computation.1 | async-start | bytes 1703936 | tf_op jit(solution)/shard_map/all_to_all | solution.py:365
  51.3 12.9 %all-to-all-done.1.up_ref = bf16[8,2,104,256]{3,2,1,0:T(8,128)(2,1)S(1)} async-done(((bf16[8,2,104,256]{3,2,1,0:T(8,128)(2,1)}), bf16[8,2,104,256]{3,2,1,0:T(8,128)(2,1)S(1)}, u32[]{:S(2)}, u32[]{:S(2)}) %all-to-all-start.1) | async-done | bytes 852000 | tf_op jit(solution)/shard_map/all_to_all | solution.py:365
  64.2 16.7 %backward.1 = (bf16[32,16,1152]{2,1,0:T(8,128)(2,1)S(1)}, bf16[32,16,1152]{2,1,0:T(8,128)(2,1)S(1)}) custom-call(s32[1]{0:T(128)} %bitcast.core_ref, bf16[2,2048,1024]{2,1,0:T(8,128)(2,1)} %bitcast.12, bf16[2,2048,1024]{2,1,0:T(8,128)(2,1)} %get-tuple-element.14.hidden_ref, bf16[2,2048,1024]{2,1,0:T(8,128)(2,1)} %get-tuple-element.15.slope_ref, ...), custom_call_target="tpu_custom_call" | custom-call | tf_op jit(solution)/shard_map/backward/pallas_call | solution.py:254
  80.9 0.1 collective-permute-start.3
  81.0 2.8 %collective-permute-done.3 = bf16[32,16,1152]{2,1,0:T(8,128)(2,1)S(1)} collective-permute-done((bf16[32,16,1152]{2,1,0:T(8,128)(2,1)S(1)}, bf16[32,16,1152]{2,1,0:T(8,128)(2,1)S(1)}, u32[]{:S(2)}, u32[]{:S(2)}) %collective-permute-start.3) | collective-permute-done | bytes 1179680 | tf_op jit(solution)/shard_map/ppermute | solution.py:337
  83.9 1.4 %add_convert_fusion = bf16[32,16,1152]{2,1,0:T(8,128)(2,1)} fusion(bf16[32,16,1152]{2,1,0:T(8,128)(2,1)S(1)} %collective-permute-done.3, bf16[32,16,1152]{2,1,0:T(8,128)(2,1)S(1)} %get-tuple-element.19), kind=kLoop, calls=%fused_computation | loop fusion | flops 2359296 | bytes 3538944 | tf_op jit(solution)/shard_map/convert_element_type | solution.py:368
  85.3 7.0 %all-to-all-start.2 = ((bf16[64,8,1152]{2,1,0:T(8,128)(2,1)}), bf16[64,8,1152]{2,1,0:T(8,128)(2,1)S(1)}, u32[]{:S(2)}, u32[]{:S(2)}) async-start(bf16[64,8,1152]{2,1,0:T(8,128)(2,1)} %bitcast.7), calls=%async_computation.2 | async-start | bytes 2359296 | tf_op jit(solution)/shard_map/all_to_all | solution.py:369
  92.2 15.4 %latent_grad.1 = bf16[2,2048,1024]{2,1,0:T(8,128)(2,1)} custom-call(bf16[2,2048,1024]{2,1,0:T(8,128)(2,1)} %get-tuple-element.15.slope_ref, bf16[8,2,104,256]{3,2,1,0:T(8,128)(2,1)S(1)} %all-to-all-done.1.up_ref, bf16[100,1024]{1,0:T(8,128)(2,1)} %bitcast.15, bf16[1024,1024]{1,0:T(8,128)(2,1)} %win_ref.3), custom_call_target="tpu_custom_call" | custom-call | flops 9663676416 | bytes 16777216 | tf_op jit(solution)/shard_map/latent_grad/pallas_call | solution.py:281
  107.6 3.8 %all-to-all-done.2.pieces_ref = bf16[64,8,1152]{2,1,0:T(8,128)(2,1)S(1)} async-done(((bf16[64,8,1152]{2,1,0:T(8,128)(2,1)}), bf16[64,8,1152]{2,1,0:T(8,128)(2,1)S(1)}, u32[]{:S(2)}, u32[]{:S(2)}) %all-to-all-start.2) | async-done | bytes 1179680 | tf_op jit(solution)/shard_map/all_to_all | solution.py:369
  111.4 0.8 finish.1
  (2 shorter events, 0.0 us)
Async XLA Ops:
  0.6 25.1 %copy-start = (s32[2048]{0:T(1024)S(1)}, s32[2048]{0:T(1024)}, u32[]{:S(2)}) copy-start(s32[2048]{0:T(1024)} %param.10) | copy-start | bytes 24580
  0.6 25.7 %copy-start.2 = (f32[100]{0:T(128)S(1)}, f32[100]{0:T(128)}, u32[]{:S(2)}) copy-start(f32[100]{0:T(128)} %param.11) | copy-start | bytes 1204
  0.7 25.7 %copy-start.1 = (bf16[1,100,2048]{2,1,0:T(8,128)(2,1)S(1)}, bf16[1,100,2048]{2,1,0:T(8,128)(2,1)}, u32[]{:S(2)}) copy-start(bf16[1,100,2048]{2,1,0:T(8,128)(2,1)} %param.9) | copy-start | bytes 1228804
  17.9 21.9 %all-to-all-start = ((bf16[8,2,104,256]{3,2,1,0:T(8,128)(2,1)}), bf16[8,2,104,256]{3,2,1,0:T(8,128)(2,1)S(1)}, u32[]{:S(2)}, u32[]{:S(2)}) async-start(bf16[8,2,104,256]{3,2,1,0:T(8,128)(2,1)} %get-tuple-element.16), calls=%async_computation | async-start | bytes 1703936 | tf_op jit(solution)/shard_map/all_to_all | solution.py:358
  26.3 1.2 %collective-permute-start = (f32[]{:T(128)}, f32[]{:T(128)}, u32[]{:S(2)}, u32[]{:S(2)}) collective-permute-start(f32[]{:T(128)} %convert_reduce_fusion), channel_id=1, source_target_pairs={{0,2},{2,0},{1,3},{3,1},{4,6},{6,4},{5,7},{7,5},{8,10},{10,8},{9,1... | collective-permute-start | bytes 20 | tf_op jit(solution)/shard_map/ppermute | solution.py:337
  28.9 3.6 %collective-permute-start.1 = (f32[]{:T(128)}, f32[]{:T(128)}, u32[]{:S(2)}, u32[]{:S(2)}) collective-permute-start(f32[]{:T(128)} %add.20), channel_id=1, source_target_pairs={{0,4},{4,0},{8,12},{12,8},{1,5},{5,1},{9,13},{13,9},{2,6},{6,2},{1... | collective-permute-start | bytes 20 | tf_op jit(solution)/shard_map/ppermute | solution.py:337
  33.1 4.8 %collective-permute-start.2 = (f32[]{:T(128)}, f32[]{:T(128)}, u32[]{:S(2)}, u32[]{:S(2)}) collective-permute-start(f32[]{:T(128)} %add.21), channel_id=1, source_target_pairs={{0,12},{4,8},{8,4},{12,0},{1,13},{5,9},{9,5},{13,1},{2,14},{6,10},... | collective-permute-start | bytes 20 | tf_op jit(solution)/shard_map/ppermute | solution.py:337
  45.2 19.0 %all-to-all-start.1 = ((bf16[8,2,104,256]{3,2,1,0:T(8,128)(2,1)}), bf16[8,2,104,256]{3,2,1,0:T(8,128)(2,1)S(1)}, u32[]{:S(2)}, u32[]{:S(2)}) async-start(bf16[8,2,104,256]{3,2,1,0:T(8,128)(2,1)} %get-tuple-element.17), calls=%async_computation.1 | async-start | bytes 1703936 | tf_op jit(solution)/shard_map/all_to_all | solution.py:365
  80.9 2.9 %collective-permute-start.3 = (bf16[32,16,1152]{2,1,0:T(8,128)(2,1)S(1)}, bf16[32,16,1152]{2,1,0:T(8,128)(2,1)S(1)}, u32[]{:S(2)}, u32[]{:S(2)}) collective-permute-start(bf16[32,16,1152]{2,1,0:T(8,128)(2,1)S(1)} %get-tuple-element.20), channel_id=1, source_target_pairs={{0,2},{2,0},{1,3},{3,1},{4,6},{6,4},{5,7},{7,5},{8,10},{10,8},{9,1... | collective-permute-start | bytes 3538952 | tf_op jit(solution)/shard_map/ppermute | solution.py:337
  85.3 26.2 %all-to-all-start.2 = ((bf16[64,8,1152]{2,1,0:T(8,128)(2,1)}), bf16[64,8,1152]{2,1,0:T(8,128)(2,1)S(1)}, u32[]{:S(2)}, u32[]{:S(2)}) async-start(bf16[64,8,1152]{2,1,0:T(8,128)(2,1)} %bitcast.7), calls=%async_computation.2 | async-start | bytes 2359296 | tf_op jit(solution)/shard_map/all_to_all | solution.py:369

commit v7 on v6

--- a/solution.py
+++ b/solution.py
@@ -41,10 +41,13 @@
     wide_ref[:variables, :] = wout_ref[...]
 
 
-def forward_kernel(lat_ref, win_ref, wout_ref, hidden_ref, slope_ref, pred_ref, wide_ref):
+def forward_kernel(
+    lat_ref, win_ref, wout_ref, area_ref, hidden_ref, slope_ref, pred_ref, total_ref, wide_ref
+):
     @pl.when((pl.program_id(0) == 0) & (pl.program_id(1) == 0))
     def _():
         widen(wide_ref, wout_ref)
+        total_ref[0, 0] = jnp.sum(area_ref[...].astype(F32))
 
     for s in range(TILE // SUB):
         rows = pl.ds(s * SUB, SUB)
@@ -62,7 +65,7 @@
         pred_ref[s, 0] = pred.T[:VPAD].astype(BF16)
 
 
-def forward(latent, w_in, w_out_t):
+def forward(latent, w_in, w_out_t, area):
     members, points, channels = latent.shape
     per = TILE // BLOCK
     tile = pl.BlockSpec((1, TILE, channels), lambda m, i: (m, i, 0))
@@ -73,37 +76,44 @@
             tile,
             pl.BlockSpec((channels, channels), lambda m, i: (0, 0)),
             pl.BlockSpec(w_out_t.shape, lambda m, i: (0, 0)),
+            pl.BlockSpec(area.shape, lambda m, i: (0, 0, 0)),
         ],
         out_specs=[
             tile,
             tile,
             pl.BlockSpec((per, 1, VPAD, BLOCK), lambda m, i: (i, m, 0, 0)),
+            pl.BlockSpec(memory_space=pltpu.SMEM),
         ],
         out_shape=[
             pltpu.HBM(latent.shape, BF16),
             pltpu.HBM(latent.shape, BF16),
             jax.ShapeDtypeStruct((points // BLOCK, members, VPAD, BLOCK), BF16),
+            jax.ShapeDtypeStruct((1, 1), F32),
         ],
         scratch_shapes=[pltpu.VMEM((WIDE, channels), BF16)],
         compiler_params=pltpu.CompilerParams(vmem_limit_bytes=FORWARD_VMEM),
         name="forward",
-    )(in_hbm(latent), in_hbm(w_in), in_hbm(w_out_t))
+    )(in_hbm(latent), in_hbm(w_in), in_hbm(w_out_t), area)
 
 
 def score_kernel(
-    members, scale_ref, pred_ref, truth_ref, var_ref, area_ref, grad_ref, share_ref, held_ref, true_ref
+    members, scale_ref, pred_ref, truth_ref, var_ref, area_ref, grad_ref, share_ref,
+    held_ref, true_ref, each_ref,
 ):
     per = pred_ref.shape[1]
     scale = scale_ref[0, 0]
     self_phi = members * math.sqrt(SMOOTH) / (2.0 * (members - 1))
-    true_ref[...] = truth_ref[...].astype(F32)
+    variables = truth_ref.shape[0]
+    true_ref[...] = jnp.zeros_like(true_ref)
+    true_ref[:variables, :] = truth_ref[...].astype(F32)
+    each_ref[...] = jnp.broadcast_to(var_ref[...], (WIDE, WIDE)).T[:VPAD]
     for m in range(members):
         held_ref[m] = pred_ref[m // per, m % per].astype(F32)
 
     def part(rows, lanes):
         truth = true_ref[rows, lanes]
         x = [held_ref[m, rows, lanes] - truth for m in range(members)]
-        weight = var_ref[rows, lanes] * (area_ref[0, :, lanes].astype(F32) * scale)
+        weight = each_ref[rows, :] * (area_ref[0, :, lanes].astype(F32) * scale)
         grads = [None] * members
         roots = None
         for m in range(members - 1):
@@ -145,7 +155,7 @@
         in_specs=[
             pl.BlockSpec(memory_space=pltpu.SMEM),
             vmem,
-            pl.BlockSpec((VPAD, BLOCK), lambda i, me: (0, me[0])),
+            pl.BlockSpec((truth.shape[0], BLOCK), lambda i, me: (0, me[0])),
             vmem,
             pl.BlockSpec((1, 1, BLOCK), lambda i, me: (me[0], 0, 0)),
         ],
@@ -153,6 +163,7 @@
         scratch_shapes=[
             pltpu.VMEM((members, VPAD, BLOCK), F32),
             pltpu.VMEM((VPAD, BLOCK), F32),
+            pltpu.VMEM((VPAD, WIDE), F32),
         ],
     )
 
@@ -347,21 +358,16 @@
     me = (lax.axis_index("xh") * lax.axis_size("z") + lax.axis_index("z")).astype(jnp.int32)
     core = lax.axis_index("core").astype(jnp.int32)
 
-    area_total = jnp.sum(area_units.astype(F32))
+    rows = latent.reshape(date_count * per, points, channels)
+    w_out_t = w_out.T
+    area = area_units.reshape(points // BLOCK, 1, BLOCK)
+    hidden, slopes, pred, area_total = forward(rows, w_in, w_out_t, area)
     for axis, xor in (("core", 1), ("y", 1), ("y", 3)):
         area_total = area_total + exchange(area_total, axis, xor)
-    scale = (npoints / area_total).reshape(1, 1)
-
-    rows = latent.reshape(date_count * per, points, channels)
-    w_out_t = w_out.T
-    hidden, slopes, pred = forward(rows, w_in, w_out_t)
+    scale = npoints / area_total
     every = lax.all_to_all(pred, MEMBER, 0, 0, tiled=True)
-    truth = jnp.pad(targets[0], ((0, VPAD - variables), (0, 0)))
-    var_wide = jnp.broadcast_to(
-        jnp.pad(var_weight, (0, VPAD - variables))[:, None], (VPAD, BLOCK)
-    )
-    area = area_units.reshape(points // BLOCK, 1, BLOCK)
-    grad_pred, share = score(me.reshape(1), scale, every, truth, var_wide, area)
+    var_row = jnp.pad(var_weight, (0, WIDE - variables)).reshape(1, WIDE)
+    grad_pred, share = score(me.reshape(1), scale, every, targets[0], var_row, area)
     upstream = lax.all_to_all(grad_pred, MEMBER, 0, 0, tiled=True)
     mine, other = backward(core.reshape(1), rows, hidden, slopes, upstream, w_out_t, share)
     wide = channels + WIDE

time: 113 us -> 113 us (level)
  transfers between devices with their start and end apart: 7 -> 7, of which waited for: 7 -> 7; matrix products, arithmetic and copies ran while one was open for 1% -> 0% of each run, Pallas kernels for 14% -> 14%
where the time goes in v7:
time: 113 us; the launch traced here: 112 us
  Pallas kernels  55.6 us (49%)
  starting transfers between devices  28.1 us (25%)
  waiting for transfers between devices  23.5 us (21%)
  between operations  3.09 us (3%)
  other arithmetic  1.41 us (1%)
    pallas_call x1, Pallas kernels, forward(): pl.pallas_call(forward_kernel, grid=(members, points // TILE), in_specs=[...  17.4 us
    pallas_call x1, Pallas kernels, backward(): pl.pallas_call(backward_kernel, grid_spec=grid_spec, out_shape=[jax.Shape...  16.7 us
    pallas_call x1, Pallas kernels, latent_grad(): pl.pallas_call(latent_kernel, grid=(members, points // TILE), in_specs=[t...  15.4 us
    all_to_all x1, waiting for transfers between devices, body(): upstream = lax.all_to_all(grad_pred, MEMBER, 0, 0, tiled=True)  12.6 us
    all_to_all x1, starting transfers between devices, body(): every = lax.all_to_all(pred, MEMBER, 0, 0, tiled=True)  7.86 us
    ppermute x4, starting transfers between devices, exchange(): return lax.ppermute(x, axis, [(i, i ^ xor) for i in range(size)])  7.43 us
    all_to_all x1, starting transfers between devices, body(): pieces = lax.all_to_all(both.reshape(-1, 8, wide), REST, 0, 0, tiled=True)  7.18 us
    all_to_all x1, starting transfers between devices, body(): upstream = lax.all_to_all(grad_pred, MEMBER, 0, 0, tiled=True)  5.67 us
  transfers between devices with their start and end apart: 7, of which 7 were waited for; matrix products, arithmetic and copies ran while one was open for 0% of the time, Pallas kernels for 14%

profile of v7, /device:TPU:0, one launch (start us, length us, event | category | flops | bytes accessed | tf_op | source)
XLA Modules:
  0.0 112.4 jit_solution(10657689249964434039)
XLA Ops:
  0.6 0.0 copy-start.1
  0.6 0.7 copy-done.1
  1.3 0.0 copy-start.3
  1.3 0.0 copy-start
  1.3 0.0 copy-start.2
  1.3 17.4 %forward.1 = (bf16[2,2048,1024]{2,1,0:T(8,128)(2,1)}, bf16[2,2048,1024]{2,1,0:T(8,128)(2,1)}, bf16[8,2,104,256]{3,2,1,0:T(8,128)(2,1)}, f32[1,1]{1,0:T(1,128)}) custom-call(bf16[2,2048,1024]{2,1,0:T(8,128)(2,1)} %bitcast.14, bf16[1024,1024]{1,0:T(8,128)(2,1)} %win_ref.3, bf16[100,1024]{1,0:T(8,128)(2,1)} %bitcast.16, s32[8,1,256]{2,1,0:T(1,128)S(1)} %bitcast.12), custom_call_target="tpu_custom_call" | custom-call | tf_op jit(solution)/shard_map/forward/pallas_call | solution.py:72
  18.7 7.9 %all-to-all-start = ((bf16[8,2,104,256]{3,2,1,0:T(8,128)(2,1)}), bf16[8,2,104,256]{3,2,1,0:T(8,128)(2,1)S(1)}, u32[]{:S(2)}, u32[]{:S(2)}) async-start(bf16[8,2,104,256]{3,2,1,0:T(8,128)(2,1)} %get-tuple-element.18), calls=%async_computation | async-start | bytes 1703936 | tf_op jit(solution)/shard_map/all_to_all | solution.py:368
  26.6 0.0 collective-permute-start
  26.6 0.0 copy-done.3
  26.6 1.3 %collective-permute-done = f32[1,1]{1,0:T(1,128)} collective-permute-done((f32[1,1]{1,0:T(1,128)}, f32[1,1]{1,0:T(1,128)}, u32[]{:S(2)}, u32[]{:S(2)}) %collective-permute-start) | collective-permute-done | bytes 36 | tf_op jit(solution)/shard_map/ppermute | solution.py:348
  29.2 3.0 %collective-permute-start.1 = (f32[1,1]{1,0:T(1,128)}, f32[1,1]{1,0:T(1,128)}, u32[]{:S(2)}, u32[]{:S(2)}) collective-permute-start(f32[1,1]{1,0:T(1,128)} %add.18), channel_id=1, source_target_pairs={{0,4},{4,0},{8,12},{12,8},{1,5},{5,1},{9,13},{13,9},{2,6},{6,2},{1... | collective-permute-start | bytes 20 | tf_op jit(solution)/shard_map/ppermute | solution.py:348
  32.1 0.8 collective-permute-done.1
  33.5 4.4 %collective-permute-start.2 = (f32[1,1]{1,0:T(1,128)}, f32[1,1]{1,0:T(1,128)}, u32[]{:S(2)}, u32[]{:S(2)}) collective-permute-start(f32[1,1]{1,0:T(1,128)} %add.19), channel_id=1, source_target_pairs={{0,12},{4,8},{8,4},{12,0},{1,13},{5,9},{9,5},{13,1},{2,14},{6,10},... | collective-permute-start | bytes 20 | tf_op jit(solution)/shard_map/ppermute | solution.py:348
  37.9 0.6 collective-permute-done.2
  39.0 1.6 %all-to-all-done.refs_1_ = bf16[8,2,104,256]{3,2,1,0:T(8,128)(2,1)S(1)} async-done(((bf16[8,2,104,256]{3,2,1,0:T(8,128)(2,1)}), bf16[8,2,104,256]{3,2,1,0:T(8,128)(2,1)S(1)}, u32[]{:S(2)}, u32[]{:S(2)}) %all-to-all-start) | async-done | bytes 852000 | tf_op jit(solution)/shard_map/all_to_all | solution.py:368
  40.6 0.0 copy-done
  40.6 0.0 copy-done.2
  40.6 5.3 %score.1 = (bf16[8,2,104,256]{3,2,1,0:T(8,128)(2,1)}, f32[8,128]{1,0:T(8,128)S(1)}) custom-call(s32[1]{0:T(128)} %bitcast.4.me_ref, f32[1,1]{1,0:T(1,128)S(6)} %div.3.refs_0_, bf16[8,2,104,256]{3,2,1,0:T(8,128)(2,1)S(1)} %all-to-all-done.refs_1_, bf16[100,2048]{1,0:T(8,128)(2,1)S(1)} %bitcast.11, f32[1,128]{1,0:T(1,128)S(1)} %pad_bitcast_fusion.refs_3_, ...), custom_call_target="tpu_custom_call" | custom-call | tf_op jit(solution)/shard_map/score/pallas_call | solution.py:173
  45.9 5.7 %all-to-all-start.1 = ((bf16[8,2,104,256]{3,2,1,0:T(8,128)(2,1)}), bf16[8,2,104,256]{3,2,1,0:T(8,128)(2,1)S(1)}, u32[]{:S(2)}, u32[]{:S(2)}) async-start(bf16[8,2,104,256]{3,2,1,0:T(8,128)(2,1)} %get-tuple-element.19), calls=%async_computation.1 | async-start | bytes 1703936 | tf_op jit(solution)/shard_map/all_to_all | solution.py:371
  51.6 12.6 %all-to-all-done.1.up_ref = bf16[8,2,104,256]{3,2,1,0:T(8,128)(2,1)S(1)} async-done(((bf16[8,2,104,256]{3,2,1,0:T(8,128)(2,1)}), bf16[8,2,104,256]{3,2,1,0:T(8,128)(2,1)S(1)}, u32[]{:S(2)}, u32[]{:S(2)}) %all-to-all-start.1) | async-done | bytes 852000 | tf_op jit(solution)/shard_map/all_to_all | solution.py:371
  64.2 16.7 %backward.1 = (bf16[32,16,1152]{2,1,0:T(8,128)(2,1)S(1)}, bf16[32,16,1152]{2,1,0:T(8,128)(2,1)S(1)}) custom-call(s32[1]{0:T(128)} %bitcast.core_ref, bf16[2,2048,1024]{2,1,0:T(8,128)(2,1)} %bitcast.15, bf16[2,2048,1024]{2,1,0:T(8,128)(2,1)} %get-tuple-element.15.hidden_ref, bf16[2,2048,1024]{2,1,0:T(8,128)(2,1)} %get-tuple-element.16.slope_ref, ...), custom_call_target="tpu_custom_call" | custom-call | tf_op jit(solution)/shard_map/backward/pallas_call | solution.py:265
  80.9 0.1 collective-permute-start.3
  81.0 2.8 %collective-permute-done.3 = bf16[32,16,1152]{2,1,0:T(8,128)(2,1)S(1)} collective-permute-done((bf16[32,16,1152]{2,1,0:T(8,128)(2,1)S(1)}, bf16[32,16,1152]{2,1,0:T(8,128)(2,1)S(1)}, u32[]{:S(2)}, u32[]{:S(2)}) %collective-permute-start.3) | collective-permute-done | bytes 1179680 | tf_op jit(solution)/shard_map/ppermute | solution.py:348
  83.9 1.4 %add_convert_fusion = bf16[32,16,1152]{2,1,0:T(8,128)(2,1)} fusion(bf16[32,16,1152]{2,1,0:T(8,128)(2,1)S(1)} %collective-permute-done.3, bf16[32,16,1152]{2,1,0:T(8,128)(2,1)S(1)} %get-tuple-element.21), kind=kLoop, calls=%fused_computation | loop fusion | flops 2359296 | bytes 3538944 | tf_op jit(solution)/shard_map/convert_element_type | solution.py:374
  85.3 7.2 %all-to-all-start.2 = ((bf16[64,8,1152]{2,1,0:T(8,128)(2,1)}), bf16[64,8,1152]{2,1,0:T(8,128)(2,1)S(1)}, u32[]{:S(2)}, u32[]{:S(2)}) async-start(bf16[64,8,1152]{2,1,0:T(8,128)(2,1)} %bitcast.7), calls=%async_computation.2 | async-start | bytes 2359296 | tf_op jit(solution)/shard_map/all_to_all | solution.py:375
  92.5 15.4 %latent_grad.1 = bf16[2,2048,1024]{2,1,0:T(8,128)(2,1)} custom-call(bf16[2,2048,1024]{2,1,0:T(8,128)(2,1)} %get-tuple-element.16.slope_ref, bf16[8,2,104,256]{3,2,1,0:T(8,128)(2,1)S(1)} %all-to-all-done.1.up_ref, bf16[100,1024]{1,0:T(8,128)(2,1)} %bitcast.18, bf16[1024,1024]{1,0:T(8,128)(2,1)} %win_ref.3), custom_call_target="tpu_custom_call" | custom-call | flops 9663676416 | bytes 16777216 | tf_op jit(solution)/shard_map/latent_grad/pallas_call | solution.py:292
  107.8 3.8 %all-to-all-done.2.pieces_ref = bf16[64,8,1152]{2,1,0:T(8,128)(2,1)S(1)} async-done(((bf16[64,8,1152]{2,1,0:T(8,128)(2,1)}), bf16[64,8,1152]{2,1,0:T(8,128)(2,1)S(1)}, u32[]{:S(2)}, u32[]{:S(2)}) %all-to-all-start.2) | async-done | bytes 1179680 | tf_op jit(solution)/shard_map/all_to_all | solution.py:375
  111.7 0.8 finish.1
  (1 shorter events, 0.0 us)
Async XLA Ops:
  0.6 0.7 copy-start.1
  1.3 25.3 %copy-start.3 = (f32[100]{0:T(128)S(1)}, f32[100]{0:T(128)}, u32[]{:S(2)}) copy-start(f32[100]{0:T(128)} %param.11) | copy-start | bytes 1204
  1.3 39.3 %copy-start = (bf16[1,100,2048]{2,1,0:T(8,128)(2,1)S(1)}, bf16[1,100,2048]{2,1,0:T(8,128)(2,1)}, u32[]{:S(2)}) copy-start(bf16[1,100,2048]{2,1,0:T(8,128)(2,1)} %param.9) | copy-start | bytes 1228804
  1.3 39.3 %copy-start.2 = (s32[2048]{0:T(1024)S(1)}, s32[2048]{0:T(1024)}, u32[]{:S(2)}) copy-start(s32[2048]{0:T(1024)} %param.10) | copy-start | bytes 24580
  18.7 21.9 %all-to-all-start = ((bf16[8,2,104,256]{3,2,1,0:T(8,128)(2,1)}), bf16[8,2,104,256]{3,2,1,0:T(8,128)(2,1)S(1)}, u32[]{:S(2)}, u32[]{:S(2)}) async-start(bf16[8,2,104,256]{3,2,1,0:T(8,128)(2,1)} %get-tuple-element.18), calls=%async_computation | async-start | bytes 1703936 | tf_op jit(solution)/shard_map/all_to_all | solution.py:368
  26.6 1.4 %collective-permute-start = (f32[1,1]{1,0:T(1,128)}, f32[1,1]{1,0:T(1,128)}, u32[]{:S(2)}, u32[]{:S(2)}) collective-permute-start(f32[1,1]{1,0:T(1,128)} %get-tuple-element.17), channel_id=1, source_target_pairs={{0,2},{2,0},{1,3},{3,1},{4,6},{6,4},{5,7},{7,5},{8,10},{10,8},{9,1... | collective-permute-start | bytes 20 | tf_op jit(solution)/shard_map/ppermute | solution.py:348
  29.2 3.7 %collective-permute-start.1 = (f32[1,1]{1,0:T(1,128)}, f32[1,1]{1,0:T(1,128)}, u32[]{:S(2)}, u32[]{:S(2)}) collective-permute-start(f32[1,1]{1,0:T(1,128)} %add.18), channel_id=1, source_target_pairs={{0,4},{4,0},{8,12},{12,8},{1,5},{5,1},{9,13},{13,9},{2,6},{6,2},{1... | collective-permute-start | bytes 20 | tf_op jit(solution)/shard_map/ppermute | solution.py:348
  33.5 4.9 %collective-permute-start.2 = (f32[1,1]{1,0:T(1,128)}, f32[1,1]{1,0:T(1,128)}, u32[]{:S(2)}, u32[]{:S(2)}) collective-permute-start(f32[1,1]{1,0:T(1,128)} %add.19), channel_id=1, source_target_pairs={{0,12},{4,8},{8,4},{12,0},{1,13},{5,9},{9,5},{13,1},{2,14},{6,10},... | collective-permute-start | bytes 20 | tf_op jit(solution)/shard_map/ppermute | solution.py:348
  45.9 18.3 %all-to-all-start.1 = ((bf16[8,2,104,256]{3,2,1,0:T(8,128)(2,1)}), bf16[8,2,104,256]{3,2,1,0:T(8,128)(2,1)S(1)}, u32[]{:S(2)}, u32[]{:S(2)}) async-start(bf16[8,2,104,256]{3,2,1,0:T(8,128)(2,1)} %get-tuple-element.19), calls=%async_computation.1 | async-start | bytes 1703936 | tf_op jit(solution)/shard_map/all_to_all | solution.py:371
  80.9 2.9 %collective-permute-start.3 = (bf16[32,16,1152]{2,1,0:T(8,128)(2,1)S(1)}, bf16[32,16,1152]{2,1,0:T(8,128)(2,1)S(1)}, u32[]{:S(2)}, u32[]{:S(2)}) collective-permute-start(bf16[32,16,1152]{2,1,0:T(8,128)(2,1)S(1)} %get-tuple-element.22), channel_id=1, source_target_pairs={{0,2},{2,0},{1,3},{3,1},{4,6},{6,4},{5,7},{7,5},{8,10},{10,8},{9,1... | collective-permute-start | bytes 3538952 | tf_op jit(solution)/shard_map/ppermute | solution.py:348
  85.3 26.4 %all-to-all-start.2 = ((bf16[64,8,1152]{2,1,0:T(8,128)(2,1)}), bf16[64,8,1152]{2,1,0:T(8,128)(2,1)S(1)}, u32[]{:S(2)}, u32[]{:S(2)}) async-start(bf16[64,8,1152]{2,1,0:T(8,128)(2,1)} %bitcast.7), calls=%async_computation.2 | async-start | bytes 2359296 | tf_op jit(solution)/shard_map/all_to_all | solution.py:375

commit v8 on v7

--- a/solution.py
+++ b/solution.py
@@ -106,7 +106,8 @@
     variables = truth_ref.shape[0]
     true_ref[...] = jnp.zeros_like(true_ref)
     true_ref[:variables, :] = truth_ref[...].astype(F32)
-    each_ref[...] = jnp.broadcast_to(var_ref[...], (WIDE, WIDE)).T[:VPAD]
+    each_ref[...] = jnp.zeros_like(each_ref)
+    each_ref[:variables, :] = jnp.broadcast_to(var_ref[...], (WIDE, variables)).T
     for m in range(members):
         held_ref[m] = pred_ref[m // per, m % per].astype(F32)
 
@@ -366,7 +367,7 @@
         area_total = area_total + exchange(area_total, axis, xor)
     scale = npoints / area_total
     every = lax.all_to_all(pred, MEMBER, 0, 0, tiled=True)
-    var_row = jnp.pad(var_weight, (0, WIDE - variables)).reshape(1, WIDE)
+    var_row = var_weight.reshape(1, variables)
     grad_pred, share = score(me.reshape(1), scale, every, targets[0], var_row, area)
     upstream = lax.all_to_all(grad_pred, MEMBER, 0, 0, tiled=True)
     mine, other = backward(core.reshape(1), rows, hidden, slopes, upstream, w_out_t, share)

time: 113 us -> 113 us (level)
  no operation moved by 1% of the time
where the time goes in v8:
time: 113 us; the launch traced here: 112 us
  Pallas kernels  55.6 us (49%)
  starting transfers between devices  28.1 us (25%)
  waiting for transfers between devices  23.5 us (21%)
  between operations  3.08 us (3%)
  other arithmetic  1.41 us (1%)
    pallas_call x1, Pallas kernels, forward(): pl.pallas_call(forward_kernel, grid=(members, points // TILE), in_specs=[...  17.4 us
    pallas_call x1, Pallas kernels, backward(): pl.pallas_call(backward_kernel, grid_spec=grid_spec, out_shape=[jax.Shape...  16.7 us
    pallas_call x1, Pallas kernels, latent_grad(): pl.pallas_call(latent_kernel, grid=(members, points // TILE), in_specs=[t...  15.4 us
    all_to_all x1, waiting for transfers between devices, body(): upstream = lax.all_to_all(grad_pred, MEMBER, 0, 0, tiled=True)  12.6 us
    all_to_all x1, starting transfers between devices, body(): every = lax.all_to_all(pred, MEMBER, 0, 0, tiled=True)  7.85 us
    ppermute x4, starting transfers between devices, exchange(): return lax.ppermute(x, axis, [(i, i ^ xor) for i in range(size)])  7.43 us
    all_to_all x1, starting transfers between devices, body(): pieces = lax.all_to_all(both.reshape(-1, 8, wide), REST, 0, 0, tiled=True)  7.18 us
    all_to_all x1, starting transfers between devices, body(): upstream = lax.all_to_all(grad_pred, MEMBER, 0, 0, tiled=True)  5.67 us
  transfers between devices with their start and end apart: 7, of which 7 were waited for; matrix products, arithmetic and copies ran while one was open for 0% of the time, Pallas kernels for 14%

profile of v8, /device:TPU:0, one launch (start us, length us, event | category | flops | bytes accessed | tf_op | source)
XLA Modules:
  0.0 112.5 jit_solution(13101090551423021846)
XLA Ops:
  0.6 0.0 copy-start.1
  0.6 0.7 copy-done.1
  1.3 0.0 copy-start
  1.3 0.0 copy-start.2
  1.3 0.0 copy-start.3
  1.3 17.4 %forward.1 = (bf16[2,2048,1024]{2,1,0:T(8,128)(2,1)}, bf16[2,2048,1024]{2,1,0:T(8,128)(2,1)}, bf16[8,2,104,256]{3,2,1,0:T(8,128)(2,1)}, f32[1,1]{1,0:T(1,128)}) custom-call(bf16[2,2048,1024]{2,1,0:T(8,128)(2,1)} %bitcast.14, bf16[1024,1024]{1,0:T(8,128)(2,1)} %win_ref.3, bf16[100,1024]{1,0:T(8,128)(2,1)} %bitcast.16, s32[8,1,256]{2,1,0:T(1,128)S(1)} %bitcast.11), custom_call_target="tpu_custom_call" | custom-call | tf_op jit(solution)/shard_map/forward/pallas_call | solution.py:72
  18.7 7.8 %all-to-all-start = ((bf16[8,2,104,256]{3,2,1,0:T(8,128)(2,1)}), bf16[8,2,104,256]{3,2,1,0:T(8,128)(2,1)S(1)}, u32[]{:S(2)}, u32[]{:S(2)}) async-start(bf16[8,2,104,256]{3,2,1,0:T(8,128)(2,1)} %get-tuple-element.18), calls=%async_computation | async-start | bytes 1703936 | tf_op jit(solution)/shard_map/all_to_all | solution.py:369
  26.6 0.0 collective-permute-start
  26.6 1.4 %collective-permute-done = f32[1,1]{1,0:T(1,128)} collective-permute-done((f32[1,1]{1,0:T(1,128)}, f32[1,1]{1,0:T(1,128)}, u32[]{:S(2)}, u32[]{:S(2)}) %collective-permute-start) | collective-permute-done | bytes 36 | tf_op jit(solution)/shard_map/ppermute | solution.py:349
  29.2 3.0 %collective-permute-start.1 = (f32[1,1]{1,0:T(1,128)}, f32[1,1]{1,0:T(1,128)}, u32[]{:S(2)}, u32[]{:S(2)}) collective-permute-start(f32[1,1]{1,0:T(1,128)} %add.16), channel_id=1, source_target_pairs={{0,4},{4,0},{8,12},{12,8},{1,5},{5,1},{9,13},{13,9},{2,6},{6,2},{1... | collective-permute-start | bytes 20 | tf_op jit(solution)/shard_map/ppermute | solution.py:349
  32.1 0.8 collective-permute-done.1
  33.5 4.4 %collective-permute-start.2 = (f32[1,1]{1,0:T(1,128)}, f32[1,1]{1,0:T(1,128)}, u32[]{:S(2)}, u32[]{:S(2)}) collective-permute-start(f32[1,1]{1,0:T(1,128)} %add.17), channel_id=1, source_target_pairs={{0,12},{4,8},{8,4},{12,0},{1,13},{5,9},{9,5},{13,1},{2,14},{6,10},... | collective-permute-start | bytes 20 | tf_op jit(solution)/shard_map/ppermute | solution.py:349
  37.9 0.5 collective-permute-done.2
  39.0 1.6 %all-to-all-done.refs_1_ = bf16[8,2,104,256]{3,2,1,0:T(8,128)(2,1)S(1)} async-done(((bf16[8,2,104,256]{3,2,1,0:T(8,128)(2,1)}), bf16[8,2,104,256]{3,2,1,0:T(8,128)(2,1)S(1)}, u32[]{:S(2)}, u32[]{:S(2)}) %all-to-all-start) | async-done | bytes 852000 | tf_op jit(solution)/shard_map/all_to_all | solution.py:369
  40.6 0.0 copy-done
  40.6 0.0 copy-done.2
  40.6 0.0 copy-done.3
  40.6 5.3 %score.1 = (bf16[8,2,104,256]{3,2,1,0:T(8,128)(2,1)}, f32[8,128]{1,0:T(8,128)S(1)}) custom-call(s32[1]{0:T(128)} %bitcast.4.me_ref, f32[1,1]{1,0:T(1,128)S(6)} %div.3.refs_0_, bf16[8,2,104,256]{3,2,1,0:T(8,128)(2,1)S(1)} %all-to-all-done.refs_1_, bf16[100,2048]{1,0:T(8,128)(2,1)S(1)} %bitcast.10, f32[1,100]{1,0:T(1,128)S(1)} %bitcast.13, ...), custom_call_target="tpu_custom_call" | custom-call | tf_op jit(solution)/shard_map/score/pallas_call | solution.py:174
  45.9 5.7 %all-to-all-start.1 = ((bf16[8,2,104,256]{3,2,1,0:T(8,128)(2,1)}), bf16[8,2,104,256]{3,2,1,0:T(8,128)(2,1)S(1)}, u32[]{:S(2)}, u32[]{:S(2)}) async-start(bf16[8,2,104,256]{3,2,1,0:T(8,128)(2,1)} %get-tuple-element.19), calls=%async_computation.1 | async-start | bytes 1703936 | tf_op jit(solution)/shard_map/all_to_all | solution.py:372
  51.6 12.6 %all-to-all-done.1.up_ref = bf16[8,2,104,256]{3,2,1,0:T(8,128)(2,1)S(1)} async-done(((bf16[8,2,104,256]{3,2,1,0:T(8,128)(2,1)}), bf16[8,2,104,256]{3,2,1,0:T(8,128)(2,1)S(1)}, u32[]{:S(2)}, u32[]{:S(2)}) %all-to-all-start.1) | async-done | bytes 852000 | tf_op jit(solution)/shard_map/all_to_all | solution.py:372
  64.2 16.7 %backward.1 = (bf16[32,16,1152]{2,1,0:T(8,128)(2,1)S(1)}, bf16[32,16,1152]{2,1,0:T(8,128)(2,1)S(1)}) custom-call(s32[1]{0:T(128)} %bitcast.core_ref, bf16[2,2048,1024]{2,1,0:T(8,128)(2,1)} %bitcast.15, bf16[2,2048,1024]{2,1,0:T(8,128)(2,1)} %get-tuple-element.15.hidden_ref, bf16[2,2048,1024]{2,1,0:T(8,128)(2,1)} %get-tuple-element.16.slope_ref, ...), custom_call_target="tpu_custom_call" | custom-call | tf_op jit(solution)/shard_map/backward/pallas_call | solution.py:266
  80.9 0.1 collective-permute-start.3
  81.0 2.8 %collective-permute-done.3 = bf16[32,16,1152]{2,1,0:T(8,128)(2,1)S(1)} collective-permute-done((bf16[32,16,1152]{2,1,0:T(8,128)(2,1)S(1)}, bf16[32,16,1152]{2,1,0:T(8,128)(2,1)S(1)}, u32[]{:S(2)}, u32[]{:S(2)}) %collective-permute-start.3) | collective-permute-done | bytes 1179680 | tf_op jit(solution)/shard_map/ppermute | solution.py:349
  83.9 1.4 %add_convert_fusion = bf16[32,16,1152]{2,1,0:T(8,128)(2,1)} fusion(bf16[32,16,1152]{2,1,0:T(8,128)(2,1)S(1)} %collective-permute-done.3, bf16[32,16,1152]{2,1,0:T(8,128)(2,1)S(1)} %get-tuple-element.21), kind=kLoop, calls=%fused_computation | loop fusion | flops 2359296 | bytes 3538944 | tf_op jit(solution)/shard_map/convert_element_type | solution.py:375
  85.3 7.2 %all-to-all-start.2 = ((bf16[64,8,1152]{2,1,0:T(8,128)(2,1)}), bf16[64,8,1152]{2,1,0:T(8,128)(2,1)S(1)}, u32[]{:S(2)}, u32[]{:S(2)}) async-start(bf16[64,8,1152]{2,1,0:T(8,128)(2,1)} %bitcast.7), calls=%async_computation.2 | async-start | bytes 2359296 | tf_op jit(solution)/shard_map/all_to_all | solution.py:376
  92.5 15.4 %latent_grad.1 = bf16[2,2048,1024]{2,1,0:T(8,128)(2,1)} custom-call(bf16[2,2048,1024]{2,1,0:T(8,128)(2,1)} %get-tuple-element.16.slope_ref, bf16[8,2,104,256]{3,2,1,0:T(8,128)(2,1)S(1)} %all-to-all-done.1.up_ref, bf16[100,1024]{1,0:T(8,128)(2,1)} %bitcast.18, bf16[1024,1024]{1,0:T(8,128)(2,1)} %win_ref.3), custom_call_target="tpu_custom_call" | custom-call | flops 9663676416 | bytes 16777216 | tf_op jit(solution)/shard_map/latent_grad/pallas_call | solution.py:293
  107.9 3.8 %all-to-all-done.2.pieces_ref = bf16[64,8,1152]{2,1,0:T(8,128)(2,1)S(1)} async-done(((bf16[64,8,1152]{2,1,0:T(8,128)(2,1)}), bf16[64,8,1152]{2,1,0:T(8,128)(2,1)S(1)}, u32[]{:S(2)}, u32[]{:S(2)}) %all-to-all-start.2) | async-done | bytes 1179680 | tf_op jit(solution)/shard_map/all_to_all | solution.py:376
  111.7 0.8 finish.1
Async XLA Ops:
  0.6 0.7 copy-start.1
  1.3 39.2 %copy-start = (bf16[1,100,2048]{2,1,0:T(8,128)(2,1)S(1)}, bf16[1,100,2048]{2,1,0:T(8,128)(2,1)}, u32[]{:S(2)}) copy-start(bf16[1,100,2048]{2,1,0:T(8,128)(2,1)} %param.9) | copy-start | bytes 1228804
  1.3 39.2 %copy-start.2 = (s32[2048]{0:T(1024)S(1)}, s32[2048]{0:T(1024)}, u32[]{:S(2)}) copy-start(s32[2048]{0:T(1024)} %param.10) | copy-start | bytes 24580
  1.3 39.2 %copy-start.3 = (f32[100]{0:T(128)S(1)}, f32[100]{0:T(128)}, u32[]{:S(2)}) copy-start(f32[100]{0:T(128)} %param.11) | copy-start | bytes 1204
  18.7 21.9 %all-to-all-start = ((bf16[8,2,104,256]{3,2,1,0:T(8,128)(2,1)}), bf16[8,2,104,256]{3,2,1,0:T(8,128)(2,1)S(1)}, u32[]{:S(2)}, u32[]{:S(2)}) async-start(bf16[8,2,104,256]{3,2,1,0:T(8,128)(2,1)} %get-tuple-element.18), calls=%async_computation | async-start | bytes 1703936 | tf_op jit(solution)/shard_map/all_to_all | solution.py:369
  26.6 1.4 %collective-permute-start = (f32[1,1]{1,0:T(1,128)}, f32[1,1]{1,0:T(1,128)}, u32[]{:S(2)}, u32[]{:S(2)}) collective-permute-start(f32[1,1]{1,0:T(1,128)} %get-tuple-element.17), channel_id=1, source_target_pairs={{0,2},{2,0},{1,3},{3,1},{4,6},{6,4},{5,7},{7,5},{8,10},{10,8},{9,1... | collective-permute-start | bytes 20 | tf_op jit(solution)/shard_map/ppermute | solution.py:349
  29.2 3.7 %collective-permute-start.1 = (f32[1,1]{1,0:T(1,128)}, f32[1,1]{1,0:T(1,128)}, u32[]{:S(2)}, u32[]{:S(2)}) collective-permute-start(f32[1,1]{1,0:T(1,128)} %add.16), channel_id=1, source_target_pairs={{0,4},{4,0},{8,12},{12,8},{1,5},{5,1},{9,13},{13,9},{2,6},{6,2},{1... | collective-permute-start | bytes 20 | tf_op jit(solution)/shard_map/ppermute | solution.py:349
  33.5 4.9 %collective-permute-start.2 = (f32[1,1]{1,0:T(1,128)}, f32[1,1]{1,0:T(1,128)}, u32[]{:S(2)}, u32[]{:S(2)}) collective-permute-start(f32[1,1]{1,0:T(1,128)} %add.17), channel_id=1, source_target_pairs={{0,12},{4,8},{8,4},{12,0},{1,13},{5,9},{9,5},{13,1},{2,14},{6,10},... | collective-permute-start | bytes 20 | tf_op jit(solution)/shard_map/ppermute | solution.py:349
  45.9 18.3 %all-to-all-start.1 = ((bf16[8,2,104,256]{3,2,1,0:T(8,128)(2,1)}), bf16[8,2,104,256]{3,2,1,0:T(8,128)(2,1)S(1)}, u32[]{:S(2)}, u32[]{:S(2)}) async-start(bf16[8,2,104,256]{3,2,1,0:T(8,128)(2,1)} %get-tuple-element.19), calls=%async_computation.1 | async-start | bytes 1703936 | tf_op jit(solution)/shard_map/all_to_all | solution.py:372
  80.9 2.9 %collective-permute-start.3 = (bf16[32,16,1152]{2,1,0:T(8,128)(2,1)S(1)}, bf16[32,16,1152]{2,1,0:T(8,128)(2,1)S(1)}, u32[]{:S(2)}, u32[]{:S(2)}) collective-permute-start(bf16[32,16,1152]{2,1,0:T(8,128)(2,1)S(1)} %get-tuple-element.22), channel_id=1, source_target_pairs={{0,2},{2,0},{1,3},{3,1},{4,6},{6,4},{5,7},{7,5},{8,10},{10,8},{9,1... | collective-permute-start | bytes 3538952 | tf_op jit(solution)/shard_map/ppermute | solution.py:349
  85.3 26.4 %all-to-all-start.2 = ((bf16[64,8,1152]{2,1,0:T(8,128)(2,1)}), bf16[64,8,1152]{2,1,0:T(8,128)(2,1)S(1)}, u32[]{:S(2)}, u32[]{:S(2)}) async-start(bf16[64,8,1152]{2,1,0:T(8,128)(2,1)} %bitcast.7), calls=%async_computation.2 | async-start | bytes 2359296 | tf_op jit(solution)/shard_map/all_to_all | solution.py:376
